TPU v7x, 128 devices: a whole 4x4x4 slice. The times are simulated.
128 devices in a mesh: scen: 8 (over y_lo, z), area: 16 (over y_hi, x, core).
Axes of the slice: x: 4, y: 4 (y_hi: 2, y_lo: 2; y = y_hi * 2 + y_lo), z: 4, core: 2. Of those that a mesh axis runs over, the one named last changes fastest.
Arguments:
- demand: bfloat16 [128, 48, 10000], P('scen', None, 'area'), may hold values from 0.5 to 1.5
- ptdf: bfloat16 [10000, 2000], P('area'), may hold values from -0.0625 to 0.0625
- branch_limits: float32 [12000], replicated, may hold values from 0.2 to 1.5
- line_ids: int32 [2000], replicated, may hold values from 0 to 11999, as said below
- unit_bus: int32 [4000], P('area'), may hold values from 0 to 624
- node_map: int32 [4, 128], replicated, may hold values from 0 to 63, as said below
- cost_linear: float32 [4000], P('area'), may hold values from -3 to 3
- cost_quad: float32 [4000], P('area'), may hold values from 0.5 to 2
- capacity: float32 [4000], P('area'), may hold values from 0.5 to 2
- ramp_limits: float32 [4000], P('area'), may hold values from 0.05 to 0.5
- gen_init: float32 [128, 48, 4000], P('scen', None, 'area'), may hold values from 0 to 1
- price_init: float32 [128, 48, 4000], P('scen', None, 'area'), may hold values from -2 to 2
Outputs:
- dispatch: float32 [128, 48, 4000], P('scen', None, 'area')
- prices: float32 [128, 48, 4000], P('scen', None, 'area')
Inputs may be any that keep to these rules, and one draw needn't show every extreme that they name: `line_ids`: distinct branch indices. Section 1 has node 0 only; at section k node_map[k, s] = leaf(s) * w_k // 64 with w_k = 1, 4, 8, 64 and leaf(s) the last-section node; every last-section node holds exactly two scenarios. `unit_bus`: A unit's bus lies in the unit's own area.
All inputs are finite; a program needn't handle non-finite values.
Results may differ from a plain program's by a relative error of at most 0.0011.
Values may be sent and summed in bfloat16 or wider, within the bound.
No kernel may reach another device: no remote copies, remote signals or barrier semaphores. Data moves between devices by JAX's collectives and lax.ppermute only.
A program may use at most 128 MiB of HBM per device.

v0:
```python
import jax
import jax.numpy as jnp
from jax import lax
from jax.sharding import PartitionSpec as P

BUSES = 10000
SECTION2_NODES = 4
SECTION3_NODES = 8
ITERS = 2


def onehot(ids, width):
    return (ids[:, None] == jnp.arange(width, dtype=jnp.int32)[None, :]).astype(jnp.float32)


def excess(flows, limits):
    return jnp.sign(flows) * jnp.maximum(jnp.abs(flows) - limits, 0.0)


def node_mean(field, node_map):
    count, hours, units = field.shape
    span = hours // 4
    widths = [1, SECTION2_NODES, SECTION3_NODES, node_map.shape[1] // 2]
    first = lax.axis_index("scen") * count
    own_ids = lax.dynamic_slice_in_dim(node_map, first, count, 1)
    own_tables = [onehot(own_ids[section], widths[section]) for section in range(4)]
    full_tables = [onehot(node_map[section], widths[section]) for section in range(4)]
    partial_value = [
        jnp.dot(
            own_tables[section].T,
            field[:, section * span : (section + 1) * span, :].reshape(count, span * units),
            precision=lax.Precision.HIGHEST,
        )
        for section in range(4)
    ]
    totals = lax.psum(
        (partial_value[0], partial_value[1], partial_value[2], partial_value[3]), "scen"
    )
    pieces = []
    for section in range(4):
        counts = jnp.maximum(jnp.sum(full_tables[section], axis=0), 1.0)
        means = jnp.dot(
            own_tables[section], totals[section] / counts[:, None], precision=lax.Precision.HIGHEST
        )
        pieces.append(means.reshape(count, span, units))
    return jnp.concatenate(pieces, axis=1)


def descend(
    dispatch,
    prices,
    average,
    demand,
    ptdf,
    limits,
    unit_bus,
    cost_linear,
    cost_quad,
    capacity,
    ramp_limits,
):
    count, hours, units = dispatch.shape
    bus_dev = ptdf.shape[0]
    rows = count * hours
    power = jnp.zeros((count, hours, bus_dev), jnp.float32).at[:, :, unit_bus].add(dispatch)
    injection = (power - demand.astype(jnp.float32)).astype(jnp.bfloat16).reshape(rows, bus_dev)
    local_balance = jnp.sum(injection.astype(jnp.float32), axis=1)
    local_flows = jnp.dot(injection, ptdf, preferred_element_type=jnp.float32)
    flows, balance = lax.psum((local_flows, local_balance), "area")
    slopes = excess(flows, limits[None, :]).astype(jnp.bfloat16)
    back = lax.dot_general(
        slopes, ptdf, (((1,), (1,)), ((), ())), preferred_element_type=jnp.float32
    )
    pull = back[:, unit_bus].reshape(count, hours, units)
    change = dispatch[:, 1:, :] - dispatch[:, :-1, :]
    ramp = excess(change, ramp_limits[None, None, :])
    zeros_row = jnp.zeros((count, 1, units), jnp.float32)
    ramp_term = jnp.concatenate([zeros_row, ramp], axis=1) - jnp.concatenate(
        [ramp, zeros_row], axis=1
    )
    gradient = (
        cost_quad * dispatch
        + cost_linear
        + prices
        + (dispatch - average)
        + pull
        + 0.5 / BUSES * balance.reshape(count, hours, 1)
        + ramp_term
    )
    return jnp.clip(dispatch - 0.25 * gradient, 0.0, capacity)


def local(
    demand,
    ptdf,
    branch_limits,
    line_ids,
    unit_bus,
    node_map,
    cost_linear,
    cost_quad,
    capacity,
    ramp_limits,
    gen_init,
    price_init,
):
    limits = branch_limits[line_ids]
    dispatch = gen_init
    prices = price_init
    average = node_mean(dispatch, node_map)
    for step in range(ITERS):
        dispatch = descend(
            dispatch,
            prices,
            average,
            demand,
            ptdf,
            limits,
            unit_bus,
            cost_linear,
            cost_quad,
            capacity,
            ramp_limits,
        )
        average = node_mean(dispatch, node_map)
        prices = prices + (dispatch - average)
    return (dispatch, prices)


def solution(mesh):
    return jax.shard_map(
        local,
        mesh=mesh,
        in_specs=(
            P("scen", None, "area"),
            P("area", None),
            P(),
            P(),
            P("area"),
            P(),
            P("area"),
            P("area"),
            P("area"),
            P("area"),
            P("scen", None, "area"),
            P("scen", None, "area"),
        ),
        out_specs=(P("scen", None, "area"), P("scen", None, "area")),
        check_vma=False,
    )
```

profile of v0, /device:TPU:0, one launch (start us, length us, event | category | flops | bytes accessed | tf_op | source)
XLA Modules:
  0.0 628.7 jit_solution(11263944136164624038)
XLA Ops:
  20.5 2.6 broadcast.107.clone
  23.1 31.7 %scatter_fusion = f32[16,48,625]{1,0,2:T(8,128)} fusion(f32[16,48,625]{1,0,2:T(8,128)} %broadcast.107.clone, s32[250]{0:T(256)S(1)} %compare_select_fusion.1, f32[250,16,48]{2,1,0:T(8,128)} %copy.33), kind=kCustom, calls=%fused_computation.3 | custom fusion | flops 192000 | bytes 2305000 | tf_op jit(solution)/shard_map/scatter-add | solution.py:65
  54.8 5.8 copy.34
  62.8 5.2 fusion.86
  69.8 36.2 %all-reduce.6 = (f32[4,3000]{1,0:T(4,128)S(1)}, f32[1,3000]{1,0:T(1,128)S(1)}) all-reduce(f32[4,3000]{1,0:T(4,128)S(1)} %fusion.52, f32[1,3000]{1,0:T(1,128)S(1)} %fusion.75), channel_id=1, replica_groups=mesh['scen'=8,'area'=16] {'scen'}, use_global_device_ids=true, to_apply=%region_2.0 | all-reduce | flops 15000 | bytes 120000 | tf_op jit(solution)/shard_map/psum | solution.py:36
  109.0 33.4 %psum.117 = f32[768]{0:T(1024)S(1)} all-reduce(f32[768]{0:T(1024)S(1)} %reduce_sum.69), channel_id=1, replica_groups=mesh['scen'=8,'area'=16] {'area'}, use_global_device_ids=true, to_apply=%region_11.0 | all-reduce | flops 768 | bytes 6144 | tf_op jit(solution)/shard_map/psum | solution.py:69
  142.6 11.8 %gather_fusion = f32[2000]{0:T(1024)S(1)} fusion(f32[12000]{0:T(1024)S(1)} %copy-done.1, s32[2048]{0:T(1024)S(1)} %pad_clamp_fusion), kind=kCustom, calls=%fused_computation | custom fusion | bytes 24000 | tf_op jit(solution)/shard_map/gather | solution.py:107
  155.5 2.7 maximum_multiply_fusion.1
  162.2 93.3 %all-reduce.16.cloned.1.call-done = f32[768,2000]{0,1:T(8,128)} async-done(((f32[768,2000]{0,1:T(8,128)}), f32[768,2000]{0,1:T(8,128)}) %all-reduce.16.cloned.1.call-update) | async-done | bytes 6144016 | tf_op jit(solution)/shard_map/psum | solution.py:69
  255.5 7.5 %fusion = f32[768,625]{0,1:T(8,128)} fusion(bf16[625,2000]{0,1:T(8,128)(2,1)S(1)} %copy-done, f32[768,2000]{0,1:T(8,128)} %all-reduce.16.cloned.1.call-done, f32[2000]{0:T(1024)S(1)} %gather_fusion), kind=kOutput, calls=%fused_computation.7 | convolution fusion | flops 1929216000 | bytes 10572000 | tf_op jit(solution)/shard_map/dot_general | solution.py:71
  263.0 3.0 gather_fusion.1
  267.1 2.9 fusion.15
  280.9 31.7 %scatter_fusion.1 = f32[16,48,625]{1,0,2:T(8,128)} fusion(f32[16,48,625]{1,0,2:T(8,128)} %broadcast.107, s32[250]{0:T(256)S(1)} %compare_select_fusion.1, f32[250,16,48]{2,1,0:T(8,128)} %copy.36), kind=kCustom, calls=%fused_computation.4 | custom fusion | flops 192000 | bytes 2305000 | tf_op jit(solution)/shard_map/scatter-add | solution.py:65
  312.5 5.8 copy.37
  320.5 5.2 fusion.87
  325.8 38.0 %psum.123 = f32[768]{0:T(1024)S(1)} all-reduce(f32[768]{0:T(1024)S(1)} %reduce_sum.71), channel_id=1, replica_groups=mesh['scen'=8,'area'=16] {'area'}, use_global_device_ids=true, to_apply=%region_19.20 | all-reduce | flops 768 | bytes 6144 | tf_op jit(solution)/shard_map/psum | solution.py:69
  369.5 36.5 %all-reduce.5 = (f32[4,3000]{1,0:T(4,128)}, f32[1,3000]{1,0:T(1,128)}) all-reduce(f32[4,3000]{1,0:T(4,128)S(1)} %fusion.51, f32[1,3000]{1,0:T(1,128)S(1)} %fusion.73), channel_id=1, replica_groups=mesh['scen'=8,'area'=16] {'scen'}, use_global_device_ids=true, to_apply=%region_13.14 | all-reduce | flops 15000 | bytes 120000 | tf_op jit(solution)/shard_map/psum | solution.py:36
  417.3 94.6 %all-reduce.18.cloned.1.call-done = f32[768,2000]{0,1:T(8,128)} async-done(((f32[768,2000]{0,1:T(8,128)}), f32[768,2000]{0,1:T(8,128)}) %all-reduce.18.cloned.1.call-update) | async-done | bytes 6144016 | tf_op jit(solution)/shard_map/psum | solution.py:69
  511.8 7.5 %fusion.1 = f32[768,625]{0,1:T(8,128)} fusion(bf16[625,2000]{0,1:T(8,128)(2,1)S(1)} %copy-done, f32[768,2000]{0,1:T(8,128)} %all-reduce.18.cloned.1.call-done, f32[2000]{0:T(1024)} %copy-done.18), kind=kOutput, calls=%fused_computation.8 | convolution fusion | flops 1929216000 | bytes 10572000 | tf_op jit(solution)/shard_map/dot_general | solution.py:71
  519.4 4.0 gather_fusion.2
  525.6 2.8 maximum_minimum_fusion
  539.7 35.2 %all-reduce.4 = (f32[4,3000]{1,0:T(4,128)}, f32[1,3000]{1,0:T(1,128)}) all-reduce(f32[4,3000]{1,0:T(4,128)} %fusion.50, f32[1,3000]{1,0:T(1,128)S(1)} %fusion.71), channel_id=1, replica_groups=mesh['scen'=8,'area'=16] {'scen'}, use_global_device_ids=true, to_apply=%region_21.22 | all-reduce | flops 15000 | bytes 120000 | tf_op jit(solution)/shard_map/psum | solution.py:36
  579.4 34.7 %all-reduce.20.cloned.1.call-done = (f32[64,3000]{1,0:T(8,128)}, f32[8,3000]{1,0:T(8,128)}) async-done(((f32[64,3000]{1,0:T(8,128)}, f32[8,3000]{1,0:T(8,128)}), (f32[64,3000]{1,0:T(8,128)}, f32[8,3000]{1,0:T(8,128)})) %all-reduce.20.cloned.1.call-update) | async-done | bytes 864016 | tf_op jit(solution)/shard_map/psum | solution.py:36
  618.9 3.3 fusion.16
  (163 shorter events, 78.3 us)
Async XLA Ops:
  7.2 55.6 %copy-start = (bf16[625,2000]{0,1:T(8,128)(2,1)S(1)}, bf16[625,2000]{0,1:T(8,128)(2,1)}, u32[]{:S(2)}) copy-start(bf16[625,2000]{0,1:T(8,128)(2,1)} %param.13) | copy-start | bytes 7500004
  7.2 10.9 %copy-start.2 = (f32[16,48,250]{2,1,0:T(8,128)S(1)}, f32[16,48,250]{2,1,0:T(8,128)}, u32[]{:S(2)}) copy-start(f32[16,48,250]{2,1,0:T(8,128)} %param.22) | copy-start | bytes 2304004
  7.2 151.0 %all-reduce.24.cloned.1.call-start = ((), (), s32[]{:S(2)}) async-start(), calls=%async_computation.4 | async-start | bytes 1769472 | tf_op jit(solution)/shard_map/psum | solution.py:36
  11.6 143.1 %copy-start.6 = (s32[4,16]{1,0:T(4,128)}, s32[4,16]{1,0:T(4,128)S(1)}, u32[]{:S(2)}) copy-start(s32[4,16]{1,0:T(4,128)S(1)} %constant_dynamic-slice_fusion) | copy-start | bytes 772
  12.2 260.0 %copy-start.9 = (s32[16]{0:T(128)}, s32[16]{0:T(128)S(1)}, u32[]{:S(2)}) copy-start(s32[16]{0:T(128)S(1)} %get-tuple-element.34) | copy-start | bytes 196
  17.3 238.2 %all-reduce.16.cloned.1.call-start = ((), (), s32[]{:S(2)}) async-start(), calls=%async_computation | async-start | bytes 12288000 | tf_op jit(solution)/shard_map/psum | solution.py:69
  68.0 38.0 %copy-start.19 = (s32[4,128]{1,0:T(4,128)S(1)}, s32[4,128]{1,0:T(4,128)}, u32[]{:S(2)}) copy-start(s32[4,128]{1,0:T(4,128)} %param.17) | copy-start | bytes 6148
  68.0 74.5 %copy-start.17 = (s32[2000]{0:T(1024)S(1)}, s32[2000]{0:T(1024)}, u32[]{:S(2)}) copy-start(s32[2000]{0:T(1024)} %param.15) | copy-start | bytes 24004
  68.0 74.5 %copy-start.1 = (f32[12000]{0:T(1024)S(1)}, f32[12000]{0:T(1024)}, u32[]{:S(2)}) copy-start(f32[12000]{0:T(1024)} %param.14) | copy-start | bytes 144004
  68.0 344.4 %all-reduce.22.cloned.1.call-start = ((), (), s32[]{:S(2)}) async-start(), calls=%async_computation.3 | async-start | bytes 1769472 | tf_op jit(solution)/shard_map/psum | solution.py:36
  106.2 36.3 %copy-start.29 = (f32[4]{0:T(128)}, f32[4]{0:T(128)S(1)}, u32[]{:S(2)}) copy-start(f32[4]{0:T(128)S(1)} %broadcast_maximum_fusion.2) | copy-start | bytes 52
  142.5 12.9 %copy-start.21 = (f32[250]{0:T(256)S(1)}, f32[250]{0:T(256)}, u32[]{:S(2)}) copy-start(f32[250]{0:T(256)} %param.21) | copy-start | bytes 3004
  154.3 101.2 %copy-start.18 = (f32[2000]{0:T(1024)}, f32[2000]{0:T(1024)S(1)}, u32[]{:S(2)}) copy-start(f32[2000]{0:T(1024)S(1)} %gather_fusion) | copy-start | bytes 24004
  154.4 6.5 %copy-start.12 = (s32[16]{0:T(128)S(1)}, s32[16]{0:T(128)}, u32[]{:S(2)}) copy-start(s32[16]{0:T(128)} %copy-done.11) | copy-start | bytes 196
  154.5 108.5 %copy-start.8 = (s32[1024]{0:T(1024)}, s32[1024]{0:T(1024)S(1)}, u32[]{:S(2)}) copy-start(s32[1024]{0:T(1024)S(1)} %pad_clamp_fusion.1) | copy-start | bytes 12292
  154.6 7.6 %copy-start.33 = (f32[64]{0:T(128)}, f32[64]{0:T(128)S(1)}, u32[]{:S(2)}) copy-start(f32[64]{0:T(128)S(1)} %broadcast_maximum_fusion) | copy-start | bytes 772
  154.6 7.5 %copy-start.30 = (f32[8]{0:T(128)}, f32[8]{0:T(128)S(1)}, u32[]{:S(2)}) copy-start(f32[8]{0:T(128)S(1)} %broadcast_maximum_fusion.1) | copy-start | bytes 100
  154.7 7.5 %copy-start.20 = (f32[16]{0:T(128)}, f32[16]{0:T(128)S(1)}, u32[]{:S(2)}) copy-start(f32[16]{0:T(128)S(1)} %bitcast_convert_fusion) | copy-start | bytes 196
  275.8 236.1 %all-reduce.18.cloned.1.call-start = ((), (), s32[]{:S(2)}) async-start(), calls=%async_computation.1 | async-start | bytes 12288000 | tf_op jit(solution)/shard_map/psum | solution.py:69
  325.7 288.4 %all-reduce.20.cloned.1.call-start = ((), (), s32[]{:S(2)}) async-start(), calls=%async_computation.2 | async-start | bytes 1769472 | tf_op jit(solution)/shard_map/psum | solution.py:36
  407.2 7.9 %copy-start.14 = (s32[16]{0:T(128)S(1)}, s32[16]{0:T(128)}, u32[]{:S(2)}) copy-start(s32[16]{0:T(128)} %copy-done.11) | copy-start | bytes 196
  407.2 7.9 %copy-start.31 = (f32[8]{0:T(128)S(1)}, f32[8]{0:T(128)}, u32[]{:S(2)}) copy-start(f32[8]{0:T(128)} %copy-done.30) | copy-start | bytes 100
  574.9 41.8 %copy-start.15 = (s32[16]{0:T(128)S(1)}, s32[16]{0:T(128)}, u32[]{:S(2)}) copy-start(s32[16]{0:T(128)} %copy-done.11) | copy-start | bytes 196
  574.9 41.8 %copy-start.32 = (f32[8]{0:T(128)S(1)}, f32[8]{0:T(128)}, u32[]{:S(2)}) copy-start(f32[8]{0:T(128)} %copy-done.30) | copy-start | bytes 100
  (15 other events, 60.3 us)
Sparse Core Ops, SparseCore 0:
  17.5 79.3 all-reduce.23
  99.6 155.8 all-reduce.15
  275.9 77.5 all-reduce.21
  356.0 155.7 all-reduce.17
  536.2 77.7 all-reduce.19
where the time goes:
time: 631 us; the launch traced here: 629 us
  waiting for transfers between devices  223 us (35%)
  blocking collectives  179 us (28%)
  other arithmetic  88.1 us (14%)
  local copies, waits for them, and re-layouts  74.7 us (12%)
  matrix products  48.6 us (8%)
  between operations  14.9 us (2%)
    psum x2, waiting for transfers between devices, descend(): flows, balance = lax.psum((local_flows, local_balance), 'area')  188 us
    psum x3, blocking collectives, node_mean(): lax.psum((partial_value[0], partial_value[1], partial_value[2], partial_v...  108 us
    psum x2, blocking collectives, descend(): flows, balance = lax.psum((local_flows, local_balance), 'area')  71.4 us
    scatter-add x2, other arithmetic, descend(): jnp.zeros((count, hours, bus_dev), jnp.float32).at[:, :, unit_bus]  63.3 us
    psum x3, waiting for transfers between devices, node_mean(): lax.psum((partial_value[0], partial_value[1], partial_value[2], partial_v...  34.7 us
    dot_general x2, matrix products, descend(): lax.dot_general(slopes, ptdf, (((1,), (1,)), ((), ())), preferred_element...  15 us
    dot_general x12, matrix products, node_mean(): jnp.dot(own_tables[section].T, field[:, section * span:(section + 1) * sp...  13.2 us
    reshape x12, local copies, waits for them, and re-layouts, node_mean(): field[:, section * span:(section + 1) * span, :]  12.9 us
  transfers between devices with their start and end apart: 5, of which 3 were waited for; matrix products, arithmetic and copies ran while one was open for 24% of the time, Pallas kernels for 0%

commit v1 on v0

v1 whole, which is shorter than its diff:
```python
import functools

import jax
import jax.numpy as jnp
from jax import lax
from jax.experimental import pallas as pl
from jax.experimental.pallas import tpu as pltpu
from jax.sharding import Mesh, PartitionSpec as P

BUSES = 10000
SECTION2_NODES = 4
SECTION3_NODES = 8
ITERS = 2

F32 = jnp.float32
BF16 = jnp.bfloat16
LINES = 2000
LANES = 2048
SCALE_LANE = 2002
BUS_PAD = 640
UNIT_PAD = 256
SPAN = 12
NODE_FIRST = (0, 1, 5)
NODE_WIDTH = (1, SECTION2_NODES, SECTION3_NODES)
ROWS = 32
VMEM = pl.BlockSpec(memory_space=pltpu.VMEM)
SMEM = pl.BlockSpec(memory_space=pltpu.SMEM)
PARAMS = pltpu.CompilerParams(vmem_limit_bytes=56 * 1024 * 1024)


def call(kernel, outs, scratch=()):
    def run(*args):
        specs = [SMEM if a.dtype == jnp.int32 and a.ndim == 1 else VMEM for a in args]
        many = isinstance(outs, (list, tuple))
        return pl.pallas_call(
            kernel,
            out_shape=list(outs) if many else outs,
            in_specs=specs,
            out_specs=[VMEM for _ in outs] if many else VMEM,
            scratch_shapes=list(scratch),
            compiler_params=PARAMS,
        )(*args)

    return run


def shape(dims, dtype):
    return jax.ShapeDtypeStruct(dims, dtype)


def parts3(x):
    hi = x.astype(BF16)
    rest = x - hi.astype(F32)
    mid = rest.astype(BF16)
    low = (rest - mid.astype(F32)).astype(BF16)
    return hi, mid, low


def mm(a, b, dims):
    return lax.dot_general(a, b, (dims, ((), ())), preferred_element_type=F32)


NN = ((1,), (0,))
NT = ((1,), (1,))
TN = ((0,), (0,))


def mm3(a, b, dims):
    return sum(mm(part, b, dims) for part in parts3(a))


def excess(x, limit):
    return x - jnp.minimum(jnp.maximum(x, -limit), limit)


def coded(flows, balance_scale):
    lanes = lax.broadcasted_iota(jnp.int32, flows.shape, 1)
    lines = lanes < LINES
    most = jnp.max(jnp.where(lines, jnp.abs(flows), 0.0), axis=1, keepdims=True)
    power = jnp.floor(14.9 - jnp.log2(jnp.maximum(most, 1e-6)))
    scaled = jnp.where(lines, flows * jnp.exp2(power), 0.0)
    scaled = jnp.where(lanes == LINES, flows * balance_scale, scaled)
    scaled = jnp.where(lanes == SCALE_LANE, power, scaled)
    return jnp.round(scaled).astype(jnp.int32).astype(jnp.int16)


def decoded(code, balance_scale):
    code = code.astype(jnp.int32).astype(F32)
    lanes = lax.broadcasted_iota(jnp.int32, code.shape, 1)
    scale = jnp.exp2(-code[:, SCALE_LANE : SCALE_LANE + 1])
    flows = code * jnp.where(lanes == LINES, 1.0 / balance_scale, scale)
    return jnp.where(lanes > LINES, 0.0, flows)


def prepare_kernel(bus_ref, ptdf_ref, pick_ref, rows_ref):
    rows = lax.broadcasted_iota(jnp.int32, (BUS_PAD, UNIT_PAD), 0)
    pick = (rows == bus_ref[...]).astype(F32).astype(BF16)
    pick_ref[...] = pick
    rows_ref[...] = mm(pick, ptdf_ref[...], TN).astype(BF16)


def limits_kernel(ids_ref, table_ref, out_ref):
    ids = ids_ref[...]
    low = ids & 127
    high = ids >> 7
    lanes = lax.broadcasted_iota(jnp.int32, (128, LANES), 0)
    spread = mm3(table_ref[...], (lanes == low).astype(F32).astype(BF16), NN)
    rows = lax.broadcasted_iota(jnp.int32, spread.shape, 0)
    out_ref[...] = jnp.sum(jnp.where(rows == high, spread, 0.0), axis=0, keepdims=True)


def flows_kernel(
    where_ref,
    own_ref,
    other_ref,
    demand_own_ref,
    demand_other_ref,
    pick_own_ref,
    pick_other_ref,
    ptdf_own_ref,
    ptdf_other_ref,
    *outs,
):
    x, core = where_ref[0], where_ref[2]
    hours, units = other_ref.shape[1:]
    buses = demand_own_ref.shape[2]

    def injected(read_dispatch, read_demand, pick_ref):
        dispatch = jnp.concatenate([read_dispatch(d) for d in range(4)], axis=0)
        demand = jnp.concatenate([read_demand(d) for d in range(4)], axis=0)
        power = mm3(dispatch, pick_ref[...][:, :units], NT)[:, :buses]
        return (power - demand.astype(F32)).astype(BF16)

    def reader(ref, base):
        def read(d):
            first = base + 2 * lax.rem(x + d, 4)
            return ref[pl.ds(first, 2)].astype(F32).reshape(2 * hours, ref.shape[2])

        return read

    own = injected(reader(own_ref, 8 * core), reader(demand_own_ref, 8 * core), pick_own_ref)
    other = injected(reader(other_ref, 0), reader(demand_other_ref, 0), pick_other_ref)
    total = mm(own, ptdf_own_ref[:buses, :], NN) + mm(other, ptdf_other_ref[:buses, :], NN)
    sent = coded(total, 8.0)
    for d in range(4):
        outs[d][...] = sent[d * 2 * hours : (d + 1) * 2 * hours]


def gathered_sum_kernel(where_ref, a_ref, b_ref, c_ref, d_ref, keep_ref, send_ref):
    y = where_ref[1]
    rows = keep_ref.shape[0]

    def total(first):
        cut = slice(first, first + rows)
        return (
            decoded(a_ref[cut, :], 8.0)
            + decoded(b_ref[cut, :], 8.0)
            + decoded(c_ref[cut, :], 8.0)
            + decoded(d_ref[cut, :], 8.0)
        )

    upper, lower = total(0), total(rows)
    keep_ref[...] = jnp.where(y == 0, upper, lower)
    send_ref[...] = coded(jnp.where(y == 0, lower, upper), 4.0)


def slopes_kernel(keep_ref, got_ref, limits_ref, out_ref):
    flows = keep_ref[...] + decoded(got_ref[...], 4.0)
    slopes = excess(flows, limits_ref[...])
    lanes = lax.broadcasted_iota(jnp.int32, flows.shape, 1)
    balance = flows[:, LINES : LINES + 1] * (0.5 / BUSES)
    high = balance.astype(BF16).astype(F32)
    slopes = jnp.where(lanes == LINES, high, slopes)
    slopes = jnp.where(lanes == LINES + 1, balance - high, slopes)
    out_ref[...] = slopes.astype(BF16)


def join_kernel(where_ref, own_ref, got_ref, out_ref):
    y = where_ref[1]
    rows = own_ref.shape[0]

    @pl.when(y == 0)
    def _():
        out_ref[:rows, :] = own_ref[...]
        out_ref[rows:, :] = got_ref[...]

    @pl.when(y != 0)
    def _():
        out_ref[:rows, :] = got_ref[...]
        out_ref[rows:, :] = own_ref[...]


def pull_kernel(where_ref, a_ref, b_ref, c_ref, d_ref, rows_own_ref, rows_other_ref, own_ref, send_ref):
    x = where_ref[0]
    hours = own_ref.shape[1]
    slopes = jnp.concatenate([a_ref[...], b_ref[...], c_ref[...], d_ref[...]], axis=0)
    for rows_ref, out_ref in ((rows_other_ref, send_ref), (rows_own_ref, own_ref)):
        pull = mm(slopes, rows_ref[...], NT)
        for d in range(4):
            first = 2 * lax.rem(x + d, 4)
            block = pull[d * 2 * hours : (d + 1) * 2 * hours]
            out_ref[pl.ds(first, 2)] = block.reshape(2, hours, UNIT_PAD)


def pack_kernel(ids_ref, field_ref, out_ref, wide):
    count, hours, units = field_ref.shape
    wide[...] = jnp.zeros(wide.shape, F32)
    for s in range(count):
        wide[s, :, :units] = field_ref[s, 3 * SPAN :, :]
    for section in range(3):
        cut = slice(section * SPAN, (section + 1) * SPAN)
        for node in range(NODE_WIDTH[section]):
            total = jnp.zeros((SPAN, units), F32)
            for s in range(count):
                inside = ids_ref[section * count + s] == node
                total = total + jnp.where(inside, field_ref[s, cut, :], 0.0)
            wide[count + NODE_FIRST[section] + node, :, :units] = total
    for tile in range(2):
        block = jnp.swapaxes(wide[:, :, tile * 128 : (tile + 1) * 128], 0, 1)
        for hour in range(SPAN):
            out_ref[2 * hour + tile] = block[hour]


def means_kernel(got_ref, leaf_row_ref, leaf_column_ref, counts_ref, out_ref):
    scenarios = leaf_row_ref.shape[1]
    parts = scenarios // 16
    same = leaf_row_ref[...] == leaf_column_ref[...]
    table = same.astype(F32)
    size = jnp.maximum(jnp.sum(table, axis=1, keepdims=True), 1.0)
    table = table.astype(BF16)
    for unit in range(3):
        rows = jnp.concatenate([got_ref[3 * p + unit, :16, :] for p in range(parts)], axis=0)
        leaf = sum(mm(table, part, NN) for part in parts3(rows)) / size
        sums = got_ref[unit, 16:, :]
        for p in range(1, parts):
            sums = sums + got_ref[3 * p + unit, 16:, :]
        node = sums / counts_ref[...]
        for p in range(parts):
            out_ref[3 * p + unit, :16, :] = leaf[16 * p : 16 * (p + 1)]
            out_ref[3 * p + unit, 16:, :] = node


def unpack(ids_ref, means_ref, wide, count):
    for tile in range(2):
        block = jnp.stack([means_ref[2 * hour + tile] for hour in range(SPAN)], axis=0)
        wide[:, :, tile * 128 : (tile + 1) * 128] = jnp.swapaxes(block, 0, 1)

    def average(s, units):
        pieces = []
        for section in range(3):
            row = count + NODE_FIRST[section] + ids_ref[section * count + s]
            pieces.append(wide[row])
        pieces.append(wide[s])
        return jnp.concatenate(pieces, axis=0)[:, :units]

    return average


def gradient_kernel(
    advance,
    where_ref,
    ids_ref,
    dispatch_ref,
    prices_ref,
    means_ref,
    pull_own_ref,
    pull_other_ref,
    quad_ref,
    linear_ref,
    cap_ref,
    ramp_ref,
    out_ref,
    send_ref,
    prices_out_ref,
    wide,
):
    core = where_ref[2]
    count, hours, units = dispatch_ref.shape
    average_of = unpack(ids_ref, means_ref, wide, count)
    zero = jnp.zeros((1, units), F32)

    def one(s, pull):
        dispatch = dispatch_ref[s]
        average = average_of(s, units)
        prices = prices_ref[s]
        if advance:
            prices = prices + (dispatch - average)
        prices_out_ref[s] = prices
        change = jnp.concatenate([dispatch[1:] - dispatch[:-1], zero], axis=0)
        ramp = excess(change, ramp_ref[...])
        ramp_term = jnp.concatenate([zero, ramp[:-1]], axis=0) - ramp
        gradient = (
            quad_ref[...] * dispatch
            + linear_ref[...]
            + prices
            + (dispatch - average)
            + pull[:, :units]
            + ramp_term
        )
        new = jnp.minimum(jnp.maximum(dispatch - 0.25 * gradient, 0.0), cap_ref[...])
        out_ref[s] = new
        return new

    def step(i, carry):
        one(8 * core + i, pull_own_ref[i])
        send_ref[i] = one(8 * (1 - core) + i, pull_other_ref[i])
        return carry

    lax.fori_loop(0, 8, step, 0)


def prices_kernel(ids_ref, dispatch_ref, prices_ref, means_ref, out_ref, wide):
    count, hours, units = dispatch_ref.shape
    average_of = unpack(ids_ref, means_ref, wide, count)

    def step(s, carry):
        out_ref[s] = prices_ref[s] + (dispatch_ref[s] - average_of(s, units))
        return carry

    lax.fori_loop(0, count, step, 0)


def shifted(value, by):
    return lax.ppermute(value, "x", [(i, (i - by) % 4) for i in range(4)])


def swapped(value, axis):
    return lax.ppermute(value, axis, [(0, 1), (1, 0)])


def local(
    demand,
    ptdf,
    branch_limits,
    line_ids,
    unit_bus,
    node_map,
    cost_linear,
    cost_quad,
    capacity,
    ramp_limits,
    gen_init,
    price_init,
):
    count, hours, units = gen_init.shape
    buses = ptdf.shape[0]
    x, y, core = lax.axis_index("x"), lax.axis_index("yhi"), lax.axis_index("core")
    where = jnp.stack([x, y, core]).astype(jnp.int32)
    first = lax.axis_index(("ylo", "z")) * count
    ids = lax.dynamic_slice_in_dim(node_map, first, count, 1).reshape(-1)

    wide_scratch = pltpu.VMEM((ROWS, SPAN, UNIT_PAD), F32)
    flat = (3 * 8, ROWS, 128)
    counts = [
        jnp.sum((node_map[k][None, :] == jnp.arange(w, dtype=jnp.int32)[:, None]).astype(F32), axis=1)
        for k, w in zip(range(3), NODE_WIDTH)
    ]
    counts = jnp.maximum(jnp.concatenate(counts + [jnp.ones((3,), F32)]), 1.0)[:, None]

    def node_means(field):
        packed = call(pack_kernel, shape(flat, F32), [wide_scratch])(ids, field)
        got = lax.all_to_all(packed, ("ylo", "z"), 0, 0, tiled=True)
        means = call(means_kernel, shape(flat, F32))(
            got, node_map[3][None, :], node_map[3][:, None], counts
        )
        return lax.all_to_all(means, ("ylo", "z"), 0, 0, tiled=True)

    def other_half(field):
        return lax.dynamic_slice_in_dim(field, 8 * (1 - core), 8, 0)

    ptdf_other = swapped(ptdf, "core")
    bus_other = swapped(unit_bus.astype(F32), "core").astype(jnp.int32)
    demand_other = swapped(other_half(demand), "core")
    dispatch_other = swapped(other_half(gen_init), "core")

    def padded(table):
        wide = jnp.pad(table, ((0, BUS_PAD - buses), (0, LANES - LINES)))
        lane = lax.broadcasted_iota(jnp.int32, wide.shape, 1)
        return jnp.where((lane == LINES) | (lane == LINES + 1), jnp.ones((), BF16), wide)

    def prepared(bus, table):
        row = jnp.pad(bus, (0, UNIT_PAD - units), constant_values=-1)[None, :]
        return call(
            prepare_kernel,
            [shape((BUS_PAD, UNIT_PAD), BF16), shape((UNIT_PAD, LANES), BF16)],
        )(row, table)

    ptdf_own, ptdf_other = padded(ptdf), padded(ptdf_other)
    pick_own, rows_own = prepared(unit_bus, ptdf_own)
    pick_other, rows_other = prepared(bus_other, ptdf_other)
    table = jnp.pad(branch_limits, (0, 96 * 128 - branch_limits.shape[0])).reshape(96, 128)
    limits = call(limits_kernel, shape((1, LANES), F32))(
        jnp.pad(line_ids, (0, LANES - LINES))[None, :], table
    )

    block = (2 * hours, LANES)
    part = (hours, LANES)
    half = (8, hours, UNIT_PAD)

    dispatch, prices = gen_init, price_init
    for step in range(ITERS):
        sums = call(flows_kernel, [shape(block, jnp.int16)] * 4)(
            where,
            dispatch,
            dispatch_other,
            demand,
            demand_other,
            pick_own,
            pick_other,
            ptdf_own,
            ptdf_other,
        )
        got = [shifted(sums[d], -d) for d in (1, 2, 3)]
        means = node_means(dispatch)
        keep, send = call(gathered_sum_kernel, [shape(part, F32), shape(part, jnp.int16)])(
            where, sums[0], *got
        )
        slopes = call(slopes_kernel, shape(part, BF16))(keep, swapped(send, "yhi"), limits)
        own = call(join_kernel, shape(block, BF16))(where, slopes, swapped(slopes, "yhi"))
        blocks = [own] + [shifted(own, d) for d in (1, 2, 3)]
        pull_own, pull_send = call(pull_kernel, [shape(half, F32)] * 2)(
            where, *blocks, rows_own, rows_other
        )
        pull_other = swapped(pull_send, "core")
        dispatch, send, prices = call(
            functools.partial(gradient_kernel, step > 0),
            [
                shape((count, hours, units), F32),
                shape((8, hours, units), F32),
                shape((count, hours, units), F32),
            ],
            [wide_scratch],
        )(
            where,
            ids,
            dispatch,
            prices,
            means,
            pull_own,
            pull_other,
            cost_quad[None, :],
            cost_linear[None, :],
            capacity[None, :],
            ramp_limits[None, :],
        )
        if step + 1 < ITERS:
            dispatch_other = swapped(send, "core")
    means = node_means(dispatch)
    prices = call(prices_kernel, shape((count, hours, units), F32), [wide_scratch])(
        ids, dispatch, prices, means
    )
    return (dispatch, prices)


def solution(mesh):
    fine = Mesh(mesh.devices.reshape(2, 4, 2, 4, 2), ("ylo", "z", "yhi", "x", "core"))
    scen, area = ("ylo", "z"), ("yhi", "x", "core")
    return jax.shard_map(
        local,
        mesh=fine,
        in_specs=(
            P(scen, None, area),
            P(area, None),
            P(),
            P(),
            P(area),
            P(),
            P(area),
            P(area),
            P(area),
            P(area),
            P(scen, None, area),
            P(scen, None, area),
        ),
        out_specs=(P(scen, None, area), P(scen, None, area)),
        check_vma=False,
    )
```

time: 631 us -> 278 us (0.44)
  waiting for transfers between devices: 223 us -> 77.2 us
  blocking collectives: 179 us -> 52.7 us
  other arithmetic: 88.1 us -> 8.99 us
  Pallas kernels: 0 us -> 72.4 us
  matrix products: 48.6 us -> 0 us
  local copies, waits for them, and re-layouts: 74.7 us -> 26.2 us
  starting transfers between devices: 0.21 us -> 38.5 us
  between operations: 14.9 us -> 0.78 us
    psum x5 -> x0, waiting for transfers between devices: 223 us -> none  [the longest x2 188 us: descend(): flows, balance = lax.psum((local_flows, local_balance), 'area')]
    psum x5 -> x0, blocking collectives: 179 us -> none  [the longest x3 108 us: node_mean(): lax.psum((partial_value[0], partial_value[1], partial_value[2], partial_v...]
    ppermute x0 -> x23, waiting for transfers between devices: none -> 77.2 us  [the longest x12 58.7 us: shifted(): return lax.ppermute(value, 'x', [(i, (i - by) % 4) for i in range(4)])]
    pallas_call x0 -> x22, Pallas kernels: none -> 72.4 us  [run(): pl.pallas_call(kernel, out_shape=list(outs) if many else outs, in_specs=s...]
    scatter-add x2 -> x0, other arithmetic: 63.3 us -> none  [descend(): jnp.zeros((count, hours, bus_dev), jnp.float32).at[:, :, unit_bus]]
    all_to_all x0 -> x4, blocking collectives: none -> 52.7 us  [the longest x3 40.4 us: node_means(): return lax.all_to_all(means, ('ylo', 'z'), 0, 0, tiled=True)]
    dot_general x25 -> x0, matrix products: 48.6 us -> none  [the longest x2 15 us: descend(): lax.dot_general(slopes, ptdf, (((1,), (1,)), ((), ())), preferred_element...]
    ppermute x0 -> x23, starting transfers between devices: none -> 29.6 us  [the longest x12 19.8 us: shifted(): return lax.ppermute(value, 'x', [(i, (i - by) % 4) for i in range(4)])]
  transfers between devices with their start and end apart: 5 -> 25, of which waited for: 3 -> 13; matrix products, arithmetic and copies ran while one was open for 24% -> 9% of each run, Pallas kernels for 0% -> 11%
where the time goes in v1:
time: 278 us; the launch traced here: 277 us
  waiting for transfers between devices  77.2 us (28%)
  Pallas kernels  72.4 us (26%)
  blocking collectives  52.7 us (19%)
  starting transfers between devices  38.5 us (14%)
  local copies, waits for them, and re-layouts  26.2 us (9%)
  other arithmetic  8.99 us (3%)
    pallas_call x22, Pallas kernels, run(): pl.pallas_call(kernel, out_shape=list(outs) if many else outs, in_specs=s...  72.4 us
    ppermute x12, waiting for transfers between devices, shifted(): return lax.ppermute(value, 'x', [(i, (i - by) % 4) for i in range(4)])  58.7 us
    all_to_all x3, blocking collectives, node_means(): return lax.all_to_all(means, ('ylo', 'z'), 0, 0, tiled=True)  40.4 us
    ppermute x12, starting transfers between devices, shifted(): return lax.ppermute(value, 'x', [(i, (i - by) % 4) for i in range(4)])  19.8 us
    ppermute x11, waiting for transfers between devices, swapped(): return lax.ppermute(value, axis, [(0, 1), (1, 0)])  18.5 us
    unnamed x55, local copies, waits for them, and re-layouts  13.8 us
    all_to_all x1, blocking collectives, node_means(): got = lax.all_to_all(packed, ('ylo', 'z'), 0, 0, tiled=True)  12.3 us
    ppermute x11, starting transfers between devices, swapped(): return lax.ppermute(value, axis, [(0, 1), (1, 0)])  9.75 us
  transfers between devices with their start and end apart: 25, of which 13 were waited for; matrix products, arithmetic and copies ran while one was open for 9% of the time, Pallas kernels for 11%

profile of v1, /device:TPU:0, one launch (start us, length us, event | category | flops | bytes accessed | tf_op | source)
XLA Modules:
  0.0 276.7 jit_solution(16437947824070760008)
XLA Ops:
  10.8 4.5 %copy.30 = bf16[625,2000]{1,0:T(8,128)(2,1)} copy(bf16[625,2000]{0,1:T(8,128)(2,1)} %collective-permute-done.3) | data formatting | bytes 5000000 | tf_op jit(solution)/shard_map/ppermute | solution.py:328
  15.2 5.5 %pad_select_fusion = (bf16[640,2048]{1,0:T(8,128)(2,1)}, bf16[640,2048]{1,0:T(8,128)(2,1)}) fusion(bf16[625,2000]{1,0:T(8,128)(2,1)} %copy.30, pred[2048]{0:T(1024)(128)(4,1)S(1)} %fusion, bf16[625,2000]{1,0:T(8,128)(2,1)S(1)} %copy.29), kind=kLoop, calls=%fused_computation | loop fusion | flops 2621440 | bytes 10244928 | tf_op jit(solution)/shard_map/jit(_where)/select_n | solution.py:379
  20.8 3.8 %shard_map.134 = (bf16[640,256]{1,0:T(8,128)(2,1)}, bf16[256,2048]{1,0:T(8,128)(2,1)}) custom-call(s32[1,256]{1,0:T(1,128)} %bitcast.33, bf16[640,2048]{1,0:T(8,128)(2,1)} %get-tuple-element.52.ptdf_ref.ptdf_other_ref), custom_call_target="tpu_custom_call" | custom-call | tf_op jit(solution)/shard_map/pallas_call | solution.py:35
  29.2 9.3 %shard_map.135 = (s16[96,2048]{1,0:T(8,128)(2,1)}, s16[96,2048]{1,0:T(8,128)(2,1)}, s16[96,2048]{1,0:T(8,128)(2,1)}, s16[96,2048]{1,0:T(8,128)(2,1)}) custom-call(s32[3]{0:T(128)} %pad_add_fusion.where_ref, f32[16,48,250]{2,1,0:T(8,128)} %dispatch_ref.1, f32[8,48,250]{2,1,0:T(8,128)} %copy-done.3, bf16[16,48,625]{2,1,0:T(8,128)(2,1)} %demand_own_ref.3, ...), custom_call_target="tpu_custom_call" | custom-call | tf_op jit(solution)/shard_map/pallas_call | solution.py:35
  44.3 6.8 %collective-permute-done.4.b_ref = s16[96,2048]{1,0:T(8,128)(2,1)S(1)} collective-permute-done((s16[96,2048]{1,0:T(8,128)(2,1)}, s16[96,2048]{1,0:T(8,128)(2,1)S(1)}, u32[]{:S(2)}, u32[]{:S(2)}) %collective-permute-start.4) | collective-permute-done | bytes 393248 | tf_op jit(solution)/shard_map/ppermute | solution.py:324
  51.1 9.5 %collective-permute-done.5.c_ref = s16[96,2048]{1,0:T(8,128)(2,1)S(1)} collective-permute-done((s16[96,2048]{1,0:T(8,128)(2,1)}, s16[96,2048]{1,0:T(8,128)(2,1)S(1)}, u32[]{:S(2)}, u32[]{:S(2)}) %collective-permute-start.5) | collective-permute-done | bytes 393248 | tf_op jit(solution)/shard_map/ppermute | solution.py:324
  70.4 5.4 %all-to-all-start = ((f32[24,32,128]{2,1,0:T(8,128)}), f32[24,32,128]{2,1,0:T(8,128)S(1)}, u32[]{:S(2)}, u32[]{:S(2)}) async-start(f32[24,32,128]{2,1,0:T(8,128)} %shard_map.131), calls=%async_computation | async-start | bytes 786432 | tf_op jit(solution)/shard_map/all_to_all | solution.py:362
  84.0 5.0 %collective-permute-done.8.got_ref = bf16[48,2048]{1,0:T(8,128)(2,1)S(1)} collective-permute-done((bf16[48,2048]{1,0:T(8,128)(2,1)}, bf16[48,2048]{1,0:T(8,128)(2,1)S(1)}, u32[]{:S(2)}, u32[]{:S(2)}) %collective-permute-start.8) | collective-permute-done | bytes 196640 | tf_op jit(solution)/shard_map/ppermute | solution.py:328
  99.0 6.5 %collective-permute-done.10.c_ref = bf16[96,2048]{1,0:T(8,128)(2,1)S(1)} collective-permute-done((bf16[96,2048]{1,0:T(8,128)(2,1)}, bf16[96,2048]{1,0:T(8,128)(2,1)S(1)}, u32[]{:S(2)}, u32[]{:S(2)}) %collective-permute-start.10) | collective-permute-done | bytes 393248 | tf_op jit(solution)/shard_map/ppermute | solution.py:324
  105.6 4.9 %collective-permute-done.11.d_ref = bf16[96,2048]{1,0:T(8,128)(2,1)S(1)} collective-permute-done((bf16[96,2048]{1,0:T(8,128)(2,1)}, bf16[96,2048]{1,0:T(8,128)(2,1)S(1)}, u32[]{:S(2)}, u32[]{:S(2)}) %collective-permute-start.11) | collective-permute-done | bytes 393248 | tf_op jit(solution)/shard_map/ppermute | solution.py:324
  112.2 4.0 %shard_map.140 = (f32[8,48,256]{2,1,0:T(8,128)}, f32[8,48,256]{2,1,0:T(8,128)}) custom-call(s32[3]{0:T(128)} %pad_add_fusion.where_ref, bf16[96,2048]{1,0:T(8,128)(2,1)} %shard_map.139.a_ref, bf16[96,2048]{1,0:T(8,128)(2,1)} %copy-done.15, bf16[96,2048]{1,0:T(8,128)(2,1)} %copy-done.13, bf16[96,2048]{1,0:T(8,128)(2,1)} %copy-done.14, ...), custom_call_target="tpu_custom_call" | custom-call | tf_op jit(solution)/shard_map/pallas_call | solution.py:35
  120.4 14.6 %all_to_all.30.means_ref = f32[24,32,128]{2,1,0:T(8,128)} all-to-all(f32[24,32,128]{2,1,0:T(8,128)} %shard_map.132), channel_id=1, replica_groups=mesh['ylo'=2,'z'=4,'yhi'=2,'x'=4,'core'=2] {'ylo','z'}, dimensions={0} | all-to-all | bytes 786432 | tf_op jit(solution)/shard_map/all_to_all | solution.py:366
  135.7 3.8 %shard_map.141 = (f32[16,48,250]{2,1,0:T(8,128)}, f32[8,48,250]{2,1,0:T(8,128)}, f32[16,48,250]{2,1,0:T(8,128)}) custom-call(s32[3]{0:T(128)} %pad_add_fusion.where_ref, s32[64]{0:T(128)} %reshape.61.ids_ref, f32[16,48,250]{2,1,0:T(8,128)} %dispatch_ref.1, f32[16,48,250]{2,1,0:T(8,128)} %prices_ref.1, f32[24,32,128]{2,1,0:T(8,128)} %all_to_all.30.means_ref, ...), custom_call_target="tpu_custom_call" | custom-call | tf_op jit(solution)/shard_map/pallas_call | solution.py:35
  142.2 9.3 %shard_map.144 = (s16[96,2048]{1,0:T(8,128)(2,1)}, s16[96,2048]{1,0:T(8,128)(2,1)}, s16[96,2048]{1,0:T(8,128)(2,1)}, s16[96,2048]{1,0:T(8,128)(2,1)}) custom-call(s32[3]{0:T(128)} %pad_add_fusion.where_ref, f32[16,48,250]{2,1,0:T(8,128)} %get-tuple-element.39.field_ref.own_ref.dispatch_ref, f32[8,48,250]{2,1,0:T(8,128)} %copy-done.4, ...), custom_call_target="tpu_custom_call" | custom-call | tf_op jit(solution)/shard_map/pallas_call | solution.py:35
  155.8 8.4 %collective-permute-done.14.b_ref = s16[96,2048]{1,0:T(8,128)(2,1)S(1)} collective-permute-done((s16[96,2048]{1,0:T(8,128)(2,1)}, s16[96,2048]{1,0:T(8,128)(2,1)S(1)}, u32[]{:S(2)}, u32[]{:S(2)}) %collective-permute-start.14) | collective-permute-done | bytes 393248 | tf_op jit(solution)/shard_map/ppermute | solution.py:324
  164.1 9.3 %collective-permute-done.15.c_ref = s16[96,2048]{1,0:T(8,128)(2,1)S(1)} collective-permute-done((s16[96,2048]{1,0:T(8,128)(2,1)}, s16[96,2048]{1,0:T(8,128)(2,1)S(1)}, u32[]{:S(2)}, u32[]{:S(2)}) %collective-permute-start.15) | collective-permute-done | bytes 393248 | tf_op jit(solution)/shard_map/ppermute | solution.py:324
  178.8 6.0 %collective-permute-done.17.got_ref = s16[48,2048]{1,0:T(8,128)(2,1)S(1)} collective-permute-done((s16[48,2048]{1,0:T(8,128)(2,1)}, s16[48,2048]{1,0:T(8,128)(2,1)S(1)}, u32[]{:S(2)}, u32[]{:S(2)}) %collective-permute-start.17) | collective-permute-done | bytes 196640 | tf_op jit(solution)/shard_map/ppermute | solution.py:328
  189.3 5.5 %collective-permute-done.18.got_ref = bf16[48,2048]{1,0:T(8,128)(2,1)S(1)} collective-permute-done((bf16[48,2048]{1,0:T(8,128)(2,1)}, bf16[48,2048]{1,0:T(8,128)(2,1)S(1)}, u32[]{:S(2)}, u32[]{:S(2)}) %collective-permute-start.18) | collective-permute-done | bytes 196640 | tf_op jit(solution)/shard_map/ppermute | solution.py:328
  207.2 8.9 %collective-permute-done.19.b_ref = bf16[96,2048]{1,0:T(8,128)(2,1)S(1)} collective-permute-done((bf16[96,2048]{1,0:T(8,128)(2,1)}, bf16[96,2048]{1,0:T(8,128)(2,1)S(1)}, u32[]{:S(2)}, u32[]{:S(2)}) %collective-permute-start.19) | collective-permute-done | bytes 393248 | tf_op jit(solution)/shard_map/ppermute | solution.py:324
  220.3 3.9 %shard_map.148 = (f32[8,48,256]{2,1,0:T(8,128)}, f32[8,48,256]{2,1,0:T(8,128)}) custom-call(s32[3]{0:T(128)} %pad_add_fusion.where_ref, bf16[96,2048]{1,0:T(8,128)(2,1)} %shard_map.147.a_ref, bf16[96,2048]{1,0:T(8,128)(2,1)} %copy-done.16, bf16[96,2048]{1,0:T(8,128)(2,1)} %copy-done.17, bf16[96,2048]{1,0:T(8,128)(2,1)} %copy-done.18, ...), custom_call_target="tpu_custom_call" | custom-call | tf_op jit(solution)/shard_map/pallas_call | solution.py:35
  227.0 13.7 %all_to_all.31.means_ref = f32[24,32,128]{2,1,0:T(8,128)} all-to-all(f32[24,32,128]{2,1,0:T(8,128)} %shard_map.143), channel_id=1, replica_groups=mesh['ylo'=2,'z'=4,'yhi'=2,'x'=4,'core'=2] {'ylo','z'}, dimensions={0} | all-to-all | bytes 786432 | tf_op jit(solution)/shard_map/all_to_all | solution.py:366
  241.5 3.8 %shard_map.149 = (f32[16,48,250]{2,1,0:T(8,128)}, f32[8,48,250]{2,1,0:T(8,128)}, f32[16,48,250]{2,1,0:T(8,128)}) custom-call(s32[3]{0:T(128)} %pad_add_fusion.where_ref, s32[64]{0:T(128)} %reshape.61.ids_ref, f32[16,48,250]{2,1,0:T(8,128)} %get-tuple-element.39.field_ref.own_ref.dispatch_ref, f32[16,48,250]{2,1,0:T(8,128)} %get-tuple-element.40.prices_ref, ...), custom_call_target="tpu_custom_call" | custom-call | tf_op jit(solution)/shard_map/pallas_call | solution.py:35
  247.6 12.3 %all_to_all.32.got_ref = f32[24,32,128]{2,1,0:T(8,128)} all-to-all(f32[24,32,128]{2,1,0:T(8,128)} %shard_map.150), channel_id=1, replica_groups=mesh['ylo'=2,'z'=4,'yhi'=2,'x'=4,'core'=2] {'ylo','z'}, dimensions={0} | all-to-all | bytes 786432 | tf_op jit(solution)/shard_map/all_to_all | solution.py:362
  262.0 12.1 %all_to_all.33.means_ref = f32[24,32,128]{2,1,0:T(8,128)} all-to-all(f32[24,32,128]{2,1,0:T(8,128)} %shard_map.151), channel_id=1, replica_groups=mesh['ylo'=2,'z'=4,'yhi'=2,'x'=4,'core'=2] {'ylo','z'}, dimensions={0} | all-to-all | bytes 786432 | tf_op jit(solution)/shard_map/all_to_all | solution.py:366
  (130 shorter events, 99.0 us)
Async XLA Ops:
  0.6 10.1 %collective-permute-start.3 = (bf16[625,2000]{0,1:T(8,128)(2,1)}, bf16[625,2000]{0,1:T(8,128)(2,1)}, u32[]{:S(2)}, u32[]{:S(2)}) collective-permute-start(bf16[625,2000]{0,1:T(8,128)(2,1)} %param.13), channel_id=1, source_target_pairs={{0,1},{1,0},{2,3},{3,2},{4,5},{5,4},{6,7},{7,6},{8,9},{9,8},{10,11... | collective-permute-start | bytes 7500008 | tf_op jit(solution)/shard_map/ppermute | solution.py:328
  2.6 25.7 %collective-permute-start.1 = (bf16[8,48,625]{2,1,0:T(8,128)(2,1)}, bf16[8,48,625]{2,1,0:T(8,128)(2,1)S(1)}, u32[]{:S(2)}, u32[]{:S(2)}) collective-permute-start(bf16[8,48,625]{2,1,0:T(8,128)(2,1)} %constant_dynamic-slice_fusion), channel_id=1, source_target_pairs={{0,1},{1,0},{2,3},{3,2},{4,5},{5,4},{6,7},{7,6},{8,9},{9,8},{10,11... | collective-permute-start | bytes 1440008 | tf_op jit(solution)/shard_map/ppermute | solution.py:328
  4.8 23.4 %collective-permute-start = (f32[8,48,250]{2,1,0:T(8,128)}, f32[8,48,250]{2,1,0:T(8,128)S(1)}, u32[]{:S(2)}, u32[]{:S(2)}) collective-permute-start(f32[8,48,250]{2,1,0:T(8,128)} %constant_dynamic-slice_fusion.1), channel_id=1, source_target_pairs={{0,1},{1,0},{2,3},{3,2},{4,5},{5,4},{6,7},{7,6},{8,9},{9,8},{10,11... | collective-permute-start | bytes 1152008 | tf_op jit(solution)/shard_map/ppermute | solution.py:328
  5.6 4.6 %collective-permute-start.2 = (f32[250]{0:T(256)S(1)}, f32[250]{0:T(256)S(1)}, u32[]{:S(2)}, u32[]{:S(2)}) collective-permute-start(f32[250]{0:T(256)S(1)} %convert_element_type.23), channel_id=1, source_target_pairs={{0,1},{1,0},{2,3},{3,2},{4,5},{5,4},{6,7},{7,6},{8,9},{9,8},{10,11... | collective-permute-start | bytes 3008 | tf_op jit(solution)/shard_map/ppermute | solution.py:328
  38.5 12.6 %collective-permute-start.4 = (s16[96,2048]{1,0:T(8,128)(2,1)}, s16[96,2048]{1,0:T(8,128)(2,1)S(1)}, u32[]{:S(2)}, u32[]{:S(2)}) collective-permute-start(s16[96,2048]{1,0:T(8,128)(2,1)} %get-tuple-element.30), channel_id=1, source_target_pairs={{0,2},{2,4},{4,6},{6,0},{1,3},{3,5},{5,7},{7,1},{8,10},{10,12},{12... | collective-permute-start | bytes 1179656 | tf_op jit(solution)/shard_map/ppermute | solution.py:324
  40.2 20.4 %collective-permute-start.5 = (s16[96,2048]{1,0:T(8,128)(2,1)}, s16[96,2048]{1,0:T(8,128)(2,1)S(1)}, u32[]{:S(2)}, u32[]{:S(2)}) collective-permute-start(s16[96,2048]{1,0:T(8,128)(2,1)} %get-tuple-element.31), channel_id=1, source_target_pairs={{0,4},{2,6},{4,0},{6,2},{1,5},{3,7},{5,1},{7,3},{8,12},{10,14},{12... | collective-permute-start | bytes 1179656 | tf_op jit(solution)/shard_map/ppermute | solution.py:324
  42.9 17.7 %collective-permute-start.6 = (s16[96,2048]{1,0:T(8,128)(2,1)}, s16[96,2048]{1,0:T(8,128)(2,1)S(1)}, u32[]{:S(2)}, u32[]{:S(2)}) collective-permute-start(s16[96,2048]{1,0:T(8,128)(2,1)} %get-tuple-element.32), channel_id=1, source_target_pairs={{0,6},{2,0},{4,2},{6,4},{1,7},{3,1},{5,3},{7,5},{8,14},{10,8},{12,... | collective-permute-start | bytes 1179656 | tf_op jit(solution)/shard_map/ppermute | solution.py:324
  64.2 14.7 %collective-permute-start.7 = (s16[48,2048]{1,0:T(8,128)(2,1)}, s16[48,2048]{1,0:T(8,128)(2,1)S(1)}, u32[]{:S(2)}, u32[]{:S(2)}) collective-permute-start(s16[48,2048]{1,0:T(8,128)(2,1)} %get-tuple-element.34), channel_id=1, source_target_pairs={{0,8},{8,0},{1,9},{9,1},{2,10},{10,2},{3,11},{11,3},{4,12},{12,4},... | collective-permute-start | bytes 589832 | tf_op jit(solution)/shard_map/ppermute | solution.py:328
  70.4 47.1 %all-to-all-start = ((f32[24,32,128]{2,1,0:T(8,128)}), f32[24,32,128]{2,1,0:T(8,128)S(1)}, u32[]{:S(2)}, u32[]{:S(2)}) async-start(f32[24,32,128]{2,1,0:T(8,128)} %shard_map.131), calls=%async_computation | async-start | bytes 786432 | tf_op jit(solution)/shard_map/all_to_all | solution.py:362
  81.6 7.4 %collective-permute-start.8 = (bf16[48,2048]{1,0:T(8,128)(2,1)}, bf16[48,2048]{1,0:T(8,128)(2,1)S(1)}, u32[]{:S(2)}, u32[]{:S(2)}) collective-permute-start(bf16[48,2048]{1,0:T(8,128)(2,1)} %shard_map.138.own_ref), channel_id=1, source_target_pairs={{0,8},{8,0},{1,9},{9,1},{2,10},{10,2},{3,11},{11,3},{4,12},{12,4},... | collective-permute-start | bytes 589832 | tf_op jit(solution)/shard_map/ppermute | solution.py:328
  91.8 13.8 %collective-permute-start.10 = (bf16[96,2048]{1,0:T(8,128)(2,1)}, bf16[96,2048]{1,0:T(8,128)(2,1)S(1)}, u32[]{:S(2)}, u32[]{:S(2)}) collective-permute-start(bf16[96,2048]{1,0:T(8,128)(2,1)} %shard_map.139.a_ref), channel_id=1, source_target_pairs={{0,4},{2,6},{4,0},{6,2},{1,5},{3,7},{5,1},{7,3},{8,12},{10,14},{12... | collective-permute-start | bytes 1179656 | tf_op jit(solution)/shard_map/ppermute | solution.py:324
  94.2 16.2 %collective-permute-start.11 = (bf16[96,2048]{1,0:T(8,128)(2,1)}, bf16[96,2048]{1,0:T(8,128)(2,1)S(1)}, u32[]{:S(2)}, u32[]{:S(2)}) collective-permute-start(bf16[96,2048]{1,0:T(8,128)(2,1)} %shard_map.139.a_ref), channel_id=1, source_target_pairs={{0,2},{2,4},{4,6},{6,0},{1,3},{3,5},{5,7},{7,1},{8,10},{10,12},{12... | collective-permute-start | bytes 1179656 | tf_op jit(solution)/shard_map/ppermute | solution.py:324
  95.3 16.2 %collective-permute-start.9 = (bf16[96,2048]{1,0:T(8,128)(2,1)}, bf16[96,2048]{1,0:T(8,128)(2,1)S(1)}, u32[]{:S(2)}, u32[]{:S(2)}) collective-permute-start(bf16[96,2048]{1,0:T(8,128)(2,1)} %shard_map.139.a_ref), channel_id=1, source_target_pairs={{0,6},{2,0},{4,2},{6,4},{1,7},{3,1},{5,3},{7,5},{8,14},{10,8},{12,... | collective-permute-start | bytes 1179656 | tf_op jit(solution)/shard_map/ppermute | solution.py:324
  116.2 18.7 %collective-permute-start.12 = (f32[8,48,256]{2,1,0:T(8,128)}, f32[8,48,256]{2,1,0:T(8,128)S(1)}, u32[]{:S(2)}, u32[]{:S(2)}) collective-permute-start(f32[8,48,256]{2,1,0:T(8,128)} %get-tuple-element.38), channel_id=1, source_target_pairs={{0,1},{1,0},{2,3},{3,2},{4,5},{5,4},{6,7},{7,6},{8,9},{9,8},{10,11... | collective-permute-start | bytes 1179656 | tf_op jit(solution)/shard_map/ppermute | solution.py:328
  151.6 12.6 %collective-permute-start.14 = (s16[96,2048]{1,0:T(8,128)(2,1)}, s16[96,2048]{1,0:T(8,128)(2,1)S(1)}, u32[]{:S(2)}, u32[]{:S(2)}) collective-permute-start(s16[96,2048]{1,0:T(8,128)(2,1)} %get-tuple-element.43), channel_id=1, source_target_pairs={{0,2},{2,4},{4,6},{6,0},{1,3},{3,5},{5,7},{7,1},{8,10},{10,12},{12... | collective-permute-start | bytes 1179656 | tf_op jit(solution)/shard_map/ppermute | solution.py:324
  152.0 21.5 %collective-permute-start.15 = (s16[96,2048]{1,0:T(8,128)(2,1)}, s16[96,2048]{1,0:T(8,128)(2,1)S(1)}, u32[]{:S(2)}, u32[]{:S(2)}) collective-permute-start(s16[96,2048]{1,0:T(8,128)(2,1)} %get-tuple-element.44), channel_id=1, source_target_pairs={{0,4},{2,6},{4,0},{6,2},{1,5},{3,7},{5,1},{7,3},{8,12},{10,14},{12... | collective-permute-start | bytes 1179656 | tf_op jit(solution)/shard_map/ppermute | solution.py:324
  155.6 17.8 %collective-permute-start.16 = (s16[96,2048]{1,0:T(8,128)(2,1)}, s16[96,2048]{1,0:T(8,128)(2,1)S(1)}, u32[]{:S(2)}, u32[]{:S(2)}) collective-permute-start(s16[96,2048]{1,0:T(8,128)(2,1)} %get-tuple-element.45), channel_id=1, source_target_pairs={{0,6},{2,0},{4,2},{6,4},{1,7},{3,1},{5,3},{7,5},{8,14},{10,8},{12,... | collective-permute-start | bytes 1179656 | tf_op jit(solution)/shard_map/ppermute | solution.py:324
  177.0 7.8 %collective-permute-start.17 = (s16[48,2048]{1,0:T(8,128)(2,1)}, s16[48,2048]{1,0:T(8,128)(2,1)S(1)}, u32[]{:S(2)}, u32[]{:S(2)}) collective-permute-start(s16[48,2048]{1,0:T(8,128)(2,1)} %get-tuple-element.47), channel_id=1, source_target_pairs={{0,8},{8,0},{1,9},{9,1},{2,10},{10,2},{3,11},{11,3},{4,12},{12,4},... | collective-permute-start | bytes 589832 | tf_op jit(solution)/shard_map/ppermute | solution.py:328
  187.4 7.4 %collective-permute-start.18 = (bf16[48,2048]{1,0:T(8,128)(2,1)}, bf16[48,2048]{1,0:T(8,128)(2,1)S(1)}, u32[]{:S(2)}, u32[]{:S(2)}) collective-permute-start(bf16[48,2048]{1,0:T(8,128)(2,1)} %shard_map.146.own_ref), channel_id=1, source_target_pairs={{0,8},{8,0},{1,9},{9,1},{2,10},{10,2},{3,11},{11,3},{4,12},{12,4},... | collective-permute-start | bytes 589832 | tf_op jit(solution)/shard_map/ppermute | solution.py:328
  197.3 18.8 %collective-permute-start.19 = (bf16[96,2048]{1,0:T(8,128)(2,1)}, bf16[96,2048]{1,0:T(8,128)(2,1)S(1)}, u32[]{:S(2)}, u32[]{:S(2)}) collective-permute-start(bf16[96,2048]{1,0:T(8,128)(2,1)} %shard_map.147.a_ref), channel_id=1, source_target_pairs={{0,6},{2,0},{4,2},{6,4},{1,7},{3,1},{5,3},{7,5},{8,14},{10,8},{12,... | collective-permute-start | bytes 1179656 | tf_op jit(solution)/shard_map/ppermute | solution.py:324
  200.6 15.5 %collective-permute-start.20 = (bf16[96,2048]{1,0:T(8,128)(2,1)}, bf16[96,2048]{1,0:T(8,128)(2,1)S(1)}, u32[]{:S(2)}, u32[]{:S(2)}) collective-permute-start(bf16[96,2048]{1,0:T(8,128)(2,1)} %shard_map.147.a_ref), channel_id=1, source_target_pairs={{0,4},{2,6},{4,0},{6,2},{1,5},{3,7},{5,1},{7,3},{8,12},{10,14},{12... | collective-permute-start | bytes 1179656 | tf_op jit(solution)/shard_map/ppermute | solution.py:324
  200.9 18.6 %collective-permute-start.21 = (bf16[96,2048]{1,0:T(8,128)(2,1)}, bf16[96,2048]{1,0:T(8,128)(2,1)S(1)}, u32[]{:S(2)}, u32[]{:S(2)}) collective-permute-start(bf16[96,2048]{1,0:T(8,128)(2,1)} %shard_map.147.a_ref), channel_id=1, source_target_pairs={{0,2},{2,4},{4,6},{6,0},{1,3},{3,5},{5,7},{7,1},{8,10},{10,12},{12... | collective-permute-start | bytes 1179656 | tf_op jit(solution)/shard_map/ppermute | solution.py:324
  203.7 20.5 %all-to-all-start.2 = ((f32[24,32,128]{2,1,0:T(8,128)}), f32[24,32,128]{2,1,0:T(8,128)S(1)}, u32[]{:S(2)}, u32[]{:S(2)}) async-start(f32[24,32,128]{2,1,0:T(8,128)} %shard_map.142), calls=%async_computation.2 | async-start | bytes 786432 | tf_op jit(solution)/shard_map/all_to_all | solution.py:362
  224.2 16.5 %collective-permute-start.22 = (f32[8,48,256]{2,1,0:T(8,128)}, f32[8,48,256]{2,1,0:T(8,128)S(1)}, u32[]{:S(2)}, u32[]{:S(2)}) collective-permute-start(f32[8,48,256]{2,1,0:T(8,128)} %get-tuple-element.49), channel_id=1, source_target_pairs={{0,1},{1,0},{2,3},{3,2},{4,5},{5,4},{6,7},{7,6},{8,9},{9,8},{10,11... | collective-permute-start | bytes 1179656 | tf_op jit(solution)/shard_map/ppermute | solution.py:328
  (28 other events, 165.9 us)

commit v2 on v1

v2 whole, which is shorter than its diff:
```python
import functools

import jax
import jax.numpy as jnp
from jax import lax
from jax.experimental import pallas as pl
from jax.experimental.pallas import tpu as pltpu
from jax.sharding import Mesh, PartitionSpec as P

BUSES = 10000
SECTION2_NODES = 4
SECTION3_NODES = 8
ITERS = 2

F32 = jnp.float32
BF16 = jnp.bfloat16
LINES = 2000
LANES = 2048
BALANCE_SCALE = 8.0
UNIT_PAD = 256
SPAN = 12
NODE_FIRST = (0, 1, 5)
NODE_WIDTH = (1, SECTION2_NODES, SECTION3_NODES)
SENDS = (6, 5, 7, 2, 4, 1, 3)
ROWS = 32
VMEM = pl.BlockSpec(memory_space=pltpu.VMEM)
SMEM = pl.BlockSpec(memory_space=pltpu.SMEM)
PARAMS = pltpu.CompilerParams(vmem_limit_bytes=56 * 1024 * 1024)


def call(kernel, outs, scratch=(), after=0):
    def run(*args):
        specs = [SMEM if a.dtype == jnp.int32 and a.ndim == 1 else VMEM for a in args]
        if after:
            specs[-after:] = [pl.BlockSpec(memory_space=pl.ANY)] * after
        many = isinstance(outs, (list, tuple))
        return pl.pallas_call(
            kernel,
            out_shape=list(outs) if many else outs,
            in_specs=specs,
            out_specs=[VMEM for _ in outs] if many else VMEM,
            scratch_shapes=list(scratch),
            compiler_params=PARAMS,
        )(*args)

    return run


def shape(dims, dtype):
    return jax.ShapeDtypeStruct(dims, dtype)


def parts3(x):
    hi = x.astype(BF16)
    rest = x - hi.astype(F32)
    mid = rest.astype(BF16)
    low = (rest - mid.astype(F32)).astype(BF16)
    return hi, mid, low


def mm(a, b, dims):
    return lax.dot_general(a, b, (dims, ((), ())), preferred_element_type=F32)


NN = ((1,), (0,))
NT = ((1,), (1,))
TN = ((0,), (0,))


def mm3(a, b, dims):
    return sum(mm(part, b, dims) for part in parts3(a))


def excess(x, limit):
    return x - jnp.minimum(jnp.maximum(x, -limit), limit)


def prepare_kernel(bus_ref, ptdf_ref, pick_ref, rows_ref):
    buses, units = pick_ref.shape
    rows = lax.broadcasted_iota(jnp.int32, (buses, units), 0)
    pick = (rows == bus_ref[...]).astype(F32).astype(BF16)
    pick_ref[...] = pick
    rows_ref[:LINES, :] = mm(ptdf_ref[...], pick, NN).astype(BF16)
    spare = lax.broadcasted_iota(jnp.int32, (LANES - LINES, units), 0) < 2
    rows_ref[LINES:, :] = spare.astype(F32).astype(BF16)


def limits_kernel(ids_ref, table_ref, out_ref):
    ids = ids_ref[...]
    low = ids & 127
    high = ids >> 7
    lanes = lax.broadcasted_iota(jnp.int32, (128, LANES), 0)
    spread = mm3(table_ref[...], (lanes == low).astype(F32).astype(BF16), NN)
    rows = lax.broadcasted_iota(jnp.int32, spread.shape, 0)
    out_ref[...] = jnp.sum(jnp.where(rows == high, spread, 0.0), axis=0, keepdims=True)


def flows_kernel(
    where_ref,
    own_ref,
    other_ref,
    demand_own_ref,
    demand_other_ref,
    pick_own_ref,
    pick_other_ref,
    ptdf_own_ref,
    ptdf_other_ref,
    *outs,
):
    x, y, core = where_ref[0], where_ref[1], where_ref[2]
    hours = other_ref.shape[1]
    order = [4 * lax.rem(y + r // 4, 2) + lax.rem(x + r % 4, 4) for r in range(8)]

    def injected(dispatch_ref, demand_ref, pick_ref):
        first = 8 * core if dispatch_ref.shape[0] > 8 else 0
        dispatch = jnp.concatenate([dispatch_ref[first + s] for s in order], axis=0)
        demand = jnp.concatenate([demand_ref[8 * core + s].astype(F32) for s in order], axis=0)
        power = mm3(dispatch, pick_ref[...], NT)
        return (power - demand).astype(BF16)

    own = injected(own_ref, demand_own_ref, pick_own_ref)
    other = injected(other_ref, demand_other_ref, pick_other_ref)
    balance = jnp.sum(own.astype(F32), axis=1, keepdims=True)
    balance = balance + jnp.sum(other.astype(F32), axis=1, keepdims=True)
    total = mm(own, ptdf_own_ref[...], NT) + mm(other, ptdf_other_ref[...], NT)
    most = jnp.max(jnp.abs(total), axis=1, keepdims=True)
    power = jnp.floor(14.9 - jnp.log2(jnp.maximum(most, 1e-6)))
    code = total * jnp.exp2(power)
    lanes = lax.broadcasted_iota(jnp.int32, (code.shape[0], LANES - LINES), 1)
    spare = jnp.where(lanes == 0, balance * BALANCE_SCALE, jnp.where(lanes == 1, power, 0.0))
    code = jnp.concatenate([code, spare], axis=1)
    code = jnp.round(code).astype(jnp.int32).astype(jnp.int16)
    for r in range(8):
        outs[r][...] = code[r * hours : (r + 1) * hours]


def slopes_kernel(*refs):
    codes, limits_ref, out_ref = refs[:8], refs[8], refs[-1]
    lanes = lax.broadcasted_iota(jnp.int32, out_ref.shape, 1)
    flows = jnp.zeros(out_ref.shape, F32)
    for ref in codes:
        code = ref[...].astype(jnp.int32).astype(F32)
        scale = jnp.exp2(-code[:, LINES + 1 : LINES + 2])
        flows = flows + code * jnp.where(lanes == LINES, 1.0 / BALANCE_SCALE, scale)
    slopes = excess(flows, limits_ref[...])
    balance = flows[:, LINES : LINES + 1] * (0.5 / BUSES)
    high = balance.astype(BF16).astype(F32)
    slopes = jnp.where(lanes == LINES, high, slopes)
    slopes = jnp.where(lanes == LINES + 1, balance - high, slopes)
    out_ref[...] = jnp.where(lanes > LINES + 1, 0.0, slopes).astype(BF16)


def pull_kernel(where_ref, *refs):
    blocks, (rows_own_ref, rows_other_ref), (own_ref, send_ref) = refs[:8], refs[8:10], refs[-2:]
    x, y = where_ref[0], where_ref[1]
    hours = own_ref.shape[1]
    slopes = jnp.concatenate([ref[...] for ref in blocks], axis=0)
    for rows_ref, out_ref in ((rows_other_ref, send_ref), (rows_own_ref, own_ref)):
        pull = mm(slopes, rows_ref[...], NN)
        for r in range(8):
            s = 4 * lax.rem(y + r // 4, 2) + lax.rem(x + r % 4, 4)
            out_ref[s] = pull[r * hours : (r + 1) * hours]


def pack_kernel(ids_ref, field_ref, out_ref, wide):
    count, hours, units = field_ref.shape
    wide[...] = jnp.zeros(wide.shape, F32)
    for s in range(count):
        wide[s, :, :units] = field_ref[s, 3 * SPAN :, :]
    for section in range(3):
        cut = slice(section * SPAN, (section + 1) * SPAN)
        for node in range(NODE_WIDTH[section]):
            total = jnp.zeros((SPAN, units), F32)
            for s in range(count):
                inside = ids_ref[section * count + s] == node
                total = total + jnp.where(inside, field_ref[s, cut, :], 0.0)
            wide[count + NODE_FIRST[section] + node, :, :units] = total
    for tile in range(2):
        block = jnp.swapaxes(wide[:, :, tile * 128 : (tile + 1) * 128], 0, 1)
        for hour in range(SPAN):
            out_ref[2 * hour + tile] = block[hour]


def means_kernel(got_ref, leaf_row_ref, leaf_column_ref, counts_ref, out_ref):
    scenarios = leaf_row_ref.shape[1]
    parts = scenarios // 16
    same = leaf_row_ref[...] == leaf_column_ref[...]
    table = same.astype(F32)
    size = jnp.maximum(jnp.sum(table, axis=1, keepdims=True), 1.0)
    table = table.astype(BF16)
    for unit in range(3):
        rows = jnp.concatenate([got_ref[3 * p + unit, :16, :] for p in range(parts)], axis=0)
        leaf = sum(mm(table, part, NN) for part in parts3(rows)) / size
        sums = got_ref[unit, 16:, :]
        for p in range(1, parts):
            sums = sums + got_ref[3 * p + unit, 16:, :]
        node = sums / counts_ref[...]
        for p in range(parts):
            out_ref[3 * p + unit, :16, :] = leaf[16 * p : 16 * (p + 1)]
            out_ref[3 * p + unit, 16:, :] = node


def unpack(ids_ref, means_ref, wide, count):
    for tile in range(2):
        block = jnp.stack([means_ref[2 * hour + tile] for hour in range(SPAN)], axis=0)
        wide[:, :, tile * 128 : (tile + 1) * 128] = jnp.swapaxes(block, 0, 1)

    def average(s, units):
        pieces = []
        for section in range(3):
            row = count + NODE_FIRST[section] + ids_ref[section * count + s]
            pieces.append(wide[row])
        pieces.append(wide[s])
        return jnp.concatenate(pieces, axis=0)[:, :units]

    return average


def gradient_kernel(
    advance,
    where_ref,
    ids_ref,
    dispatch_ref,
    prices_ref,
    means_ref,
    pull_own_ref,
    pull_other_ref,
    quad_ref,
    linear_ref,
    cap_ref,
    ramp_ref,
    out_ref,
    send_ref,
    prices_out_ref,
    wide,
):
    core = where_ref[2]
    count, hours, units = dispatch_ref.shape
    average_of = unpack(ids_ref, means_ref, wide, count)
    zero = jnp.zeros((1, units), F32)

    def one(s, pull):
        dispatch = dispatch_ref[s]
        average = average_of(s, units)
        prices = prices_ref[s]
        if advance:
            prices = prices + (dispatch - average)
        prices_out_ref[s] = prices
        change = jnp.concatenate([dispatch[1:] - dispatch[:-1], zero], axis=0)
        ramp = excess(change, ramp_ref[...])
        ramp_term = jnp.concatenate([zero, ramp[:-1]], axis=0) - ramp
        gradient = (
            quad_ref[...] * dispatch
            + linear_ref[...]
            + prices
            + (dispatch - average)
            + pull
            + ramp_term
        )
        new = jnp.minimum(jnp.maximum(dispatch - 0.25 * gradient, 0.0), cap_ref[...])
        out_ref[s] = new
        return new

    def step(i, carry):
        one(8 * core + i, pull_own_ref[i])
        send_ref[i] = one(8 * (1 - core) + i, pull_other_ref[i])
        return carry

    lax.fori_loop(0, 8, step, 0)


def prices_kernel(ids_ref, dispatch_ref, prices_ref, means_ref, out_ref, wide):
    count, hours, units = dispatch_ref.shape
    average_of = unpack(ids_ref, means_ref, wide, count)

    def step(s, carry):
        out_ref[s] = prices_ref[s] + (dispatch_ref[s] - average_of(s, units))
        return carry

    lax.fori_loop(0, count, step, 0)


def sent_to(value, r):
    pairs = [(y * 4 + x, (y + r // 4) % 2 * 4 + (x + r % 4) % 4) for y in range(2) for x in range(4)]
    return lax.ppermute(value, ("yhi", "x"), pairs)


def swapped(value):
    return lax.ppermute(value, "core", [(0, 1), (1, 0)])


def local(
    demand,
    ptdf,
    branch_limits,
    line_ids,
    unit_bus,
    node_map,
    cost_linear,
    cost_quad,
    capacity,
    ramp_limits,
    gen_init,
    price_init,
):
    count, hours, units = gen_init.shape
    buses = ptdf.shape[0]
    x, y, core = lax.axis_index("x"), lax.axis_index("yhi"), lax.axis_index("core")
    where = jnp.stack([x, y, core]).astype(jnp.int32)
    first = lax.axis_index(("ylo", "z")) * count
    ids = lax.dynamic_slice_in_dim(node_map, first, count, 1).reshape(-1)

    wide_scratch = pltpu.VMEM((ROWS, SPAN, UNIT_PAD), F32)
    flat = (3 * 8, ROWS, 128)
    counts = [
        jnp.sum((node_map[k][None, :] == jnp.arange(w, dtype=jnp.int32)[:, None]).astype(F32), axis=1)
        for k, w in zip(range(3), NODE_WIDTH)
    ]
    counts = jnp.maximum(jnp.concatenate(counts + [jnp.ones((3,), F32)]), 1.0)[:, None]

    def packed(field):
        sums = call(pack_kernel, shape(flat, F32), [wide_scratch])(ids, field)
        return lax.all_to_all(sums, ("ylo", "z"), 0, 0, tiled=True)

    def meaned(sums):
        return call(means_kernel, shape(flat, F32))(sums, node_map[3][None, :], node_map[3][:, None], counts)

    def returned(means):
        return lax.all_to_all(means, ("ylo", "z"), 0, 0, tiled=True)

    lines = ptdf.T
    lines_other = swapped(lines)
    bus_other = swapped(unit_bus)
    demand_other = swapped(demand)
    dispatch_other = swapped(gen_init)

    prepared = call(prepare_kernel, [shape((buses, units), BF16), shape((LANES, units), BF16)])
    pick_own, rows_own = prepared(unit_bus[None, :], lines)
    pick_other, rows_other = prepared(bus_other[None, :], lines_other)
    table = jnp.pad(branch_limits, (0, 96 * 128 - branch_limits.shape[0])).reshape(96, 128)
    limits = call(limits_kernel, shape((1, LANES), F32))(
        jnp.pad(line_ids, (0, LANES - LINES))[None, :], table
    )

    block = (hours, LANES)
    half = (8, hours, units)
    whole = (count, hours, units)

    dispatch, prices = gen_init, price_init
    for step in range(ITERS):
        codes = call(flows_kernel, [shape(block, jnp.int16)] * 8)(
            where,
            dispatch,
            dispatch_other,
            demand,
            demand_other,
            pick_own,
            pick_other,
            lines,
            lines_other,
        )
        got = [sent_to(codes[r], r) for r in SENDS]
        means = meaned(packed(dispatch))
        slopes = call(slopes_kernel, shape(block, BF16), after=1)(codes[0], *got, limits, means)
        means = returned(means)
        blocks = {r: sent_to(slopes, (r // 4) * 4 + (4 - r % 4) % 4) for r in SENDS}
        pull_own, pull_send = call(pull_kernel, [shape(half, F32)] * 2, after=1)(
            where, slopes, *[blocks[r] for r in range(1, 8)], rows_own, rows_other, means
        )
        pull_other = swapped(pull_send)
        dispatch, send, prices = call(
            functools.partial(gradient_kernel, step > 0),
            [shape(whole, F32), shape(half, F32), shape(whole, F32)],
            [wide_scratch],
        )(
            where,
            ids,
            dispatch,
            prices,
            means,
            pull_own,
            pull_other,
            cost_quad[None, :],
            cost_linear[None, :],
            capacity[None, :],
            ramp_limits[None, :],
        )
        if step + 1 < ITERS:
            dispatch_other = swapped(send)
    means = returned(meaned(packed(dispatch)))
    prices = call(prices_kernel, shape(whole, F32), [wide_scratch])(ids, dispatch, prices, means)
    return (dispatch, prices)


def solution(mesh):
    fine = Mesh(mesh.devices.reshape(2, 4, 2, 4, 2), ("ylo", "z", "yhi", "x", "core"))
    scen, area = ("ylo", "z"), ("yhi", "x", "core")
    return jax.shard_map(
        local,
        mesh=fine,
        in_specs=(
            P(scen, None, area),
            P(area, None),
            P(),
            P(),
            P(area),
            P(),
            P(area),
            P(area),
            P(area),
            P(area),
            P(scen, None, area),
            P(scen, None, area),
        ),
        out_specs=(P(scen, None, area), P(scen, None, area)),
        check_vma=False,
    )
```

time: 278 us -> 231 us (0.83)
  starting transfers between devices: 38.5 us -> 76.7 us
  waiting for transfers between devices: 77.2 us -> 44.2 us
  blocking collectives: 52.7 us -> 25.9 us
  local copies, waits for them, and re-layouts: 26.2 us -> 13.8 us
  Pallas kernels: 72.4 us -> 64.9 us
  other arithmetic: 8.99 us -> 3.54 us
    ppermute x23 -> x35, waiting for transfers between devices: 77.2 us -> 29.8 us  [the longest x28 24.2 us: sent_to(): return lax.ppermute(value, ('yhi', 'x'), pairs)]
    all_to_all x4 -> x2, blocking collectives: 52.7 us -> 25.9 us  [the longest x1 13.9 us: packed(): return lax.all_to_all(sums, ('ylo', 'z'), 0, 0, tiled=True)]
    ppermute x23 -> x35, starting transfers between devices: 29.6 us -> 55.6 us  [the longest x28 54.7 us: sent_to(): return lax.ppermute(value, ('yhi', 'x'), pairs)]
    all_to_all x2 -> x4, waiting for transfers between devices: 0.01 us -> 14.4 us  [the longest x2 10.2 us: returned(): return lax.all_to_all(means, ('ylo', 'z'), 0, 0, tiled=True)]
    all_to_all x2 -> x4, starting transfers between devices: 8.89 us -> 21.1 us  [the longest x2 11.2 us: packed(): return lax.all_to_all(sums, ('ylo', 'z'), 0, 0, tiled=True)]
    pallas_call x22 -> x18, Pallas kernels: 72.4 us -> 64.9 us  [run(): pl.pallas_call(kernel, out_shape=list(outs) if many else outs, in_specs=s...]
    select_n x1 -> x0, other arithmetic: 5.54 us -> none  [padded(): jnp.where((lane == LINES) | (lane == LINES + 1), jnp.ones((), BF16), wide)]
    unnamed x55 -> x78, local copies, waits for them, and re-layouts: 13.8 us -> 9.17 us
  transfers between devices with their start and end apart: 25 -> 39, of which waited for: 13 -> 12; matrix products, arithmetic and copies ran while one was open for 9% -> 4% of each run, Pallas kernels for 11% -> 12%
where the time goes in v2:
time: 231 us; the launch traced here: 230 us
  starting transfers between devices  76.7 us (33%)
  Pallas kernels  64.9 us (28%)
  waiting for transfers between devices  44.2 us (19%)
  blocking collectives  25.9 us (11%)
  local copies, waits for them, and re-layouts  13.8 us (6%)
  other arithmetic  3.54 us (2%)
    pallas_call x18, Pallas kernels, run(): pl.pallas_call(kernel, out_shape=list(outs) if many else outs, in_specs=s...  64.9 us
    ppermute x28, starting transfers between devices, sent_to(): return lax.ppermute(value, ('yhi', 'x'), pairs)  54.7 us
    ppermute x28, waiting for transfers between devices, sent_to(): return lax.ppermute(value, ('yhi', 'x'), pairs)  24.2 us
    all_to_all x1, blocking collectives, packed(): return lax.all_to_all(sums, ('ylo', 'z'), 0, 0, tiled=True)  13.9 us
    all_to_all x1, blocking collectives, returned(): return lax.all_to_all(means, ('ylo', 'z'), 0, 0, tiled=True)  12.1 us
    all_to_all x2, starting transfers between devices, packed(): return lax.all_to_all(sums, ('ylo', 'z'), 0, 0, tiled=True)  11.2 us
    all_to_all x2, waiting for transfers between devices, returned(): return lax.all_to_all(means, ('ylo', 'z'), 0, 0, tiled=True)  10.2 us
    all_to_all x2, starting transfers between devices, returned(): return lax.all_to_all(means, ('ylo', 'z'), 0, 0, tiled=True)  9.88 us
  transfers between devices with their start and end apart: 39, of which 12 were waited for; matrix products, arithmetic and copies ran while one was open for 4% of the time, Pallas kernels for 12%

profile of v2, /device:TPU:0, one launch (start us, length us, event | category | flops | bytes accessed | tf_op | source)
XLA Modules:
  0.0 230.0 jit_solution(8978426238661689511)
XLA Ops:
  4.9 6.4 %all-to-all-start = ((f32[24,32,128]{2,1,0:T(8,128)}), f32[24,32,128]{2,1,0:T(8,128)}, u32[]{:S(2)}, u32[]{:S(2)}) async-start(f32[24,32,128]{2,1,0:T(8,128)} %shard_map.131), calls=%async_computation | async-start | bytes 786432 | tf_op jit(solution)/shard_map/all_to_all | solution.py:323
  15.0 3.7 %shard_map.133 = (bf16[625,250]{1,0:T(8,128)(2,1)}, bf16[2048,250]{1,0:T(8,128)(2,1)}) custom-call(s32[1,250]{1,0:T(1,128)} %bitcast.37, bf16[2000,625]{1,0:T(8,128)(2,1)} %bitcast.25), custom_call_target="tpu_custom_call" | custom-call | tf_op jit(solution)/shard_map/pallas_call | solution.py:37
  20.2 3.7 %shard_map.134 = (bf16[625,250]{1,0:T(8,128)(2,1)}, bf16[2048,250]{1,0:T(8,128)(2,1)}) custom-call(s32[1,250]{1,0:T(1,128)} %bitcast.38, bf16[2000,625]{1,0:T(8,128)(2,1)} %copy-done), custom_call_target="tpu_custom_call" | custom-call | tf_op jit(solution)/shard_map/pallas_call | solution.py:37
  24.9 9.5 %shard_map.135 = (s16[48,2048]{1,0:T(8,128)(2,1)}, s16[48,2048]{1,0:T(8,128)(2,1)}, s16[48,2048]{1,0:T(8,128)(2,1)}, s16[48,2048]{1,0:T(8,128)(2,1)}, s16[48,204...) custom-call(s32[3]{0:T(128)} %pad_add_fusion.where_ref, ...), custom_call_target="tpu_custom_call" | custom-call | tf_op jit(solution)/shard_map/pallas_call | solution.py:37
  37.2 3.1 %collective-permute-start.4 = (s16[48,2048]{1,0:T(8,128)(2,1)}, s16[48,2048]{1,0:T(8,128)(2,1)S(1)}, u32[]{:S(2)}, u32[]{:S(2)}) collective-permute-start(s16[48,2048]{1,0:T(8,128)(2,1)} %get-tuple-element.34), channel_id=1, source_target_pairs={{0,12},{2,14},{4,8},{6,10},{8,4},{10,6},{12,0},{14,2},{1,13},{3,15... | collective-permute-start | bytes 589832 | tf_op jit(solution)/shard_map/ppermute | solution.py:285
  45.9 4.7 %collective-permute-start.6 = (s16[48,2048]{1,0:T(8,128)(2,1)}, s16[48,2048]{1,0:T(8,128)(2,1)S(1)}, u32[]{:S(2)}, u32[]{:S(2)}) collective-permute-start(s16[48,2048]{1,0:T(8,128)(2,1)} %get-tuple-element.36), channel_id=1, source_target_pairs={{0,14},{2,8},{4,10},{6,12},{8,6},{10,0},{12,2},{14,4},{1,15},{3,9}... | collective-permute-start | bytes 589832 | tf_op jit(solution)/shard_map/ppermute | solution.py:285
  55.5 5.5 %collective-permute-done.5.refs_2_ = s16[48,2048]{1,0:T(8,128)(2,1)S(1)} collective-permute-done((s16[48,2048]{1,0:T(8,128)(2,1)}, s16[48,2048]{1,0:T(8,128)(2,1)S(1)}, u32[]{:S(2)}, u32[]{:S(2)}) %collective-permute-start.5) | collective-permute-done | bytes 196640 | tf_op jit(solution)/shard_map/ppermute | solution.py:285
  69.0 5.1 %all-to-all-start.1 = ((f32[24,32,128]{2,1,0:T(8,128)}), f32[24,32,128]{2,1,0:T(8,128)S(1)}, u32[]{:S(2)}, u32[]{:S(2)}) async-start(f32[24,32,128]{2,1,0:T(8,128)} %shard_map.132.refs_9_), calls=%async_computation.1 | async-start | bytes 786432 | tf_op jit(solution)/shard_map/all_to_all | solution.py:329
  85.3 9.4 %all-to-all-done.1.refs_10_.means_ref = f32[24,32,128]{2,1,0:T(8,128)S(1)} async-done(((f32[24,32,128]{2,1,0:T(8,128)}), f32[24,32,128]{2,1,0:T(8,128)S(1)}, u32[]{:S(2)}, u32[]{:S(2)}) %all-to-all-start.1) | async-done | bytes 393248 | tf_op jit(solution)/shard_map/all_to_all | solution.py:329
  98.3 4.0 %shard_map.138 = (f32[8,48,250]{2,1,0:T(8,128)}, f32[8,48,250]{2,1,0:T(8,128)}) custom-call(s32[3]{0:T(128)} %pad_add_fusion.where_ref, bf16[48,2048]{1,0:T(8,128)(2,1)} %shard_map.137.refs_0_, bf16[48,2048]{1,0:T(8,128)(2,1)} %copy-done.8, bf16[48,2048]{1,0:T(8,128)(2,1)} %copy-done.10, bf16[48,2048]{1,0:T(8,128)(2,1)} %copy-done.12, ...), custom_call_target="tpu_custom_call" | custom-call | tf_op jit(solution)/shard_map/pallas_call | solution.py:37
  105.0 3.8 %shard_map.139 = (f32[16,48,250]{2,1,0:T(8,128)}, f32[8,48,250]{2,1,0:T(8,128)}, f32[16,48,250]{2,1,0:T(8,128)}) custom-call(s32[3]{0:T(128)} %pad_add_fusion.where_ref, s32[64]{0:T(128)} %reshape.61.ids_ref, f32[16,48,250]{2,1,0:T(8,128)} %dispatch_ref.1, f32[16,48,250]{2,1,0:T(8,128)} %prices_ref.1, f32[24,32,128]{2,1,0:T(8,128)} %copy-done.3, ...), custom_call_target="tpu_custom_call" | custom-call | tf_op jit(solution)/shard_map/pallas_call | solution.py:37
  111.5 9.5 %shard_map.142 = (s16[48,2048]{1,0:T(8,128)(2,1)}, s16[48,2048]{1,0:T(8,128)(2,1)}, s16[48,2048]{1,0:T(8,128)(2,1)}, s16[48,2048]{1,0:T(8,128)(2,1)}, s16[48,204...) custom-call(s32[3]{0:T(128)} %pad_add_fusion.where_ref, ...), custom_call_target="tpu_custom_call" | custom-call | tf_op jit(solution)/shard_map/pallas_call | solution.py:37
  121.0 3.2 %collective-permute-start.20 = (s16[48,2048]{1,0:T(8,128)(2,1)}, s16[48,2048]{1,0:T(8,128)(2,1)S(1)}, u32[]{:S(2)}, u32[]{:S(2)}) collective-permute-start(s16[48,2048]{1,0:T(8,128)(2,1)} %get-tuple-element.49), channel_id=1, source_target_pairs={{0,12},{2,14},{4,8},{6,10},{8,4},{10,6},{12,0},{14,2},{1,13},{3,15... | collective-permute-start | bytes 589832 | tf_op jit(solution)/shard_map/ppermute | solution.py:285
  129.4 4.8 %all-to-all-start.2 = ((f32[24,32,128]{2,1,0:T(8,128)}), f32[24,32,128]{2,1,0:T(8,128)S(1)}, u32[]{:S(2)}, u32[]{:S(2)}) async-start(f32[24,32,128]{2,1,0:T(8,128)} %shard_map.140), calls=%async_computation.2 | async-start | bytes 786432 | tf_op jit(solution)/shard_map/all_to_all | solution.py:323
  134.2 4.0 %collective-permute-start.22 = (s16[48,2048]{1,0:T(8,128)(2,1)}, s16[48,2048]{1,0:T(8,128)(2,1)S(1)}, u32[]{:S(2)}, u32[]{:S(2)}) collective-permute-start(s16[48,2048]{1,0:T(8,128)(2,1)} %get-tuple-element.51), channel_id=1, source_target_pairs={{0,14},{2,8},{4,10},{6,12},{8,6},{10,0},{12,2},{14,4},{1,15},{3,9}... | collective-permute-start | bytes 589832 | tf_op jit(solution)/shard_map/ppermute | solution.py:285
  142.2 4.2 %all-to-all-done.2.got_ref = f32[24,32,128]{2,1,0:T(8,128)S(1)} async-done(((f32[24,32,128]{2,1,0:T(8,128)}), f32[24,32,128]{2,1,0:T(8,128)S(1)}, u32[]{:S(2)}, u32[]{:S(2)}) %all-to-all-start.2) | async-done | bytes 393248 | tf_op jit(solution)/shard_map/all_to_all | solution.py:323
  157.6 4.8 %all-to-all-start.3 = ((f32[24,32,128]{2,1,0:T(8,128)}), f32[24,32,128]{2,1,0:T(8,128)S(1)}, u32[]{:S(2)}, u32[]{:S(2)}) async-start(f32[24,32,128]{2,1,0:T(8,128)} %shard_map.141.refs_9_), calls=%async_computation.3 | async-start | bytes 786432 | tf_op jit(solution)/shard_map/all_to_all | solution.py:329
  165.0 3.5 %collective-permute-start.31 = (bf16[48,2048]{1,0:T(8,128)(2,1)}, bf16[48,2048]{1,0:T(8,128)(2,1)S(1)}, u32[]{:S(2)}, u32[]{:S(2)}) collective-permute-start(bf16[48,2048]{1,0:T(8,128)(2,1)} %shard_map.143.refs_0_), channel_id=1, source_target_pairs={{0,14},{2,8},{4,10},{6,12},{8,6},{10,0},{12,2},{14,4},{1,15},{3,9}... | collective-permute-start | bytes 589832 | tf_op jit(solution)/shard_map/ppermute | solution.py:285
  168.5 3.6 %collective-permute-start.32 = (bf16[48,2048]{1,0:T(8,128)(2,1)}, bf16[48,2048]{1,0:T(8,128)(2,1)S(1)}, u32[]{:S(2)}, u32[]{:S(2)}) collective-permute-start(bf16[48,2048]{1,0:T(8,128)(2,1)} %shard_map.143.refs_0_), channel_id=1, source_target_pairs={{0,12},{2,14},{4,8},{6,10},{8,4},{10,6},{12,0},{14,2},{1,13},{3,15... | collective-permute-start | bytes 589832 | tf_op jit(solution)/shard_map/ppermute | solution.py:285
  173.5 11.7 %collective-permute-done.30.refs_4_ = bf16[48,2048]{1,0:T(8,128)(2,1)S(1)} collective-permute-done((bf16[48,2048]{1,0:T(8,128)(2,1)}, bf16[48,2048]{1,0:T(8,128)(2,1)S(1)}, u32[]{:S(2)}, u32[]{:S(2)}) %collective-permute-start.30) | collective-permute-done | bytes 196640 | tf_op jit(solution)/shard_map/ppermute | solution.py:285
  186.6 4.0 %shard_map.144 = (f32[8,48,250]{2,1,0:T(8,128)}, f32[8,48,250]{2,1,0:T(8,128)}) custom-call(s32[3]{0:T(128)} %pad_add_fusion.where_ref, bf16[48,2048]{1,0:T(8,128)(2,1)} %shard_map.143.refs_0_, bf16[48,2048]{1,0:T(8,128)(2,1)} %copy-done.9, bf16[48,2048]{1,0:T(8,128)(2,1)} %copy-done.11, bf16[48,2048]{1,0:T(8,128)(2,1)} %copy-done.13, ...), custom_call_target="tpu_custom_call" | custom-call | tf_op jit(solution)/shard_map/pallas_call | solution.py:37
  193.3 3.8 %shard_map.145 = (f32[16,48,250]{2,1,0:T(8,128)}, f32[8,48,250]{2,1,0:T(8,128)}, f32[16,48,250]{2,1,0:T(8,128)}) custom-call(s32[3]{0:T(128)} %pad_add_fusion.where_ref, s32[64]{0:T(128)} %reshape.61.ids_ref, f32[16,48,250]{2,1,0:T(8,128)} %get-tuple-element.45.field_ref.own_ref.dispatch_ref, f32[16,48,250]{2,1,0:T(8,128)} %get-tuple-element.46.prices_ref, ...), custom_call_target="tpu_custom_call" | custom-call | tf_op jit(solution)/shard_map/pallas_call | solution.py:37
  199.4 13.9 %all_to_all.30.got_ref = f32[24,32,128]{2,1,0:T(8,128)} all-to-all(f32[24,32,128]{2,1,0:T(8,128)} %shard_map.146), channel_id=1, replica_groups=mesh['ylo'=2,'z'=4,'yhi'=2,'x'=4,'core'=2] {'ylo','z'}, dimensions={0} | all-to-all | bytes 786432 | tf_op jit(solution)/shard_map/all_to_all | solution.py:323
  215.3 12.1 %all_to_all.31.means_ref = f32[24,32,128]{2,1,0:T(8,128)} all-to-all(f32[24,32,128]{2,1,0:T(8,128)} %shard_map.147), channel_id=1, replica_groups=mesh['ylo'=2,'z'=4,'yhi'=2,'x'=4,'core'=2] {'ylo','z'}, dimensions={0} | all-to-all | bytes 786432 | tf_op jit(solution)/shard_map/all_to_all | solution.py:329
  (166 shorter events, 87.0 us)
Async XLA Ops:
  0.6 18.1 %collective-permute-start.3 = (bf16[2000,625]{1,0:T(8,128)(2,1)}, bf16[2000,625]{1,0:T(8,128)(2,1)S(1)}, u32[]{:S(2)}, u32[]{:S(2)}) collective-permute-start(bf16[2000,625]{1,0:T(8,128)(2,1)} %bitcast.24), channel_id=1, source_target_pairs={{0,1},{1,0},{2,3},{3,2},{4,5},{5,4},{6,7},{7,6},{8,9},{9,8},{10,11... | collective-permute-start | bytes 7500008 | tf_op jit(solution)/shard_map/ppermute | solution.py:289
  0.7 23.2 %collective-permute-start.1 = (bf16[16,48,625]{2,1,0:T(8,128)(2,1)}, bf16[16,48,625]{2,1,0:T(8,128)(2,1)S(1)}, u32[]{:S(2)}, u32[]{:S(2)}) collective-permute-start(bf16[16,48,625]{2,1,0:T(8,128)(2,1)} %demand_own_ref.3), channel_id=1, source_target_pairs={{0,1},{1,0},{2,3},{3,2},{4,5},{5,4},{6,7},{7,6},{8,9},{9,8},{10,11... | collective-permute-start | bytes 2880008 | tf_op jit(solution)/shard_map/ppermute | solution.py:289
  1.2 22.7 %collective-permute-start = (f32[16,48,250]{2,1,0:T(8,128)}, f32[16,48,250]{2,1,0:T(8,128)}, u32[]{:S(2)}, u32[]{:S(2)}) collective-permute-start(f32[16,48,250]{2,1,0:T(8,128)} %dispatch_ref.1), channel_id=1, source_target_pairs={{0,1},{1,0},{2,3},{3,2},{4,5},{5,4},{6,7},{7,6},{8,9},{9,8},{10,11... | collective-permute-start | bytes 2304008 | tf_op jit(solution)/shard_map/ppermute | solution.py:289
  4.9 48.5 %all-to-all-start = ((f32[24,32,128]{2,1,0:T(8,128)}), f32[24,32,128]{2,1,0:T(8,128)}, u32[]{:S(2)}, u32[]{:S(2)}) async-start(f32[24,32,128]{2,1,0:T(8,128)} %shard_map.131), calls=%async_computation | async-start | bytes 786432 | tf_op jit(solution)/shard_map/all_to_all | solution.py:323
  34.4 17.7 %collective-permute-start.10 = (s16[48,2048]{1,0:T(8,128)(2,1)}, s16[48,2048]{1,0:T(8,128)(2,1)S(1)}, u32[]{:S(2)}, u32[]{:S(2)}) collective-permute-start(s16[48,2048]{1,0:T(8,128)(2,1)} %get-tuple-element.40), channel_id=1, source_target_pairs={{0,6},{2,0},{4,2},{6,4},{8,14},{10,8},{12,10},{14,12},{1,7},{3,1},... | collective-permute-start | bytes 589832 | tf_op jit(solution)/shard_map/ppermute | solution.py:285
  37.2 15.6 %collective-permute-start.4 = (s16[48,2048]{1,0:T(8,128)(2,1)}, s16[48,2048]{1,0:T(8,128)(2,1)S(1)}, u32[]{:S(2)}, u32[]{:S(2)}) collective-permute-start(s16[48,2048]{1,0:T(8,128)(2,1)} %get-tuple-element.34), channel_id=1, source_target_pairs={{0,12},{2,14},{4,8},{6,10},{8,4},{10,6},{12,0},{14,2},{1,13},{3,15... | collective-permute-start | bytes 589832 | tf_op jit(solution)/shard_map/ppermute | solution.py:285
  45.0 16.0 %collective-permute-start.5 = (s16[48,2048]{1,0:T(8,128)(2,1)}, s16[48,2048]{1,0:T(8,128)(2,1)S(1)}, u32[]{:S(2)}, u32[]{:S(2)}) collective-permute-start(s16[48,2048]{1,0:T(8,128)(2,1)} %get-tuple-element.35), channel_id=1, source_target_pairs={{0,10},{2,12},{4,14},{6,8},{8,2},{10,4},{12,6},{14,0},{1,11},{3,13... | collective-permute-start | bytes 589832 | tf_op jit(solution)/shard_map/ppermute | solution.py:285
  45.9 15.0 %collective-permute-start.6 = (s16[48,2048]{1,0:T(8,128)(2,1)}, s16[48,2048]{1,0:T(8,128)(2,1)S(1)}, u32[]{:S(2)}, u32[]{:S(2)}) collective-permute-start(s16[48,2048]{1,0:T(8,128)(2,1)} %get-tuple-element.36), channel_id=1, source_target_pairs={{0,14},{2,8},{4,10},{6,12},{8,6},{10,0},{12,2},{14,4},{1,15},{3,9}... | collective-permute-start | bytes 589832 | tf_op jit(solution)/shard_map/ppermute | solution.py:285
  67.7 15.2 %collective-permute-start.12 = (bf16[48,2048]{1,0:T(8,128)(2,1)}, bf16[48,2048]{1,0:T(8,128)(2,1)S(1)}, u32[]{:S(2)}, u32[]{:S(2)}) collective-permute-start(bf16[48,2048]{1,0:T(8,128)(2,1)} %shard_map.137.refs_0_), channel_id=1, source_target_pairs={{0,4},{2,6},{4,0},{6,2},{8,12},{10,14},{12,8},{14,10},{1,5},{3,7},... | collective-permute-start | bytes 589832 | tf_op jit(solution)/shard_map/ppermute | solution.py:285
  69.0 25.8 %all-to-all-start.1 = ((f32[24,32,128]{2,1,0:T(8,128)}), f32[24,32,128]{2,1,0:T(8,128)S(1)}, u32[]{:S(2)}, u32[]{:S(2)}) async-start(f32[24,32,128]{2,1,0:T(8,128)} %shard_map.132.refs_9_), calls=%async_computation.1 | async-start | bytes 786432 | tf_op jit(solution)/shard_map/all_to_all | solution.py:329
  74.1 20.7 %collective-permute-start.13 = (bf16[48,2048]{1,0:T(8,128)(2,1)}, bf16[48,2048]{1,0:T(8,128)(2,1)S(1)}, u32[]{:S(2)}, u32[]{:S(2)}) collective-permute-start(bf16[48,2048]{1,0:T(8,128)(2,1)} %shard_map.137.refs_0_), channel_id=1, source_target_pairs={{0,2},{2,4},{4,6},{6,0},{8,10},{10,12},{12,14},{14,8},{1,3},{3,5},... | collective-permute-start | bytes 589832 | tf_op jit(solution)/shard_map/ppermute | solution.py:285
  75.3 22.0 %collective-permute-start.14 = (bf16[48,2048]{1,0:T(8,128)(2,1)}, bf16[48,2048]{1,0:T(8,128)(2,1)S(1)}, u32[]{:S(2)}, u32[]{:S(2)}) collective-permute-start(bf16[48,2048]{1,0:T(8,128)(2,1)} %shard_map.137.refs_0_), channel_id=1, source_target_pairs={{0,8},{2,10},{4,12},{6,14},{8,0},{10,2},{12,4},{14,6},{1,9},{3,11}... | collective-permute-start | bytes 589832 | tf_op jit(solution)/shard_map/ppermute | solution.py:285
  77.7 19.7 %collective-permute-start.15 = (bf16[48,2048]{1,0:T(8,128)(2,1)}, bf16[48,2048]{1,0:T(8,128)(2,1)S(1)}, u32[]{:S(2)}, u32[]{:S(2)}) collective-permute-start(bf16[48,2048]{1,0:T(8,128)(2,1)} %shard_map.137.refs_0_), channel_id=1, source_target_pairs={{0,14},{2,8},{4,10},{6,12},{8,6},{10,0},{12,2},{14,4},{1,15},{3,9}... | collective-permute-start | bytes 589832 | tf_op jit(solution)/shard_map/ppermute | solution.py:285
  80.3 17.0 %collective-permute-start.16 = (bf16[48,2048]{1,0:T(8,128)(2,1)}, bf16[48,2048]{1,0:T(8,128)(2,1)S(1)}, u32[]{:S(2)}, u32[]{:S(2)}) collective-permute-start(bf16[48,2048]{1,0:T(8,128)(2,1)} %shard_map.137.refs_0_), channel_id=1, source_target_pairs={{0,12},{2,14},{4,8},{6,10},{8,4},{10,6},{12,0},{14,2},{1,13},{3,15... | collective-permute-start | bytes 589832 | tf_op jit(solution)/shard_map/ppermute | solution.py:285
  83.0 14.4 %collective-permute-start.17 = (bf16[48,2048]{1,0:T(8,128)(2,1)}, bf16[48,2048]{1,0:T(8,128)(2,1)S(1)}, u32[]{:S(2)}, u32[]{:S(2)}) collective-permute-start(bf16[48,2048]{1,0:T(8,128)(2,1)} %shard_map.137.refs_0_), channel_id=1, source_target_pairs={{0,10},{2,12},{4,14},{6,8},{8,2},{10,4},{12,6},{14,0},{1,11},{3,13... | collective-permute-start | bytes 589832 | tf_op jit(solution)/shard_map/ppermute | solution.py:285
  121.0 18.0 %collective-permute-start.20 = (s16[48,2048]{1,0:T(8,128)(2,1)}, s16[48,2048]{1,0:T(8,128)(2,1)S(1)}, u32[]{:S(2)}, u32[]{:S(2)}) collective-permute-start(s16[48,2048]{1,0:T(8,128)(2,1)} %get-tuple-element.49), channel_id=1, source_target_pairs={{0,12},{2,14},{4,8},{6,10},{8,4},{10,6},{12,0},{14,2},{1,13},{3,15... | collective-permute-start | bytes 589832 | tf_op jit(solution)/shard_map/ppermute | solution.py:285
  124.2 16.1 %collective-permute-start.21 = (s16[48,2048]{1,0:T(8,128)(2,1)}, s16[48,2048]{1,0:T(8,128)(2,1)S(1)}, u32[]{:S(2)}, u32[]{:S(2)}) collective-permute-start(s16[48,2048]{1,0:T(8,128)(2,1)} %get-tuple-element.50), channel_id=1, source_target_pairs={{0,10},{2,12},{4,14},{6,8},{8,2},{10,4},{12,6},{14,0},{1,11},{3,13... | collective-permute-start | bytes 589832 | tf_op jit(solution)/shard_map/ppermute | solution.py:285
  129.4 17.0 %all-to-all-start.2 = ((f32[24,32,128]{2,1,0:T(8,128)}), f32[24,32,128]{2,1,0:T(8,128)S(1)}, u32[]{:S(2)}, u32[]{:S(2)}) async-start(f32[24,32,128]{2,1,0:T(8,128)} %shard_map.140), calls=%async_computation.2 | async-start | bytes 786432 | tf_op jit(solution)/shard_map/all_to_all | solution.py:323
  134.2 15.0 %collective-permute-start.22 = (s16[48,2048]{1,0:T(8,128)(2,1)}, s16[48,2048]{1,0:T(8,128)(2,1)S(1)}, u32[]{:S(2)}, u32[]{:S(2)}) collective-permute-start(s16[48,2048]{1,0:T(8,128)(2,1)} %get-tuple-element.51), channel_id=1, source_target_pairs={{0,14},{2,8},{4,10},{6,12},{8,6},{10,0},{12,2},{14,4},{1,15},{3,9}... | collective-permute-start | bytes 589832 | tf_op jit(solution)/shard_map/ppermute | solution.py:285
  157.5 14.6 %collective-permute-start.28 = (bf16[48,2048]{1,0:T(8,128)(2,1)}, bf16[48,2048]{1,0:T(8,128)(2,1)S(1)}, u32[]{:S(2)}, u32[]{:S(2)}) collective-permute-start(bf16[48,2048]{1,0:T(8,128)(2,1)} %shard_map.143.refs_0_), channel_id=1, source_target_pairs={{0,4},{2,6},{4,0},{6,2},{8,12},{10,14},{12,8},{14,10},{1,5},{3,7},... | collective-permute-start | bytes 589832 | tf_op jit(solution)/shard_map/ppermute | solution.py:285
  157.6 15.9 %all-to-all-start.3 = ((f32[24,32,128]{2,1,0:T(8,128)}), f32[24,32,128]{2,1,0:T(8,128)S(1)}, u32[]{:S(2)}, u32[]{:S(2)}) async-start(f32[24,32,128]{2,1,0:T(8,128)} %shard_map.141.refs_9_), calls=%async_computation.3 | async-start | bytes 786432 | tf_op jit(solution)/shard_map/all_to_all | solution.py:329
  163.2 21.9 %collective-permute-start.30 = (bf16[48,2048]{1,0:T(8,128)(2,1)}, bf16[48,2048]{1,0:T(8,128)(2,1)S(1)}, u32[]{:S(2)}, u32[]{:S(2)}) collective-permute-start(bf16[48,2048]{1,0:T(8,128)(2,1)} %shard_map.143.refs_0_), channel_id=1, source_target_pairs={{0,8},{2,10},{4,12},{6,14},{8,0},{10,2},{12,4},{14,6},{1,9},{3,11}... | collective-permute-start | bytes 589832 | tf_op jit(solution)/shard_map/ppermute | solution.py:285
  165.0 20.1 %collective-permute-start.31 = (bf16[48,2048]{1,0:T(8,128)(2,1)}, bf16[48,2048]{1,0:T(8,128)(2,1)S(1)}, u32[]{:S(2)}, u32[]{:S(2)}) collective-permute-start(bf16[48,2048]{1,0:T(8,128)(2,1)} %shard_map.143.refs_0_), channel_id=1, source_target_pairs={{0,14},{2,8},{4,10},{6,12},{8,6},{10,0},{12,2},{14,4},{1,15},{3,9}... | collective-permute-start | bytes 589832 | tf_op jit(solution)/shard_map/ppermute | solution.py:285
  168.5 16.6 %collective-permute-start.32 = (bf16[48,2048]{1,0:T(8,128)(2,1)}, bf16[48,2048]{1,0:T(8,128)(2,1)S(1)}, u32[]{:S(2)}, u32[]{:S(2)}) collective-permute-start(bf16[48,2048]{1,0:T(8,128)(2,1)} %shard_map.143.refs_0_), channel_id=1, source_target_pairs={{0,12},{2,14},{4,8},{6,10},{8,4},{10,6},{12,0},{14,2},{1,13},{3,15... | collective-permute-start | bytes 589832 | tf_op jit(solution)/shard_map/ppermute | solution.py:285
  (54 other events, 339.3 us)

commit v3 on v2

v3 whole, which is shorter than its diff:
```python
import functools

import jax
import jax.numpy as jnp
from jax import lax
from jax.experimental import pallas as pl
from jax.experimental.pallas import tpu as pltpu
from jax.sharding import Mesh, PartitionSpec as P

BUSES = 10000
SECTION2_NODES = 4
SECTION3_NODES = 8
ITERS = 2

F32 = jnp.float32
BF16 = jnp.bfloat16
LINES = 2000
LANES = 2048
WIDTH = 512
BALANCE_SCALE = 8.0
UNIT_PAD = 256
SPAN = 12
NODE_FIRST = (0, 1, 5)
NODE_WIDTH = (1, SECTION2_NODES, SECTION3_NODES)
VALUE_SCALE = 16383.0
SUM_SCALE = 1023.0
VMEM = pl.BlockSpec(memory_space=pltpu.VMEM)
SMEM = pl.BlockSpec(memory_space=pltpu.SMEM)
PARAMS = pltpu.CompilerParams(vmem_limit_bytes=56 * 1024 * 1024)


def call(kernel, outs, scratch=(), after=0, large=(), out=VMEM):
    def run(*args):
        specs = [SMEM if a.dtype == jnp.int32 and a.ndim == 1 else VMEM for a in args]
        for i in large:
            specs[i] = pl.BlockSpec(memory_space=pl.ANY)
        if after:
            specs[-after:] = [pl.BlockSpec(memory_space=pl.ANY)] * after
        many = isinstance(outs, (list, tuple))
        return pl.pallas_call(
            kernel,
            out_shape=list(outs) if many else outs,
            in_specs=specs,
            out_specs=[out for _ in outs] if many else out,
            scratch_shapes=list(scratch),
            compiler_params=PARAMS,
        )(*args)

    return run


def shape(dims, dtype):
    return jax.ShapeDtypeStruct(dims, dtype)


def parts3(x):
    hi = x.astype(BF16)
    rest = x - hi.astype(F32)
    mid = rest.astype(BF16)
    low = (rest - mid.astype(F32)).astype(BF16)
    return hi, mid, low


def mm(a, b, dims):
    return lax.dot_general(a, b, (dims, ((), ())), preferred_element_type=F32)


NN = ((1,), (0,))
NT = ((1,), (1,))
TN = ((0,), (0,))


def mm3(a, b, dims):
    return sum(mm(part, b, dims) for part in parts3(a))


def excess(x, limit):
    return x - jnp.minimum(jnp.maximum(x, -limit), limit)


def pick(bus_ref, buses):
    rows = lax.broadcasted_iota(jnp.int32, (buses, bus_ref.shape[1]), 0)
    return (rows == bus_ref[...]).astype(F32).astype(BF16)


def unit_rows_kernel(bus_ref, ptdf_ref, _, out_ref):
    out_ref[:LINES, :] = mm(ptdf_ref[...], pick(bus_ref, ptdf_ref.shape[1]), NN).astype(BF16)
    spare = lax.broadcasted_iota(jnp.int32, (LANES - LINES, out_ref.shape[1]), 0) < 2
    out_ref[LINES:, :] = spare.astype(F32).astype(BF16)


def limits_kernel(ids_ref, table_ref, _, out_ref):
    ids = ids_ref[...]
    low = ids & 127
    high = ids >> 7
    lanes = lax.broadcasted_iota(jnp.int32, (128, LANES), 0)
    spread = mm3(table_ref[...], (lanes == low).astype(F32).astype(BF16), NN)
    rows = lax.broadcasted_iota(jnp.int32, spread.shape, 0)
    out_ref[...] = jnp.sum(jnp.where(rows == high, spread, 0.0), axis=0, keepdims=True)


def flows_kernel(
    where_ref,
    own_ref,
    other_ref,
    bus_own_ref,
    bus_other_ref,
    demand_own_ref,
    demand_other_ref,
    ptdf_own_ref,
    ptdf_other_ref,
    *rest,
):
    out_ref, demand, ptdf, sems = rest[-4:]
    core = where_ref[2]
    hours = other_ref.shape[1]
    buses = demand.shape[3]
    rows = 8 * hours
    copies = [
        pltpu.make_async_copy(demand_own_ref.at[pl.ds(8 * core, 8)], demand.at[0], sems.at[0]),
        pltpu.make_async_copy(demand_other_ref.at[pl.ds(8 * core, 8)], demand.at[1], sems.at[1]),
        pltpu.make_async_copy(ptdf_own_ref, ptdf.at[0], sems.at[2]),
        pltpu.make_async_copy(ptdf_other_ref, ptdf.at[1], sems.at[3]),
    ]
    for copy in copies:
        copy.start()

    def injected(i, dispatch_ref, bus_ref):
        first = 8 * core if dispatch_ref.shape[0] > 8 else 0
        dispatch = dispatch_ref[pl.ds(first, 8)].reshape(rows, dispatch_ref.shape[2])
        power = mm3(dispatch, pick(bus_ref, buses), NT)
        copies[i].wait()
        load = demand[i].astype(F32).reshape(rows, buses)
        return (power - load).astype(BF16)

    own = injected(0, own_ref, bus_own_ref)
    other = injected(1, other_ref, bus_other_ref)
    balance = jnp.sum(own.astype(F32), axis=1, keepdims=True)
    balance = balance + jnp.sum(other.astype(F32), axis=1, keepdims=True)
    copies[2].wait()
    copies[3].wait()
    lanes = lax.broadcasted_iota(jnp.int32, (own.shape[0], LANES - LINES), 1)
    spare = jnp.where(lanes == 0, balance * BALANCE_SCALE, 0.0)
    for tile in range(LANES // WIDTH):
        lines = slice(tile * WIDTH, min((tile + 1) * WIDTH, LINES))
        total = mm(own, ptdf[0, lines, :], NT) + mm(other, ptdf[1, lines, :], NT)
        most = jnp.max(jnp.abs(total), axis=1, keepdims=True)
        power = jnp.floor(14.9 - jnp.log2(jnp.maximum(most, 1e-6)))
        code = total * jnp.exp2(power)
        spare = jnp.where(lanes == 1 + tile, power, spare)
        if lines.stop == LINES:
            code = jnp.concatenate([code, spare], axis=1)
        code = jnp.round(code).astype(jnp.int32).astype(jnp.int16)
        for r in range(8):
            out_ref[r, :, tile * WIDTH : (tile + 1) * WIDTH] = code[r * hours : (r + 1) * hours]


def slopes_kernel(codes_ref, limits_ref, *rest):
    out_ref = rest[-1]
    rows = out_ref.shape[1]
    tiles = LANES // WIDTH
    lanes = lax.broadcasted_iota(jnp.int32, (rows, WIDTH), 1) + (LANES - WIDTH)
    last = LANES - WIDTH
    spare = [codes_ref[r, :, last:].astype(jnp.int32).astype(F32)[:, LINES - last :] for r in range(8)]
    for tile in range(tiles):
        cut = slice(tile * WIDTH, (tile + 1) * WIDTH)
        flows = jnp.zeros((rows, WIDTH), F32)
        for r in range(8):
            code = codes_ref[r, :, cut].astype(jnp.int32).astype(F32)
            flows = flows + code * jnp.exp2(-spare[r][:, 1 + tile : 2 + tile])
        slopes = excess(flows, limits_ref[:, cut])
        if tile == tiles - 1:
            balance = sum(part[:, :1] for part in spare) * (0.5 / BUSES / BALANCE_SCALE)
            high = balance.astype(BF16).astype(F32)
            slopes = jnp.where(lanes == LINES, high, slopes)
            slopes = jnp.where(lanes == LINES + 1, balance - high, slopes)
            slopes = jnp.where(lanes > LINES + 1, 0.0, slopes)
        slopes = slopes.astype(BF16)
        for r in range(8):
            out_ref[r, :, cut] = slopes


def ids_kernel(count, where_ref, flat_ref, map_ref, out_ref):
    scenarios = map_ref.shape[1]
    ylo, z = where_ref[0], where_ref[1]
    first = (4 * ylo + z) * count
    lanes = lax.broadcasted_iota(jnp.int32, (1, scenarios), 1)
    holder = lanes // count
    place = (2 * ((holder - z) & 3) + (((holder >> 2) - ylo) & 1)) * count + (lanes & (count - 1))
    for s in range(count):
        for section in range(3):
            out_ref[section * count + s] = flat_ref[section * scenarios + first + s]
        leaf = flat_ref[3 * scenarios + first + s]
        paired = (map_ref[3:4, :] == leaf) & (lanes != first + s)
        out_ref[3 * count + s] = jnp.max(jnp.where(paired, place, 0))
    row = 4 * count
    for section in range(3):
        for node in range(NODE_WIDTH[section]):
            inside = (map_ref[section : section + 1, :] == node).astype(jnp.int32)
            out_ref[row] = jnp.maximum(jnp.sum(inside), 1)
            row += 1
    for rest in range(row, 5 * count):
        out_ref[rest] = 0


def folded(x):
    x = jnp.concatenate([x, jnp.zeros((SPAN, UNIT_PAD - x.shape[1]), F32)], axis=1)
    return jnp.concatenate([x[:, :128], x[:, 128:]], axis=0)


def unfolded(x, units):
    return jnp.concatenate([x[:SPAN], x[SPAN:]], axis=1)[:, :units]


def fixed(x, scale):
    code = jnp.round(x * scale).astype(jnp.int32)
    return jnp.minimum(jnp.maximum(code, -32767), 32767).astype(jnp.int16)


def pack_kernel(ids_ref, field_ref, out_ref):
    count = field_ref.shape[0]
    for s in range(count):
        out_ref[s] = fixed(folded(field_ref[s, 3 * SPAN :, :]), VALUE_SCALE)
    for section in range(3):
        cut = slice(section * SPAN, (section + 1) * SPAN)
        fields = [field_ref[s, cut, :] for s in range(count)]
        for node in range(NODE_WIDTH[section]):
            total = jnp.zeros(fields[0].shape, F32)
            for s in range(count):
                inside = ids_ref[section * count + s] == node
                total = total + jnp.where(inside, fields[s], 0.0)
            out_ref[count + NODE_FIRST[section] + node] = fixed(folded(total), SUM_SCALE)


def join_kernel(own_ref, got_ref, out_ref):
    count = own_ref.shape[0] - sum(NODE_WIDTH)
    out_ref[:count] = own_ref[:count]
    out_ref[count : 2 * count] = got_ref[:count]
    for node in range(sum(NODE_WIDTH)):
        total = own_ref[count + node].astype(jnp.int32) + got_ref[count + node].astype(jnp.int32)
        if node < NODE_FIRST[2]:
            total = jnp.round(total.astype(F32) * 0.5).astype(jnp.int32)
        out_ref[2 * count + node] = total.astype(jnp.int16)


def unpack(ids_ref, got_refs, rows, means, count, units):
    for i, ref in enumerate(got_refs):
        rows[2 * i * count : 2 * (i + 1) * count] = ref[: 2 * count]
    for node in range(sum(NODE_WIDTH)):
        total = jnp.zeros((2 * SPAN, 128), F32)
        for ref in got_refs:
            total = total + ref[2 * count + node].astype(jnp.int32).astype(F32)
        scale = SUM_SCALE if node >= NODE_FIRST[2] else SUM_SCALE / 2
        size = ids_ref[4 * count + node].astype(F32)
        means[node] = unfolded(total * (1.0 / scale) / size, units)

    def average(s, dispatch):
        pieces = [means[NODE_FIRST[k] + ids_ref[k * count + s]] for k in range(3)]
        partner = rows[ids_ref[3 * count + s]].astype(jnp.int32).astype(F32)
        partner = unfolded(partner, units) * (1.0 / VALUE_SCALE)
        pieces.append((dispatch[3 * SPAN :] + partner) * 0.5)
        return jnp.concatenate(pieces, axis=0)

    return average


def gradient_kernel(
    advance,
    where_ref,
    ids_ref,
    dispatch_ref,
    prices_ref,
    pull_own_ref,
    pull_other_ref,
    quad_ref,
    linear_ref,
    cap_ref,
    ramp_ref,
    *rest,
):
    got_refs, (out_ref, send_ref, prices_out_ref, rows, means) = rest[:4], rest[4:]
    core = where_ref[2]
    count, hours, units = dispatch_ref.shape
    average_of = unpack(ids_ref, got_refs, rows, means, count, units)
    zero = jnp.zeros((1, units), F32)

    def one(s, pull):
        dispatch = dispatch_ref[s]
        average = average_of(s, dispatch)
        prices = prices_ref[s]
        if advance:
            prices = prices + (dispatch - average)
        prices_out_ref[s] = prices
        change = jnp.concatenate([dispatch[1:] - dispatch[:-1], zero], axis=0)
        ramp = excess(change, ramp_ref[...])
        ramp_term = jnp.concatenate([zero, ramp[:-1]], axis=0) - ramp
        gradient = (
            quad_ref[...] * dispatch
            + linear_ref[...]
            + prices
            + (dispatch - average)
            + pull
            + ramp_term
        )
        new = jnp.minimum(jnp.maximum(dispatch - 0.25 * gradient, 0.0), cap_ref[...])
        out_ref[s] = new
        return new

    def step(i, carry):
        one(8 * core + i, pull_own_ref[i])
        send_ref[i] = one(8 * (1 - core) + i, pull_other_ref[i])
        return carry

    lax.fori_loop(0, 8, step, 0)


def prices_kernel(ids_ref, dispatch_ref, prices_ref, *rest):
    got_refs, (out_ref, rows, means) = rest[:4], rest[4:]
    count, hours, units = dispatch_ref.shape
    average_of = unpack(ids_ref, got_refs, rows, means, count, units)

    def step(s, carry):
        dispatch = dispatch_ref[s]
        out_ref[s] = prices_ref[s] + (dispatch - average_of(s, dispatch))
        return carry

    lax.fori_loop(0, count, step, 0)


def swapped(value, axis="core"):
    return lax.ppermute(value, axis, [(0, 1), (1, 0)])


def exchanged(blocks):
    return lax.all_to_all(blocks, ("yhi", "x"), 0, 0, tiled=True)


def local(
    demand,
    ptdf,
    branch_limits,
    line_ids,
    unit_bus,
    node_map,
    cost_linear,
    cost_quad,
    capacity,
    ramp_limits,
    gen_init,
    price_init,
):
    count, hours, units = gen_init.shape
    buses = ptdf.shape[0]
    x, y, core = lax.axis_index("x"), lax.axis_index("yhi"), lax.axis_index("core")
    where = jnp.stack([x, y, core]).astype(jnp.int32)
    ylo, z = lax.axis_index("ylo"), lax.axis_index("z")
    ids = call(
        functools.partial(ids_kernel, count),
        shape((5 * count,), jnp.int32),
        out=SMEM,
    )(jnp.stack([ylo, z]).astype(jnp.int32), node_map.reshape(-1), node_map)

    payload = (count + sum(NODE_WIDTH), 2 * SPAN, 128)
    unpacking = [
        pltpu.VMEM((node_map.shape[1],) + payload[1:], jnp.int16),
        pltpu.VMEM((sum(NODE_WIDTH), SPAN, units), F32),
    ]

    def packed(field):
        return call(pack_kernel, shape(payload, jnp.int16))(ids, field)

    def joined(own, beside):
        both = (2 * count + sum(NODE_WIDTH),) + payload[1:]
        return call(join_kernel, shape(both, jnp.int16))(own, beside)

    def gathered(pair):
        return [pair] + [lax.ppermute(pair, "z", [(i, (i - d) % 4) for i in range(4)]) for d in (1, 2, 3)]

    lines = ptdf.T
    lines_other = swapped(lines)
    bus_other = swapped(unit_bus)
    demand_other = swapped(demand)
    dispatch_other = swapped(gen_init)

    bus_own, bus_other = unit_bus[None, :], bus_other[None, :]
    table = jnp.pad(branch_limits, (0, 96 * 128 - branch_limits.shape[0])).reshape(96, 128)
    block = (8, hours, LANES)
    half = (8, hours, units)
    whole = (count, hours, units)

    def pulled(slopes, rows):
        pull = jnp.dot(slopes.reshape(8 * hours, LANES), rows, preferred_element_type=F32)
        return pull.reshape(half)

    dispatch, prices = gen_init, price_init
    own = packed(dispatch)
    for step in range(ITERS):
        codes = call(
            flows_kernel,
            shape(block, jnp.int16),
            [
                pltpu.VMEM((2, 8, hours, buses), BF16),
                pltpu.VMEM((2, LINES, buses), BF16),
                pltpu.SemaphoreType.DMA((4,)),
            ],
            after=1,
            large=(5, 6, 7, 8),
        )(
            where,
            dispatch,
            dispatch_other,
            bus_own,
            bus_other,
            demand,
            demand_other,
            lines,
            lines_other,
            own,
        )
        codes, beside = lax.optimization_barrier((codes, swapped(own, "ylo")))
        got = exchanged(codes)
        pair = joined(own, beside)
        if step == 0:
            rows_of = call(unit_rows_kernel, shape((LANES, units), BF16), after=1)
            rows_own = rows_of(bus_own, lines, codes)
            rows_other = rows_of(bus_other, lines_other, codes)
            limits = call(limits_kernel, shape((1, LANES), F32), after=1)(
                jnp.pad(line_ids, (0, LANES - LINES))[None, :], table, codes
            )
        nodes = gathered(pair)
        slopes = exchanged(
            call(slopes_kernel, shape(block, BF16), after=5)(got, limits, *nodes[1:], rows_own, rows_other)
        )
        pull_other = swapped(pulled(slopes, rows_other))
        pull_own = pulled(slopes, rows_own)
        dispatch, send, prices = call(
            functools.partial(gradient_kernel, step > 0),
            [shape(whole, F32), shape(half, F32), shape(whole, F32)],
            unpacking,
        )(
            where,
            ids,
            dispatch,
            prices,
            pull_own,
            pull_other,
            cost_quad[None, :],
            cost_linear[None, :],
            capacity[None, :],
            ramp_limits[None, :],
            *nodes,
        )
        if step + 1 < ITERS:
            dispatch_other = swapped(send)
        own = packed(dispatch)
    nodes = gathered(joined(own, swapped(own, "ylo")))
    prices = call(prices_kernel, shape(whole, F32), unpacking)(ids, dispatch, prices, *nodes)
    return (dispatch, prices)


def solution(mesh):
    fine = Mesh(mesh.devices.reshape(2, 4, 2, 4, 2), ("ylo", "z", "yhi", "x", "core"))
    scen, area = ("ylo", "z"), ("yhi", "x", "core")
    return jax.shard_map(
        local,
        mesh=fine,
        in_specs=(
            P(scen, None, area),
            P(area, None),
            P(),
            P(),
            P(area),
            P(),
            P(area),
            P(area),
            P(area),
            P(area),
            P(scen, None, area),
            P(scen, None, area),
        ),
        out_specs=(P(scen, None, area), P(scen, None, area)),
        check_vma=False,
    )
```

time: 231 us -> 199 us (0.86)
  starting transfers between devices: 76.7 us -> 34.7 us
  blocking collectives: 25.9 us -> 53.7 us
  waiting for transfers between devices: 44.2 us -> 35.8 us
  Pallas kernels: 64.9 us -> 56.9 us
  matrix products: 0 us -> 3.79 us
  local copies, waits for them, and re-layouts: 13.8 us -> 10.7 us
  other arithmetic: 3.54 us -> 1.22 us
    ppermute x35 -> x19, starting transfers between devices: 55.6 us -> 24.5 us  [the longest x9 19.5 us: gathered(): lax.ppermute(pair, 'z', [(i, (i - d) % 4) for i in range(4)])]
    all_to_all x2, blocking collectives: 25.9 us -> 53.7 us  [exchanged(): return lax.all_to_all(blocks, ('yhi', 'x'), 0, 0, tiled=True)]
    all_to_all x4 -> x2, starting transfers between devices: 21.1 us -> 10.2 us  [exchanged(): return lax.all_to_all(blocks, ('yhi', 'x'), 0, 0, tiled=True)]
    pallas_call x18 -> x17, Pallas kernels: 64.9 us -> 56.9 us  [run(): pl.pallas_call(kernel, out_shape=list(outs) if many else outs, in_specs=s...]
    all_to_all x4 -> x2, waiting for transfers between devices: 14.4 us -> 6.69 us  [exchanged(): return lax.all_to_all(blocks, ('yhi', 'x'), 0, 0, tiled=True)]
    dot_general x0 -> x4, matrix products: none -> 3.79 us  [pulled(): jnp.dot(slopes.reshape(8 * hours, LANES), rows, preferred_element_type=F32)]
    ppermute x35 -> x19, waiting for transfers between devices: 29.8 us -> 29.2 us  [the longest x9 23.3 us: gathered(): lax.ppermute(pair, 'z', [(i, (i - d) % 4) for i in range(4)])]
    unnamed x78 -> x50, local copies, waits for them, and re-layouts: 9.17 us -> 9.48 us
  transfers between devices with their start and end apart: 39 -> 21, of which waited for: 12 -> 9; matrix products, arithmetic and copies ran while one was open for 4% -> 3% of each run, Pallas kernels for 12% -> 18%
where the time goes in v3:
time: 199 us; the launch traced here: 198 us
  Pallas kernels  56.9 us (29%)
  blocking collectives  53.7 us (27%)
  waiting for transfers between devices  35.8 us (18%)
  starting transfers between devices  34.7 us (17%)
  local copies, waits for them, and re-layouts  10.7 us (5%)
  matrix products  3.79 us (2%)
    pallas_call x17, Pallas kernels, run(): pl.pallas_call(kernel, out_shape=list(outs) if many else outs, in_specs=s...  56.9 us
    all_to_all x2, blocking collectives, exchanged(): return lax.all_to_all(blocks, ('yhi', 'x'), 0, 0, tiled=True)  53.7 us
    ppermute x9, waiting for transfers between devices, gathered(): lax.ppermute(pair, 'z', [(i, (i - d) % 4) for i in range(4)])  23.3 us
    ppermute x9, starting transfers between devices, gathered(): lax.ppermute(pair, 'z', [(i, (i - d) % 4) for i in range(4)])  19.5 us
    all_to_all x2, starting transfers between devices, exchanged(): return lax.all_to_all(blocks, ('yhi', 'x'), 0, 0, tiled=True)  10.2 us
    unnamed x50, local copies, waits for them, and re-layouts  9.48 us
    all_to_all x2, waiting for transfers between devices, exchanged(): return lax.all_to_all(blocks, ('yhi', 'x'), 0, 0, tiled=True)  6.69 us
    ppermute x10, waiting for transfers between devices, swapped(): return lax.ppermute(value, axis, [(0, 1), (1, 0)])  5.81 us
  transfers between devices with their start and end apart: 21, of which 9 were waited for; matrix products, arithmetic and copies ran while one was open for 3% of the time, Pallas kernels for 18%

profile of v3, /device:TPU:0, one launch (start us, length us, event | category | flops | bytes accessed | tf_op | source)
XLA Modules:
  0.0 197.8 jit_solution(6034078537143584799)
XLA Ops:
  3.4 2.2 %shard_map.132.rest_0_.own_ref = s16[29,24,128]{2,1,0:T(8,128)(2,1)} custom-call(s32[80]{0:T(128)} %shard_map.131.ids_ref, f32[16,48,250]{2,1,0:T(8,128)} %dispatch_ref.1), custom_call_target="tpu_custom_call" | custom-call | tf_op jit(solution)/shard_map/pallas_call | solution.py:40
  10.4 8.4 %shard_map.133._ = s16[8,48,2048]{2,1,0:T(8,128)(2,1)} custom-call(s32[3]{0:T(128)} %pad_add_fusion.where_ref, f32[16,48,250]{2,1,0:T(8,128)} %dispatch_ref.1, f32[16,48,250]{2,1,0:T(8,128)} %collective-permute-done.other_ref, s32[1,250]{1,0:T(1,128)} %bitcast.35, s32[1,250]{1,0:T(1,128)} %bitcast.38, bf16[16,48,625]{2,1,0:T(8,128)(2,1)} %demand_own_ref.3, ...), custom_call_target="tpu_custom_call" | custom-call | tf_op jit(solution)/shard_map/pallas_call | solution.py:40
  18.9 6.7 %all-to-all-start = ((s16[8,48,2048]{2,1,0:T(8,128)(2,1)}), s16[8,48,2048]{2,1,0:T(8,128)(2,1)S(1)}, u32[]{:S(2)}, u32[]{:S(2)}) async-start(s16[8,48,2048]{2,1,0:T(8,128)(2,1)} %shard_map.133._), calls=%async_computation | async-start | bytes 3145728 | tf_op jit(solution)/shard_map/all_to_all | solution.py:335
  29.2 3.6 %collective-permute-start.6 = (s16[45,24,128]{2,1,0:T(8,128)(2,1)}, s16[45,24,128]{2,1,0:T(8,128)(2,1)S(1)}, u32[]{:S(2)}, u32[]{:S(2)}) collective-permute-start(s16[45,24,128]{2,1,0:T(8,128)(2,1)} %shard_map.135.rest_0_), channel_id=1, source_target_pairs={{0,32},{16,48},{32,0},{48,16},{1,33},{17,49},{33,1},{49,17},{2,34}... | collective-permute-start | bytes 829448 | tf_op jit(solution)/shard_map/ppermute | solution.py:377
  35.0 3.7 %shard_map.136.rest_3_ = bf16[2048,250]{1,0:T(8,128)(2,1)} custom-call(s32[1,250]{1,0:T(1,128)} %bitcast.36, bf16[2000,625]{1,0:T(8,128)(2,1)} %bitcast.32, s16[8,48,2048]{2,1,0:T(8,128)(2,1)} %shard_map.133._), custom_call_target="tpu_custom_call" | custom-call | tf_op jit(solution)/shard_map/pallas_call | solution.py:40
  40.7 3.7 %shard_map.137.rest_4_ = bf16[2048,250]{1,0:T(8,128)(2,1)} custom-call(s32[1,250]{1,0:T(1,128)} %bitcast.39, bf16[2000,625]{1,0:T(8,128)(2,1)} %copy-done.4, s16[8,48,2048]{2,1,0:T(8,128)(2,1)} %shard_map.133._), custom_call_target="tpu_custom_call" | custom-call | tf_op jit(solution)/shard_map/pallas_call | solution.py:40
  45.3 3.4 %all-to-all-done.codes_ref = s16[8,48,2048]{2,1,0:T(8,128)(2,1)S(1)} async-done(((s16[8,48,2048]{2,1,0:T(8,128)(2,1)}), s16[8,48,2048]{2,1,0:T(8,128)(2,1)S(1)}, u32[]{:S(2)}, u32[]{:S(2)}) %all-to-all-start) | async-done | bytes 1572896 | tf_op jit(solution)/shard_map/all_to_all | solution.py:335
  49.9 3.1 %shard_map.138 = bf16[8,48,2048]{2,1,0:T(8,128)(2,1)} custom-call(s16[8,48,2048]{2,1,0:T(8,128)(2,1)} %copy-done.5, f32[1,2048]{1,0:T(1,128)} %shard_map.134.limits_ref, s16[45,24,128]{2,1,0:T(8,128)(2,1)} %copy-done.12, s16[45,24,128]{2,1,0:T(8,128)(2,1)} %copy-done.10, s16[45,24,128]{2,1,0:T(8,128)(2,1)} %copy-done.8, ...), custom_call_target="tpu_custom_call" | custom-call | tf_op jit(solution)/shard_map/pallas_call | solution.py:40
  53.0 26.6 %all_to_all.20 = bf16[8,48,2048]{2,1,0:T(8,128)(2,1)S(1)} all-to-all(bf16[8,48,2048]{2,1,0:T(8,128)(2,1)} %shard_map.138), channel_id=1, replica_groups=mesh['ylo'=2,'z'=4,'yhi'=2,'x'=4,'core'=2] {'yhi','x'}, dimensions={0} | all-to-all | bytes 3145728 | tf_op jit(solution)/shard_map/all_to_all | solution.py:335
  82.9 4.1 %shard_map.139 = (f32[16,48,250]{2,1,0:T(8,128)}, f32[8,48,250]{2,1,0:T(8,128)}, f32[16,48,250]{2,1,0:T(8,128)}) custom-call(s32[3]{0:T(128)} %pad_add_fusion.where_ref, s32[80]{0:T(128)} %shard_map.131.ids_ref, f32[16,48,250]{2,1,0:T(8,128)} %dispatch_ref.1, f32[16,48,250]{2,1,0:T(8,128)} %prices_ref.1, f32[8,48,250]{2,1,0:T(8,128)} %fusion.6.pull_own_ref, ...), custom_call_target="tpu_custom_call" | custom-call | tf_op jit(solution)/shard_map/pallas_call | solution.py:40
  90.8 8.3 %shard_map.141 = s16[8,48,2048]{2,1,0:T(8,128)(2,1)} custom-call(s32[3]{0:T(128)} %pad_add_fusion.where_ref, f32[16,48,250]{2,1,0:T(8,128)} %get-tuple-element.13.field_ref.own_ref.dispatch_ref, f32[8,48,250]{2,1,0:T(8,128)} %copy-done.14, s32[1,250]{1,0:T(1,128)} %bitcast.37, s32[1,250]{1,0:T(1,128)} %bitcast.40, bf16[16,48,625]{2,1,0:T(8,128)(2,1)} %demand_own_ref.3, ...), custom_call_target="tpu_custom_call" | custom-call | tf_op jit(solution)/shard_map/pallas_call | solution.py:40
  99.7 3.6 %all-to-all-start.2 = ((s16[8,48,2048]{2,1,0:T(8,128)(2,1)}), s16[8,48,2048]{2,1,0:T(8,128)(2,1)S(1)}, u32[]{:S(2)}, u32[]{:S(2)}) async-start(s16[8,48,2048]{2,1,0:T(8,128)(2,1)} %shard_map.141), calls=%async_computation.2 | async-start | bytes 3145728 | tf_op jit(solution)/shard_map/all_to_all | solution.py:335
  107.0 3.6 %collective-permute-start.12 = (s16[45,24,128]{2,1,0:T(8,128)(2,1)}, s16[45,24,128]{2,1,0:T(8,128)(2,1)S(1)}, u32[]{:S(2)}, u32[]{:S(2)}) collective-permute-start(s16[45,24,128]{2,1,0:T(8,128)(2,1)} %shard_map.142.rest_0_), channel_id=1, source_target_pairs={{0,32},{16,48},{32,0},{48,16},{1,33},{17,49},{33,1},{49,17},{2,34}... | collective-permute-start | bytes 829448 | tf_op jit(solution)/shard_map/ppermute | solution.py:377
  111.6 4.6 %collective-permute-done.13.rest_2_.rest_3_ = s16[45,24,128]{2,1,0:T(8,128)(2,1)S(1)} collective-permute-done((s16[45,24,128]{2,1,0:T(8,128)(2,1)}, s16[45,24,128]{2,1,0:T(8,128)(2,1)S(1)}, u32[]{:S(2)}, u32[]{:S(2)}) %collective-permute-start.13) | collective-permute-done | bytes 276512 | tf_op jit(solution)/shard_map/ppermute | solution.py:377
  116.2 7.1 %collective-permute-done.12.rest_1_.rest_2_ = s16[45,24,128]{2,1,0:T(8,128)(2,1)S(1)} collective-permute-done((s16[45,24,128]{2,1,0:T(8,128)(2,1)}, s16[45,24,128]{2,1,0:T(8,128)(2,1)S(1)}, u32[]{:S(2)}, u32[]{:S(2)}) %collective-permute-start.12) | collective-permute-done | bytes 276512 | tf_op jit(solution)/shard_map/ppermute | solution.py:377
  123.3 3.3 %all-to-all-done.2.codes_ref = s16[8,48,2048]{2,1,0:T(8,128)(2,1)S(1)} async-done(((s16[8,48,2048]{2,1,0:T(8,128)(2,1)}), s16[8,48,2048]{2,1,0:T(8,128)(2,1)S(1)}, u32[]{:S(2)}, u32[]{:S(2)}) %all-to-all-start.2) | async-done | bytes 1572896 | tf_op jit(solution)/shard_map/all_to_all | solution.py:335
  127.8 3.1 %shard_map.143 = bf16[8,48,2048]{2,1,0:T(8,128)(2,1)} custom-call(s16[8,48,2048]{2,1,0:T(8,128)(2,1)} %copy-done.6, f32[1,2048]{1,0:T(1,128)} %shard_map.134.limits_ref, s16[45,24,128]{2,1,0:T(8,128)(2,1)} %copy-done.13, s16[45,24,128]{2,1,0:T(8,128)(2,1)} %copy-done.11, s16[45,24,128]{2,1,0:T(8,128)(2,1)} %copy-done.9, ...), custom_call_target="tpu_custom_call" | custom-call | tf_op jit(solution)/shard_map/pallas_call | solution.py:40
  130.9 27.1 %all_to_all.21 = bf16[8,48,2048]{2,1,0:T(8,128)(2,1)S(1)} all-to-all(bf16[8,48,2048]{2,1,0:T(8,128)(2,1)} %shard_map.143), channel_id=1, replica_groups=mesh['ylo'=2,'z'=4,'yhi'=2,'x'=4,'core'=2] {'yhi','x'}, dimensions={0} | all-to-all | bytes 3145728 | tf_op jit(solution)/shard_map/all_to_all | solution.py:335
  161.4 4.1 %shard_map.144 = (f32[16,48,250]{2,1,0:T(8,128)}, f32[8,48,250]{2,1,0:T(8,128)}, f32[16,48,250]{2,1,0:T(8,128)}) custom-call(s32[3]{0:T(128)} %pad_add_fusion.where_ref, s32[80]{0:T(128)} %shard_map.131.ids_ref, f32[16,48,250]{2,1,0:T(8,128)} %get-tuple-element.13.field_ref.own_ref.dispatch_ref, f32[16,48,250]{2,1,0:T(8,128)} %get-tuple-element.14.prices_ref, ...), custom_call_target="tpu_custom_call" | custom-call | tf_op jit(solution)/shard_map/pallas_call | solution.py:40
  169.1 5.2 %collective-permute-done.15.got_ref = s16[29,24,128]{2,1,0:T(8,128)(2,1)S(1)} collective-permute-done((s16[29,24,128]{2,1,0:T(8,128)(2,1)}, s16[29,24,128]{2,1,0:T(8,128)(2,1)S(1)}, u32[]{:S(2)}, u32[]{:S(2)}) %collective-permute-start.15) | collective-permute-done | bytes 178208 | tf_op jit(solution)/shard_map/ppermute | solution.py:331
  178.6 3.6 %collective-permute-start.17 = (s16[45,24,128]{2,1,0:T(8,128)(2,1)}, s16[45,24,128]{2,1,0:T(8,128)(2,1)S(1)}, u32[]{:S(2)}, u32[]{:S(2)}) collective-permute-start(s16[45,24,128]{2,1,0:T(8,128)(2,1)} %shard_map.146.rest_0_), channel_id=1, source_target_pairs={{0,32},{16,48},{32,0},{48,16},{1,33},{17,49},{33,1},{49,17},{2,34}... | collective-permute-start | bytes 829448 | tf_op jit(solution)/shard_map/ppermute | solution.py:377
  183.2 4.3 %collective-permute-done.18.rest_3_ = s16[45,24,128]{2,1,0:T(8,128)(2,1)S(1)} collective-permute-done((s16[45,24,128]{2,1,0:T(8,128)(2,1)}, s16[45,24,128]{2,1,0:T(8,128)(2,1)S(1)}, u32[]{:S(2)}, u32[]{:S(2)}) %collective-permute-start.18) | collective-permute-done | bytes 276512 | tf_op jit(solution)/shard_map/ppermute | solution.py:377
  187.6 6.4 %collective-permute-done.17.rest_2_ = s16[45,24,128]{2,1,0:T(8,128)(2,1)S(1)} collective-permute-done((s16[45,24,128]{2,1,0:T(8,128)(2,1)}, s16[45,24,128]{2,1,0:T(8,128)(2,1)S(1)}, u32[]{:S(2)}, u32[]{:S(2)}) %collective-permute-start.17) | collective-permute-done | bytes 276512 | tf_op jit(solution)/shard_map/ppermute | solution.py:377
  194.7 3.0 %shard_map.147 = f32[16,48,250]{2,1,0:T(8,128)} custom-call(s32[80]{0:T(128)} %shard_map.131.ids_ref, f32[16,48,250]{2,1,0:T(8,128)} %get-tuple-element.9.field_ref.dispatch_ref, f32[16,48,250]{2,1,0:T(8,128)} %get-tuple-element.19.prices_ref, s16[45,24,128]{2,1,0:T(8,128)(2,1)} %shard_map.146.rest_0_, s16[45,24,128]{2,1,0:T(8,128)(2,1)} %copy-done.19, ...), custom_call_target="tpu_custom_call" | custom-call | tf_op jit(solution)/shard_map/pallas_call | solution.py:40
  (95 shorter events, 44.1 us)
Async XLA Ops:
  0.6 8.0 %collective-permute-start.3 = (bf16[2000,625]{1,0:T(8,128)(2,1)}, bf16[2000,625]{1,0:T(8,128)(2,1)S(1)}, u32[]{:S(2)}, u32[]{:S(2)}) collective-permute-start(bf16[2000,625]{1,0:T(8,128)(2,1)} %bitcast.30), channel_id=1, source_target_pairs={{0,1},{1,0},{2,3},{3,2},{4,5},{5,4},{6,7},{7,6},{8,9},{9,8},{10,11... | collective-permute-start | bytes 7500008 | tf_op jit(solution)/shard_map/ppermute | solution.py:331
  0.7 7.9 %collective-permute-start.2 = (bf16[16,48,625]{2,1,0:T(8,128)(2,1)}, bf16[16,48,625]{2,1,0:T(8,128)(2,1)S(1)}, u32[]{:S(2)}, u32[]{:S(2)}) collective-permute-start(bf16[16,48,625]{2,1,0:T(8,128)(2,1)} %demand_own_ref.3), channel_id=1, source_target_pairs={{0,1},{1,0},{2,3},{3,2},{4,5},{5,4},{6,7},{7,6},{8,9},{9,8},{10,11... | collective-permute-start | bytes 2880008 | tf_op jit(solution)/shard_map/ppermute | solution.py:331
  1.2 7.4 %collective-permute-start = (f32[16,48,250]{2,1,0:T(8,128)}, f32[16,48,250]{2,1,0:T(8,128)}, u32[]{:S(2)}, u32[]{:S(2)}) collective-permute-start(f32[16,48,250]{2,1,0:T(8,128)} %dispatch_ref.1), channel_id=1, source_target_pairs={{0,1},{1,0},{2,3},{3,2},{4,5},{5,4},{6,7},{7,6},{8,9},{9,8},{10,11... | collective-permute-start | bytes 2304008 | tf_op jit(solution)/shard_map/ppermute | solution.py:331
  5.6 13.2 %collective-permute-start.4 = (s16[29,24,128]{2,1,0:T(8,128)(2,1)}, s16[29,24,128]{2,1,0:T(8,128)(2,1)}, u32[]{:S(2)}, u32[]{:S(2)}) collective-permute-start(s16[29,24,128]{2,1,0:T(8,128)(2,1)} %shard_map.132.rest_0_.own_ref), channel_id=1, source_target_pairs={{0,64},{64,0},{1,65},{65,1},{2,66},{66,2},{3,67},{67,3},{4,68},{68... | collective-permute-start | bytes 534536 | tf_op jit(solution)/shard_map/ppermute | solution.py:331
  7.3 1.4 collective-permute-start.1
  18.8 15.5 %copy-start.22 = (f32[12000]{0:T(1024)S(1)}, f32[12000]{0:T(1024)}, u32[]{:S(2)}) copy-start(f32[12000]{0:T(1024)} %param.14) | copy-start | bytes 144004
  18.9 29.8 %all-to-all-start = ((s16[8,48,2048]{2,1,0:T(8,128)(2,1)}), s16[8,48,2048]{2,1,0:T(8,128)(2,1)S(1)}, u32[]{:S(2)}, u32[]{:S(2)}) async-start(s16[8,48,2048]{2,1,0:T(8,128)(2,1)} %shard_map.133._), calls=%async_computation | async-start | bytes 3145728 | tf_op jit(solution)/shard_map/all_to_all | solution.py:335
  27.3 17.1 %collective-permute-start.7 = (s16[45,24,128]{2,1,0:T(8,128)(2,1)}, s16[45,24,128]{2,1,0:T(8,128)(2,1)S(1)}, u32[]{:S(2)}, u32[]{:S(2)}) collective-permute-start(s16[45,24,128]{2,1,0:T(8,128)(2,1)} %shard_map.135.rest_0_), channel_id=1, source_target_pairs={{0,16},{16,32},{32,48},{48,0},{1,17},{17,33},{33,49},{49,1},{2,18}... | collective-permute-start | bytes 829448 | tf_op jit(solution)/shard_map/ppermute | solution.py:377
  29.2 16.1 %collective-permute-start.6 = (s16[45,24,128]{2,1,0:T(8,128)(2,1)}, s16[45,24,128]{2,1,0:T(8,128)(2,1)S(1)}, u32[]{:S(2)}, u32[]{:S(2)}) collective-permute-start(s16[45,24,128]{2,1,0:T(8,128)(2,1)} %shard_map.135.rest_0_), channel_id=1, source_target_pairs={{0,32},{16,48},{32,0},{48,16},{1,33},{17,49},{33,1},{49,17},{2,34}... | collective-permute-start | bytes 829448 | tf_op jit(solution)/shard_map/ppermute | solution.py:377
  32.8 12.5 %collective-permute-start.5 = (s16[45,24,128]{2,1,0:T(8,128)(2,1)}, s16[45,24,128]{2,1,0:T(8,128)(2,1)S(1)}, u32[]{:S(2)}, u32[]{:S(2)}) collective-permute-start(s16[45,24,128]{2,1,0:T(8,128)(2,1)} %shard_map.135.rest_0_), channel_id=1, source_target_pairs={{0,48},{16,0},{32,16},{48,32},{1,49},{17,1},{33,17},{49,33},{2,50}... | collective-permute-start | bytes 829448 | tf_op jit(solution)/shard_map/ppermute | solution.py:377
  53.0 26.6 %copy-start.2 = (bf16[2048,250]{1,0:T(8,128)(2,1)S(1)}, bf16[2048,250]{1,0:T(8,128)(2,1)}, u32[]{:S(2)}) copy-start(bf16[2048,250]{1,0:T(8,128)(2,1)} %shard_map.137.rest_4_) | copy-start | bytes 3072004
  80.2 2.0 %collective-permute-start.8 = (f32[8,48,250]{2,1,0:T(8,128)S(1)}, f32[8,48,250]{2,1,0:T(8,128)S(1)}, u32[]{:S(2)}, u32[]{:S(2)}) collective-permute-start(f32[8,48,250]{2,1,0:T(8,128)S(1)} %fusion.2), channel_id=1, source_target_pairs={{0,1},{1,0},{2,3},{3,2},{4,5},{5,4},{6,7},{7,6},{8,9},{9,8},{10,11... | collective-permute-start | bytes 1152008 | tf_op jit(solution)/shard_map/ppermute | solution.py:331
  87.0 3.0 %collective-permute-start.9 = (f32[8,48,250]{2,1,0:T(8,128)}, f32[8,48,250]{2,1,0:T(8,128)S(1)}, u32[]{:S(2)}, u32[]{:S(2)}) collective-permute-start(f32[8,48,250]{2,1,0:T(8,128)} %get-tuple-element.15), channel_id=1, source_target_pairs={{0,1},{1,0},{2,3},{3,2},{4,5},{5,4},{6,7},{7,6},{8,9},{9,8},{10,11... | collective-permute-start | bytes 1152008 | tf_op jit(solution)/shard_map/ppermute | solution.py:331
  89.4 9.7 %collective-permute-start.10 = (s16[29,24,128]{2,1,0:T(8,128)(2,1)}, s16[29,24,128]{2,1,0:T(8,128)(2,1)S(1)}, u32[]{:S(2)}, u32[]{:S(2)}) collective-permute-start(s16[29,24,128]{2,1,0:T(8,128)(2,1)} %shard_map.140.rest_0_.own_ref), channel_id=1, source_target_pairs={{0,64},{64,0},{1,65},{65,1},{2,66},{66,2},{3,67},{67,3},{4,68},{68... | collective-permute-start | bytes 534536 | tf_op jit(solution)/shard_map/ppermute | solution.py:331
  99.7 26.9 %all-to-all-start.2 = ((s16[8,48,2048]{2,1,0:T(8,128)(2,1)}), s16[8,48,2048]{2,1,0:T(8,128)(2,1)S(1)}, u32[]{:S(2)}, u32[]{:S(2)}) async-start(s16[8,48,2048]{2,1,0:T(8,128)(2,1)} %shard_map.141), calls=%async_computation.2 | async-start | bytes 3145728 | tf_op jit(solution)/shard_map/all_to_all | solution.py:335
  105.1 11.1 %collective-permute-start.13 = (s16[45,24,128]{2,1,0:T(8,128)(2,1)}, s16[45,24,128]{2,1,0:T(8,128)(2,1)S(1)}, u32[]{:S(2)}, u32[]{:S(2)}) collective-permute-start(s16[45,24,128]{2,1,0:T(8,128)(2,1)} %shard_map.142.rest_0_), channel_id=1, source_target_pairs={{0,16},{16,32},{32,48},{48,0},{1,17},{17,33},{33,49},{49,1},{2,18}... | collective-permute-start | bytes 829448 | tf_op jit(solution)/shard_map/ppermute | solution.py:377
  107.0 16.3 %collective-permute-start.12 = (s16[45,24,128]{2,1,0:T(8,128)(2,1)}, s16[45,24,128]{2,1,0:T(8,128)(2,1)S(1)}, u32[]{:S(2)}, u32[]{:S(2)}) collective-permute-start(s16[45,24,128]{2,1,0:T(8,128)(2,1)} %shard_map.142.rest_0_), channel_id=1, source_target_pairs={{0,32},{16,48},{32,0},{48,16},{1,33},{17,49},{33,1},{49,17},{2,34}... | collective-permute-start | bytes 829448 | tf_op jit(solution)/shard_map/ppermute | solution.py:377
  110.6 12.7 %collective-permute-start.11 = (s16[45,24,128]{2,1,0:T(8,128)(2,1)}, s16[45,24,128]{2,1,0:T(8,128)(2,1)S(1)}, u32[]{:S(2)}, u32[]{:S(2)}) collective-permute-start(s16[45,24,128]{2,1,0:T(8,128)(2,1)} %shard_map.142.rest_0_), channel_id=1, source_target_pairs={{0,48},{16,0},{32,16},{48,32},{1,49},{17,1},{33,17},{49,33},{2,50}... | collective-permute-start | bytes 829448 | tf_op jit(solution)/shard_map/ppermute | solution.py:377
  130.9 27.1 %copy-start.3 = (bf16[2048,250]{1,0:T(8,128)(2,1)S(1)}, bf16[2048,250]{1,0:T(8,128)(2,1)}, u32[]{:S(2)}) copy-start(bf16[2048,250]{1,0:T(8,128)(2,1)} %shard_map.137.rest_4_) | copy-start | bytes 3072004
  158.6 2.0 collective-permute-start.14
  167.7 6.6 %collective-permute-start.15 = (s16[29,24,128]{2,1,0:T(8,128)(2,1)}, s16[29,24,128]{2,1,0:T(8,128)(2,1)S(1)}, u32[]{:S(2)}, u32[]{:S(2)}) collective-permute-start(s16[29,24,128]{2,1,0:T(8,128)(2,1)} %shard_map.145.own_ref), channel_id=1, source_target_pairs={{0,64},{64,0},{1,65},{65,1},{2,66},{66,2},{3,67},{67,3},{4,68},{68... | collective-permute-start | bytes 534536 | tf_op jit(solution)/shard_map/ppermute | solution.py:331
  176.7 10.8 %collective-permute-start.18 = (s16[45,24,128]{2,1,0:T(8,128)(2,1)}, s16[45,24,128]{2,1,0:T(8,128)(2,1)S(1)}, u32[]{:S(2)}, u32[]{:S(2)}) collective-permute-start(s16[45,24,128]{2,1,0:T(8,128)(2,1)} %shard_map.146.rest_0_), channel_id=1, source_target_pairs={{0,16},{16,32},{32,48},{48,0},{1,17},{17,33},{33,49},{49,1},{2,18}... | collective-permute-start | bytes 829448 | tf_op jit(solution)/shard_map/ppermute | solution.py:377
  178.6 15.3 %collective-permute-start.17 = (s16[45,24,128]{2,1,0:T(8,128)(2,1)}, s16[45,24,128]{2,1,0:T(8,128)(2,1)S(1)}, u32[]{:S(2)}, u32[]{:S(2)}) collective-permute-start(s16[45,24,128]{2,1,0:T(8,128)(2,1)} %shard_map.146.rest_0_), channel_id=1, source_target_pairs={{0,32},{16,48},{32,0},{48,16},{1,33},{17,49},{33,1},{49,17},{2,34}... | collective-permute-start | bytes 829448 | tf_op jit(solution)/shard_map/ppermute | solution.py:377
  182.2 11.7 %collective-permute-start.16 = (s16[45,24,128]{2,1,0:T(8,128)(2,1)}, s16[45,24,128]{2,1,0:T(8,128)(2,1)S(1)}, u32[]{:S(2)}, u32[]{:S(2)}) collective-permute-start(s16[45,24,128]{2,1,0:T(8,128)(2,1)} %shard_map.146.rest_0_), channel_id=1, source_target_pairs={{0,48},{16,0},{32,16},{48,32},{1,49},{17,1},{33,17},{49,33},{2,50}... | collective-permute-start | bytes 829448 | tf_op jit(solution)/shard_map/ppermute | solution.py:377
  (22 other events, 62.8 us)

commit v4 on v3

--- a/solution.py
+++ b/solution.py
@@ -217,7 +217,7 @@
     return jnp.minimum(jnp.maximum(code, -32767), 32767).astype(jnp.int16)
 
 
-def pack_kernel(ids_ref, field_ref, out_ref):
+def pack(ids_ref, field_ref, out_ref):
     count = field_ref.shape[0]
     for s in range(count):
         out_ref[s] = fixed(folded(field_ref[s, 3 * SPAN :, :]), VALUE_SCALE)
@@ -244,13 +244,15 @@
 
 
 def unpack(ids_ref, got_refs, rows, means, count, units):
+    held = rows.shape[0] // len(got_refs)
     for i, ref in enumerate(got_refs):
-        rows[2 * i * count : 2 * (i + 1) * count] = ref[: 2 * count]
+        rows[i * held : (i + 1) * held] = ref[:held]
     for node in range(sum(NODE_WIDTH)):
         total = jnp.zeros((2 * SPAN, 128), F32)
         for ref in got_refs:
-            total = total + ref[2 * count + node].astype(jnp.int32).astype(F32)
-        scale = SUM_SCALE if node >= NODE_FIRST[2] else SUM_SCALE / 2
+            total = total + ref[held + node].astype(jnp.int32).astype(F32)
+        halved = held > count and node < NODE_FIRST[2]
+        scale = SUM_SCALE / 2 if halved else SUM_SCALE
         size = ids_ref[4 * count + node].astype(F32)
         means[node] = unfolded(total * (1.0 / scale) / size, units)
 
@@ -266,25 +268,20 @@
 
 def gradient_kernel(
     advance,
-    where_ref,
     ids_ref,
     dispatch_ref,
     prices_ref,
-    pull_own_ref,
-    pull_other_ref,
     quad_ref,
     linear_ref,
-    cap_ref,
     ramp_ref,
     *rest,
 ):
-    got_refs, (out_ref, send_ref, prices_out_ref, rows, means) = rest[:4], rest[4:]
-    core = where_ref[2]
+    got_refs, (out_ref, prices_out_ref, rows, means) = rest[:4], rest[4:]
     count, hours, units = dispatch_ref.shape
     average_of = unpack(ids_ref, got_refs, rows, means, count, units)
     zero = jnp.zeros((1, units), F32)
 
-    def one(s, pull):
+    def step(s, carry):
         dispatch = dispatch_ref[s]
         average = average_of(s, dispatch)
         prices = prices_ref[s]
@@ -295,14 +292,21 @@
         ramp = excess(change, ramp_ref[...])
         ramp_term = jnp.concatenate([zero, ramp[:-1]], axis=0) - ramp
         gradient = (
-            quad_ref[...] * dispatch
-            + linear_ref[...]
-            + prices
-            + (dispatch - average)
-            + pull
-            + ramp_term
+            quad_ref[...] * dispatch + linear_ref[...] + prices + (dispatch - average) + ramp_term
         )
-        new = jnp.minimum(jnp.maximum(dispatch - 0.25 * gradient, 0.0), cap_ref[...])
+        out_ref[s] = dispatch - 0.25 * gradient
+        return carry
+
+    lax.fori_loop(0, count, step, 0)
+
+
+def clip_kernel(
+    where_ref, ids_ref, stepped_ref, pull_own_ref, pull_other_ref, cap_ref, out_ref, send_ref, pack_ref
+):
+    core = where_ref[2]
+
+    def one(s, pull):
+        new = jnp.minimum(jnp.maximum(stepped_ref[s] - 0.25 * pull, 0.0), cap_ref[...])
         out_ref[s] = new
         return new
 
@@ -312,10 +316,11 @@
         return carry
 
     lax.fori_loop(0, 8, step, 0)
+    pack(ids_ref, out_ref, pack_ref)
 
 
 def prices_kernel(ids_ref, dispatch_ref, prices_ref, *rest):
-    got_refs, (out_ref, rows, means) = rest[:4], rest[4:]
+    got_refs, (out_ref, rows, means) = rest[:-3], rest[-3:]
     count, hours, units = dispatch_ref.shape
     average_of = unpack(ids_ref, got_refs, rows, means, count, units)
 
@@ -367,14 +372,14 @@
     ]
 
     def packed(field):
-        return call(pack_kernel, shape(payload, jnp.int16))(ids, field)
+        return call(pack, shape(payload, jnp.int16))(ids, field)
 
     def joined(own, beside):
         both = (2 * count + sum(NODE_WIDTH),) + payload[1:]
         return call(join_kernel, shape(both, jnp.int16))(own, beside)
 
-    def gathered(pair):
-        return [pair] + [lax.ppermute(pair, "z", [(i, (i - d) % 4) for i in range(4)]) for d in (1, 2, 3)]
+    def round_z(value):
+        return [lax.ppermute(value, "z", [(i, (i - d) % 4) for i in range(4)]) for d in (1, 2, 3)]
 
     lines = ptdf.T
     lines_other = swapped(lines)
@@ -427,33 +432,31 @@
             limits = call(limits_kernel, shape((1, LANES), F32), after=1)(
                 jnp.pad(line_ids, (0, LANES - LINES))[None, :], table, codes
             )
-        nodes = gathered(pair)
+        nodes = [pair] + round_z(pair)
+        stepped, prices = call(
+            functools.partial(gradient_kernel, step > 0), [shape(whole, F32)] * 2, unpacking
+        )(
+            ids,
+            dispatch,
+            prices,
+            cost_quad[None, :],
+            cost_linear[None, :],
+            ramp_limits[None, :],
+            *nodes,
+        )
         slopes = exchanged(
-            call(slopes_kernel, shape(block, BF16), after=5)(got, limits, *nodes[1:], rows_own, rows_other)
+            call(slopes_kernel, shape(block, BF16), after=3)(got, limits, stepped, rows_own, rows_other)
         )
         pull_other = swapped(pulled(slopes, rows_other))
         pull_own = pulled(slopes, rows_own)
-        dispatch, send, prices = call(
-            functools.partial(gradient_kernel, step > 0),
-            [shape(whole, F32), shape(half, F32), shape(whole, F32)],
-            unpacking,
-        )(
-            where,
-            ids,
-            dispatch,
-            prices,
-            pull_own,
-            pull_other,
-            cost_quad[None, :],
-            cost_linear[None, :],
-            capacity[None, :],
-            ramp_limits[None, :],
-            *nodes,
-        )
+        dispatch, send, own = call(
+            clip_kernel, [shape(whole, F32), shape(half, F32), shape(payload, jnp.int16)]
+        )(where, ids, stepped, pull_own, pull_other, capacity[None, :])
         if step + 1 < ITERS:
             dispatch_other = swapped(send)
-        own = packed(dispatch)
-    nodes = gathered(joined(own, swapped(own, "ylo")))
+    beside = swapped(own, "ylo")
+    near, far = [own] + round_z(own), [beside] + round_z(beside)
+    nodes = [payloads[d] for d in range(4) for payloads in (near, far)]
     prices = call(prices_kernel, shape(whole, F32), unpacking)(ids, dispatch, prices, *nodes)
     return (dispatch, prices)
 

time: 199 us -> 193 us (0.970)
  waiting for transfers between devices: 35.8 us -> 26.4 us
  blocking collectives: 53.7 us -> 57.7 us
    all_to_all x2, waiting for transfers between devices: 6.69 us -> 0.01 us  [exchanged(): return lax.all_to_all(blocks, ('yhi', 'x'), 0, 0, tiled=True)]
    all_to_all x2, blocking collectives: 53.7 us -> 57.7 us  [exchanged(): return lax.all_to_all(blocks, ('yhi', 'x'), 0, 0, tiled=True)]
    ppermute x10, waiting for transfers between devices: 5.81 us -> 3.17 us  [swapped(): return lax.ppermute(value, axis, [(0, 1), (1, 0)])]
    ppermute x9 -> x12, starting transfers between devices: 19.5 us -> 20.5 us  [round_z(): lax.ppermute(value, 'z', [(i, (i - d) % 4) for i in range(4)])]
    pallas_call x17 -> x16, Pallas kernels: 56.9 us -> 55.9 us  [run(): pl.pallas_call(kernel, out_shape=list(outs) if many else outs, in_specs=s...]
    unnamed x50 -> x56, local copies, waits for them, and re-layouts: 9.48 us -> 10.3 us
    ppermute x9 -> x12, waiting for transfers between devices: 23.3 us -> 23.2 us  [round_z(): lax.ppermute(value, 'z', [(i, (i - d) % 4) for i in range(4)])]
  transfers between devices with their start and end apart: 21 -> 24, of which waited for: 9 -> 9; matrix products, arithmetic and copies ran while one was open for 3% -> 3% of each run, Pallas kernels for 18% -> 21%
where the time goes in v4:
time: 193 us
  blocking collectives  57.7 us (30%)
  Pallas kernels  55.9 us (29%)
  starting transfers between devices  35.1 us (18%)
  waiting for transfers between devices  26.4 us (14%)
  local copies, waits for them, and re-layouts  11.6 us (6%)
  matrix products  3.82 us (2%)
    all_to_all x2, blocking collectives, exchanged(): return lax.all_to_all(blocks, ('yhi', 'x'), 0, 0, tiled=True)  57.7 us
    pallas_call x16, Pallas kernels, run(): pl.pallas_call(kernel, out_shape=list(outs) if many else outs, in_specs=s...  55.9 us
    ppermute x12, waiting for transfers between devices, round_z(): lax.ppermute(value, 'z', [(i, (i - d) % 4) for i in range(4)])  23.2 us
    ppermute x12, starting transfers between devices, round_z(): lax.ppermute(value, 'z', [(i, (i - d) % 4) for i in range(4)])  20.5 us
    unnamed x56, local copies, waits for them, and re-layouts  10.3 us
    all_to_all x2, starting transfers between devices, exchanged(): return lax.all_to_all(blocks, ('yhi', 'x'), 0, 0, tiled=True)  10.3 us
    ppermute x10, starting transfers between devices, swapped(): return lax.ppermute(value, axis, [(0, 1), (1, 0)])  4.31 us
  transfers between devices with their start and end apart: 24, of which 9 were waited for; matrix products, arithmetic and copies ran while one was open for 3% of the time, Pallas kernels for 21%

profile of v4, /device:TPU:0, one launch (start us, length us, event | category | flops | bytes accessed | tf_op | source)
XLA Modules:
  0.0 192.5 jit_solution(427390319294866714)
XLA Ops:
  10.4 8.4 %shard_map.133._ = s16[8,48,2048]{2,1,0:T(8,128)(2,1)} custom-call(s32[3]{0:T(128)} %pad_add_fusion.where_ref, f32[16,48,250]{2,1,0:T(8,128)} %dispatch_ref.1, f32[16,48,250]{2,1,0:T(8,128)} %collective-permute-done.other_ref, s32[1,250]{1,0:T(1,128)} %bitcast.35, s32[1,250]{1,0:T(1,128)} %bitcast.38, bf16[16,48,625]{2,1,0:T(8,128)(2,1)} %demand_own_ref.3, ...), custom_call_target="tpu_custom_call" | custom-call | tf_op jit(solution)/shard_map/pallas_call | solution.py:40
  18.9 6.7 %all-to-all-start = ((s16[8,48,2048]{2,1,0:T(8,128)(2,1)}), s16[8,48,2048]{2,1,0:T(8,128)(2,1)S(1)}, u32[]{:S(2)}, u32[]{:S(2)}) async-start(s16[8,48,2048]{2,1,0:T(8,128)(2,1)} %shard_map.133._), calls=%async_computation | async-start | bytes 3145728 | tf_op jit(solution)/shard_map/all_to_all | solution.py:340
  29.2 3.6 %collective-permute-start.6 = (s16[45,24,128]{2,1,0:T(8,128)(2,1)}, s16[45,24,128]{2,1,0:T(8,128)(2,1)S(1)}, u32[]{:S(2)}, u32[]{:S(2)}) collective-permute-start(s16[45,24,128]{2,1,0:T(8,128)(2,1)} %shard_map.134.rest_0_), channel_id=1, source_target_pairs={{0,32},{16,48},{32,0},{48,16},{1,33},{17,49},{33,1},{49,17},{2,34}... | collective-permute-start | bytes 829448 | tf_op jit(solution)/shard_map/ppermute | solution.py:382
  35.0 3.7 %shard_map.137.rest_1_ = bf16[2048,250]{1,0:T(8,128)(2,1)} custom-call(s32[1,250]{1,0:T(1,128)} %bitcast.36, bf16[2000,625]{1,0:T(8,128)(2,1)} %bitcast.32, s16[8,48,2048]{2,1,0:T(8,128)(2,1)} %shard_map.133._), custom_call_target="tpu_custom_call" | custom-call | tf_op jit(solution)/shard_map/pallas_call | solution.py:40
  40.6 3.8 %shard_map.138.rest_2_ = bf16[2048,250]{1,0:T(8,128)(2,1)} custom-call(s32[1,250]{1,0:T(1,128)} %bitcast.39, bf16[2000,625]{1,0:T(8,128)(2,1)} %copy-done.4, s16[8,48,2048]{2,1,0:T(8,128)(2,1)} %shard_map.133._), custom_call_target="tpu_custom_call" | custom-call | tf_op jit(solution)/shard_map/pallas_call | solution.py:40
  46.1 3.6 %shard_map.135 = (f32[16,48,250]{2,1,0:T(8,128)}, f32[16,48,250]{2,1,0:T(8,128)}) custom-call(s32[80]{0:T(128)} %shard_map.131.ids_ref, f32[16,48,250]{2,1,0:T(8,128)} %dispatch_ref.1, f32[16,48,250]{2,1,0:T(8,128)} %prices_ref.1, f32[1,250]{1,0:T(1,128)} %bitcast.42, f32[1,250]{1,0:T(1,128)} %bitcast.44, f32[1,250]{1,0:T(1,128)} %bitcast.46, ...), custom_call_target="tpu_custom_call" | custom-call | tf_op jit(solution)/shard_map/pallas_call | solution.py:40
  50.9 3.1 %shard_map.139 = bf16[8,48,2048]{2,1,0:T(8,128)(2,1)} custom-call(s16[8,48,2048]{2,1,0:T(8,128)(2,1)} %copy-done.5, f32[1,2048]{1,0:T(1,128)} %shard_map.136.limits_ref, f32[16,48,250]{2,1,0:T(8,128)} %get-tuple-element.16.rest_0_.stepped_ref, bf16[2048,250]{1,0:T(8,128)(2,1)} %shard_map.137.rest_1_, bf16[2048,250]{1,0:T(8,128)(2,1)} %shard_map.138.rest_2_), custom_call_target="tpu_custom_call" | custom-call | tf_op jit(solution)/shard_map/pallas_call | solution.py:40
  54.1 28.7 %all_to_all.20 = bf16[8,48,2048]{2,1,0:T(8,128)(2,1)S(1)} all-to-all(bf16[8,48,2048]{2,1,0:T(8,128)(2,1)} %shard_map.139), channel_id=1, replica_groups=mesh['ylo'=2,'z'=4,'yhi'=2,'x'=4,'core'=2] {'yhi','x'}, dimensions={0} | all-to-all | bytes 3145728 | tf_op jit(solution)/shard_map/all_to_all | solution.py:340
  86.1 3.0 %shard_map.140 = (f32[16,48,250]{2,1,0:T(8,128)}, f32[8,48,250]{2,1,0:T(8,128)}, s16[29,24,128]{2,1,0:T(8,128)(2,1)}) custom-call(s32[3]{0:T(128)} %pad_add_fusion.where_ref, s32[80]{0:T(128)} %shard_map.131.ids_ref, f32[16,48,250]{2,1,0:T(8,128)} %get-tuple-element.16.rest_0_.stepped_ref, f32[8,48,250]{2,1,0:T(8,128)} %fusion.6.pull_own_ref, ...), custom_call_target="tpu_custom_call" | custom-call | tf_op jit(solution)/shard_map/pallas_call | solution.py:40
  91.8 8.3 %shard_map.141 = s16[8,48,2048]{2,1,0:T(8,128)(2,1)} custom-call(s32[3]{0:T(128)} %pad_add_fusion.where_ref, f32[16,48,250]{2,1,0:T(8,128)} %get-tuple-element.18.own_ref.dispatch_ref, f32[8,48,250]{2,1,0:T(8,128)} %copy-done.8, s32[1,250]{1,0:T(1,128)} %bitcast.37, s32[1,250]{1,0:T(1,128)} %bitcast.40, bf16[16,48,625]{2,1,0:T(8,128)(2,1)} %demand_own_ref.3, ...), custom_call_target="tpu_custom_call" | custom-call | tf_op jit(solution)/shard_map/pallas_call | solution.py:40
  100.8 3.6 %all-to-all-start.2 = ((s16[8,48,2048]{2,1,0:T(8,128)(2,1)}), s16[8,48,2048]{2,1,0:T(8,128)(2,1)S(1)}, u32[]{:S(2)}, u32[]{:S(2)}) async-start(s16[8,48,2048]{2,1,0:T(8,128)(2,1)} %shard_map.141), calls=%async_computation.2 | async-start | bytes 3145728 | tf_op jit(solution)/shard_map/all_to_all | solution.py:340
  108.0 2.9 %collective-permute-start.12 = (s16[45,24,128]{2,1,0:T(8,128)(2,1)}, s16[45,24,128]{2,1,0:T(8,128)(2,1)S(1)}, u32[]{:S(2)}, u32[]{:S(2)}) collective-permute-start(s16[45,24,128]{2,1,0:T(8,128)(2,1)} %shard_map.142.rest_0_), channel_id=1, source_target_pairs={{0,32},{16,48},{32,0},{48,16},{1,33},{17,49},{33,1},{49,17},{2,34}... | collective-permute-start | bytes 829448 | tf_op jit(solution)/shard_map/ppermute | solution.py:382
  110.9 5.7 %collective-permute-done.13.rest_3_ = s16[45,24,128]{2,1,0:T(8,128)(2,1)S(1)} collective-permute-done((s16[45,24,128]{2,1,0:T(8,128)(2,1)}, s16[45,24,128]{2,1,0:T(8,128)(2,1)S(1)}, u32[]{:S(2)}, u32[]{:S(2)}) %collective-permute-start.13) | collective-permute-done | bytes 276512 | tf_op jit(solution)/shard_map/ppermute | solution.py:382
  116.5 7.1 %collective-permute-done.12.rest_2_ = s16[45,24,128]{2,1,0:T(8,128)(2,1)S(1)} collective-permute-done((s16[45,24,128]{2,1,0:T(8,128)(2,1)}, s16[45,24,128]{2,1,0:T(8,128)(2,1)S(1)}, u32[]{:S(2)}, u32[]{:S(2)}) %collective-permute-start.12) | collective-permute-done | bytes 276512 | tf_op jit(solution)/shard_map/ppermute | solution.py:382
  124.5 3.7 %shard_map.143 = (f32[16,48,250]{2,1,0:T(8,128)}, f32[16,48,250]{2,1,0:T(8,128)}) custom-call(s32[80]{0:T(128)} %shard_map.131.ids_ref, f32[16,48,250]{2,1,0:T(8,128)} %get-tuple-element.18.own_ref.dispatch_ref, f32[16,48,250]{2,1,0:T(8,128)} %get-tuple-element.19.prices_ref, f32[1,250]{1,0:T(1,128)} %bitcast.43, f32[1,250]{1,0:T(1,128)} %bitcast.45, ...), custom_call_target="tpu_custom_call" | custom-call | tf_op jit(solution)/shard_map/pallas_call | solution.py:40
  129.3 3.1 %shard_map.144 = bf16[8,48,2048]{2,1,0:T(8,128)(2,1)} custom-call(s16[8,48,2048]{2,1,0:T(8,128)(2,1)} %copy-done.6, f32[1,2048]{1,0:T(1,128)} %shard_map.136.limits_ref, f32[16,48,250]{2,1,0:T(8,128)} %get-tuple-element.23.rest_0_.stepped_ref, bf16[2048,250]{1,0:T(8,128)(2,1)} %shard_map.137.rest_1_, bf16[2048,250]{1,0:T(8,128)(2,1)} %shard_map.138.rest_2_), custom_call_target="tpu_custom_call" | custom-call | tf_op jit(solution)/shard_map/pallas_call | solution.py:40
  132.4 28.9 %all_to_all.21 = bf16[8,48,2048]{2,1,0:T(8,128)(2,1)S(1)} all-to-all(bf16[8,48,2048]{2,1,0:T(8,128)(2,1)} %shard_map.144), channel_id=1, replica_groups=mesh['ylo'=2,'z'=4,'yhi'=2,'x'=4,'core'=2] {'yhi','x'}, dimensions={0} | all-to-all | bytes 3145728 | tf_op jit(solution)/shard_map/all_to_all | solution.py:340
  164.7 2.9 %shard_map.145 = (f32[16,48,250]{2,1,0:T(8,128)}, f32[8,48,250]{2,1,0:T(8,128)}, s16[29,24,128]{2,1,0:T(8,128)(2,1)}) custom-call(s32[3]{0:T(128)} %pad_add_fusion.where_ref, s32[80]{0:T(128)} %shard_map.131.ids_ref, f32[16,48,250]{2,1,0:T(8,128)} %get-tuple-element.23.rest_0_.stepped_ref, f32[8,48,250]{2,1,0:T(8,128)} %fusion.4.pull_own_ref, ...), custom_call_target="tpu_custom_call" | custom-call | tf_op jit(solution)/shard_map/pallas_call | solution.py:40
  169.9 2.9 %collective-permute-start.18 = (s16[29,24,128]{2,1,0:T(8,128)(2,1)}, s16[29,24,128]{2,1,0:T(8,128)(2,1)S(1)}, u32[]{:S(2)}, u32[]{:S(2)}) collective-permute-start(s16[29,24,128]{2,1,0:T(8,128)(2,1)} %get-tuple-element.27.rest_0_), channel_id=1, source_target_pairs={{0,32},{16,48},{32,0},{48,16},{1,33},{17,49},{33,1},{49,17},{2,34}... | collective-permute-start | bytes 534536 | tf_op jit(solution)/shard_map/ppermute | solution.py:382
  175.8 2.9 %collective-permute-start.19 = (s16[29,24,128]{2,1,0:T(8,128)(2,1)S(1)}, s16[29,24,128]{2,1,0:T(8,128)(2,1)S(1)}, u32[]{:S(2)}, u32[]{:S(2)}) collective-permute-start(s16[29,24,128]{2,1,0:T(8,128)(2,1)S(1)} %collective-permute-done.15.rest_1_), channel_id=1, source_target_pairs={{0,32},{16,48},{32,0},{48,16},{1,33},{17,49},{33,1},{49,17},{2,34}... | collective-permute-start | bytes 534536 | tf_op jit(solution)/shard_map/ppermute | solution.py:382
  179.0 3.3 %collective-permute-done.18.rest_4_ = s16[29,24,128]{2,1,0:T(8,128)(2,1)S(1)} collective-permute-done((s16[29,24,128]{2,1,0:T(8,128)(2,1)}, s16[29,24,128]{2,1,0:T(8,128)(2,1)S(1)}, u32[]{:S(2)}, u32[]{:S(2)}) %collective-permute-start.18) | collective-permute-done | bytes 178208 | tf_op jit(solution)/shard_map/ppermute | solution.py:382
  182.3 2.5 %collective-permute-done.21.rest_7_ = s16[29,24,128]{2,1,0:T(8,128)(2,1)S(1)} collective-permute-done((s16[29,24,128]{2,1,0:T(8,128)(2,1)S(1)}, s16[29,24,128]{2,1,0:T(8,128)(2,1)S(1)}, u32[]{:S(2)}, u32[]{:S(2)}) %collective-permute-start.21) | collective-permute-done | bytes 178208 | tf_op jit(solution)/shard_map/ppermute | solution.py:382
  184.8 3.8 %collective-permute-done.19.rest_5_ = s16[29,24,128]{2,1,0:T(8,128)(2,1)S(1)} collective-permute-done((s16[29,24,128]{2,1,0:T(8,128)(2,1)S(1)}, s16[29,24,128]{2,1,0:T(8,128)(2,1)S(1)}, u32[]{:S(2)}, u32[]{:S(2)}) %collective-permute-start.19) | collective-permute-done | bytes 178208 | tf_op jit(solution)/shard_map/ppermute | solution.py:382
  189.3 3.2 %shard_map.146 = f32[16,48,250]{2,1,0:T(8,128)} custom-call(s32[80]{0:T(128)} %shard_map.131.ids_ref, f32[16,48,250]{2,1,0:T(8,128)} %get-tuple-element.13.dispatch_ref, f32[16,48,250]{2,1,0:T(8,128)} %get-tuple-element.26.prices_ref, s16[29,24,128]{2,1,0:T(8,128)(2,1)} %get-tuple-element.27.rest_0_, s16[29,24,128]{2,1,0:T(8,128)(2,1)} %copy-done.18, ...), custom_call_target="tpu_custom_call" | custom-call | tf_op jit(solution)/shard_map/pallas_call | solution.py:40
  (106 shorter events, 42.3 us)
Async XLA Ops:
  0.6 8.0 %collective-permute-start.3 = (bf16[2000,625]{1,0:T(8,128)(2,1)}, bf16[2000,625]{1,0:T(8,128)(2,1)S(1)}, u32[]{:S(2)}, u32[]{:S(2)}) collective-permute-start(bf16[2000,625]{1,0:T(8,128)(2,1)} %bitcast.30), channel_id=1, source_target_pairs={{0,1},{1,0},{2,3},{3,2},{4,5},{5,4},{6,7},{7,6},{8,9},{9,8},{10,11... | collective-permute-start | bytes 7500008 | tf_op jit(solution)/shard_map/ppermute | solution.py:336
  0.7 7.9 %collective-permute-start.2 = (bf16[16,48,625]{2,1,0:T(8,128)(2,1)}, bf16[16,48,625]{2,1,0:T(8,128)(2,1)S(1)}, u32[]{:S(2)}, u32[]{:S(2)}) collective-permute-start(bf16[16,48,625]{2,1,0:T(8,128)(2,1)} %demand_own_ref.3), channel_id=1, source_target_pairs={{0,1},{1,0},{2,3},{3,2},{4,5},{5,4},{6,7},{7,6},{8,9},{9,8},{10,11... | collective-permute-start | bytes 2880008 | tf_op jit(solution)/shard_map/ppermute | solution.py:336
  1.2 7.4 %collective-permute-start = (f32[16,48,250]{2,1,0:T(8,128)}, f32[16,48,250]{2,1,0:T(8,128)}, u32[]{:S(2)}, u32[]{:S(2)}) collective-permute-start(f32[16,48,250]{2,1,0:T(8,128)} %dispatch_ref.1), channel_id=1, source_target_pairs={{0,1},{1,0},{2,3},{3,2},{4,5},{5,4},{6,7},{7,6},{8,9},{9,8},{10,11... | collective-permute-start | bytes 2304008 | tf_op jit(solution)/shard_map/ppermute | solution.py:336
  5.6 13.2 %collective-permute-start.4 = (s16[29,24,128]{2,1,0:T(8,128)(2,1)}, s16[29,24,128]{2,1,0:T(8,128)(2,1)}, u32[]{:S(2)}, u32[]{:S(2)}) collective-permute-start(s16[29,24,128]{2,1,0:T(8,128)(2,1)} %shard_map.132.rest_0_.own_ref), channel_id=1, source_target_pairs={{0,64},{64,0},{1,65},{65,1},{2,66},{66,2},{3,67},{67,3},{4,68},{68... | collective-permute-start | bytes 534536 | tf_op jit(solution)/shard_map/ppermute | solution.py:336
  7.3 1.4 collective-permute-start.1
  18.9 30.9 %all-to-all-start = ((s16[8,48,2048]{2,1,0:T(8,128)(2,1)}), s16[8,48,2048]{2,1,0:T(8,128)(2,1)S(1)}, u32[]{:S(2)}, u32[]{:S(2)}) async-start(s16[8,48,2048]{2,1,0:T(8,128)(2,1)} %shard_map.133._), calls=%async_computation | async-start | bytes 3145728 | tf_op jit(solution)/shard_map/all_to_all | solution.py:340
  27.3 17.1 %collective-permute-start.7 = (s16[45,24,128]{2,1,0:T(8,128)(2,1)}, s16[45,24,128]{2,1,0:T(8,128)(2,1)S(1)}, u32[]{:S(2)}, u32[]{:S(2)}) collective-permute-start(s16[45,24,128]{2,1,0:T(8,128)(2,1)} %shard_map.134.rest_0_), channel_id=1, source_target_pairs={{0,16},{16,32},{32,48},{48,0},{1,17},{17,33},{33,49},{49,1},{2,18}... | collective-permute-start | bytes 829448 | tf_op jit(solution)/shard_map/ppermute | solution.py:382
  29.2 16.1 %collective-permute-start.6 = (s16[45,24,128]{2,1,0:T(8,128)(2,1)}, s16[45,24,128]{2,1,0:T(8,128)(2,1)S(1)}, u32[]{:S(2)}, u32[]{:S(2)}) collective-permute-start(s16[45,24,128]{2,1,0:T(8,128)(2,1)} %shard_map.134.rest_0_), channel_id=1, source_target_pairs={{0,32},{16,48},{32,0},{48,16},{1,33},{17,49},{33,1},{49,17},{2,34}... | collective-permute-start | bytes 829448 | tf_op jit(solution)/shard_map/ppermute | solution.py:382
  32.8 12.5 %collective-permute-start.5 = (s16[45,24,128]{2,1,0:T(8,128)(2,1)}, s16[45,24,128]{2,1,0:T(8,128)(2,1)S(1)}, u32[]{:S(2)}, u32[]{:S(2)}) collective-permute-start(s16[45,24,128]{2,1,0:T(8,128)(2,1)} %shard_map.134.rest_0_), channel_id=1, source_target_pairs={{0,48},{16,0},{32,16},{48,32},{1,49},{17,1},{33,17},{49,33},{2,50}... | collective-permute-start | bytes 829448 | tf_op jit(solution)/shard_map/ppermute | solution.py:382
  83.4 2.0 %collective-permute-start.8 = (f32[8,48,250]{2,1,0:T(8,128)S(1)}, f32[8,48,250]{2,1,0:T(8,128)S(1)}, u32[]{:S(2)}, u32[]{:S(2)}) collective-permute-start(f32[8,48,250]{2,1,0:T(8,128)S(1)} %fusion.2), channel_id=1, source_target_pairs={{0,1},{1,0},{2,3},{3,2},{4,5},{5,4},{6,7},{7,6},{8,9},{9,8},{10,11... | collective-permute-start | bytes 1152008 | tf_op jit(solution)/shard_map/ppermute | solution.py:336
  89.1 1.9 %collective-permute-start.9 = (f32[8,48,250]{2,1,0:T(8,128)}, f32[8,48,250]{2,1,0:T(8,128)S(1)}, u32[]{:S(2)}, u32[]{:S(2)}) collective-permute-start(f32[8,48,250]{2,1,0:T(8,128)} %get-tuple-element.21), channel_id=1, source_target_pairs={{0,1},{1,0},{2,3},{3,2},{4,5},{5,4},{6,7},{7,6},{8,9},{9,8},{10,11... | collective-permute-start | bytes 1152008 | tf_op jit(solution)/shard_map/ppermute | solution.py:336
  89.2 10.8 %collective-permute-start.10 = (s16[29,24,128]{2,1,0:T(8,128)(2,1)}, s16[29,24,128]{2,1,0:T(8,128)(2,1)S(1)}, u32[]{:S(2)}, u32[]{:S(2)}) collective-permute-start(s16[29,24,128]{2,1,0:T(8,128)(2,1)} %get-tuple-element.20.rest_0_.own_ref), channel_id=1, source_target_pairs={{0,64},{64,0},{1,65},{65,1},{2,66},{66,2},{3,67},{67,3},{4,68},{68... | collective-permute-start | bytes 534536 | tf_op jit(solution)/shard_map/ppermute | solution.py:336
  100.8 27.4 %all-to-all-start.2 = ((s16[8,48,2048]{2,1,0:T(8,128)(2,1)}), s16[8,48,2048]{2,1,0:T(8,128)(2,1)S(1)}, u32[]{:S(2)}, u32[]{:S(2)}) async-start(s16[8,48,2048]{2,1,0:T(8,128)(2,1)} %shard_map.141), calls=%async_computation.2 | async-start | bytes 3145728 | tf_op jit(solution)/shard_map/all_to_all | solution.py:340
  106.1 10.4 %collective-permute-start.13 = (s16[45,24,128]{2,1,0:T(8,128)(2,1)}, s16[45,24,128]{2,1,0:T(8,128)(2,1)S(1)}, u32[]{:S(2)}, u32[]{:S(2)}) collective-permute-start(s16[45,24,128]{2,1,0:T(8,128)(2,1)} %shard_map.142.rest_0_), channel_id=1, source_target_pairs={{0,16},{16,32},{32,48},{48,0},{1,17},{17,33},{33,49},{49,1},{2,18}... | collective-permute-start | bytes 829448 | tf_op jit(solution)/shard_map/ppermute | solution.py:382
  108.0 15.7 %collective-permute-start.12 = (s16[45,24,128]{2,1,0:T(8,128)(2,1)}, s16[45,24,128]{2,1,0:T(8,128)(2,1)S(1)}, u32[]{:S(2)}, u32[]{:S(2)}) collective-permute-start(s16[45,24,128]{2,1,0:T(8,128)(2,1)} %shard_map.142.rest_0_), channel_id=1, source_target_pairs={{0,32},{16,48},{32,0},{48,16},{1,33},{17,49},{33,1},{49,17},{2,34}... | collective-permute-start | bytes 829448 | tf_op jit(solution)/shard_map/ppermute | solution.py:382
  110.9 12.8 %collective-permute-start.11 = (s16[45,24,128]{2,1,0:T(8,128)(2,1)}, s16[45,24,128]{2,1,0:T(8,128)(2,1)S(1)}, u32[]{:S(2)}, u32[]{:S(2)}) collective-permute-start(s16[45,24,128]{2,1,0:T(8,128)(2,1)} %shard_map.142.rest_0_), channel_id=1, source_target_pairs={{0,48},{16,0},{32,16},{48,32},{1,49},{17,1},{33,17},{49,33},{2,50}... | collective-permute-start | bytes 829448 | tf_op jit(solution)/shard_map/ppermute | solution.py:382
  162.0 2.0 %collective-permute-start.14 = (f32[8,48,250]{2,1,0:T(8,128)S(1)}, f32[8,48,250]{2,1,0:T(8,128)S(1)}, u32[]{:S(2)}, u32[]{:S(2)}) collective-permute-start(f32[8,48,250]{2,1,0:T(8,128)S(1)} %fusion), channel_id=1, source_target_pairs={{0,1},{1,0},{2,3},{3,2},{4,5},{5,4},{6,7},{7,6},{8,9},{9,8},{10,11... | collective-permute-start | bytes 1152008 | tf_op jit(solution)/shard_map/ppermute | solution.py:336
  167.7 6.6 %collective-permute-start.15 = (s16[29,24,128]{2,1,0:T(8,128)(2,1)}, s16[29,24,128]{2,1,0:T(8,128)(2,1)S(1)}, u32[]{:S(2)}, u32[]{:S(2)}) collective-permute-start(s16[29,24,128]{2,1,0:T(8,128)(2,1)} %get-tuple-element.27.rest_0_), channel_id=1, source_target_pairs={{0,64},{64,0},{1,65},{65,1},{2,66},{66,2},{3,67},{67,3},{4,68},{68... | collective-permute-start | bytes 534536 | tf_op jit(solution)/shard_map/ppermute | solution.py:336
  168.3 10.4 %collective-permute-start.20 = (s16[29,24,128]{2,1,0:T(8,128)(2,1)}, s16[29,24,128]{2,1,0:T(8,128)(2,1)S(1)}, u32[]{:S(2)}, u32[]{:S(2)}) collective-permute-start(s16[29,24,128]{2,1,0:T(8,128)(2,1)} %get-tuple-element.27.rest_0_), channel_id=1, source_target_pairs={{0,16},{16,32},{32,48},{48,0},{1,17},{17,33},{33,49},{49,1},{2,18}... | collective-permute-start | bytes 534536 | tf_op jit(solution)/shard_map/ppermute | solution.py:382
  169.9 12.4 %collective-permute-start.18 = (s16[29,24,128]{2,1,0:T(8,128)(2,1)}, s16[29,24,128]{2,1,0:T(8,128)(2,1)S(1)}, u32[]{:S(2)}, u32[]{:S(2)}) collective-permute-start(s16[29,24,128]{2,1,0:T(8,128)(2,1)} %get-tuple-element.27.rest_0_), channel_id=1, source_target_pairs={{0,32},{16,48},{32,0},{48,16},{1,33},{17,49},{33,1},{49,17},{2,34}... | collective-permute-start | bytes 534536 | tf_op jit(solution)/shard_map/ppermute | solution.py:382
  172.8 9.5 %collective-permute-start.16 = (s16[29,24,128]{2,1,0:T(8,128)(2,1)}, s16[29,24,128]{2,1,0:T(8,128)(2,1)S(1)}, u32[]{:S(2)}, u32[]{:S(2)}) collective-permute-start(s16[29,24,128]{2,1,0:T(8,128)(2,1)} %get-tuple-element.27.rest_0_), channel_id=1, source_target_pairs={{0,48},{16,0},{32,16},{48,32},{1,49},{17,1},{33,17},{49,33},{2,50}... | collective-permute-start | bytes 534536 | tf_op jit(solution)/shard_map/ppermute | solution.py:382
  174.2 10.5 %collective-permute-start.21 = (s16[29,24,128]{2,1,0:T(8,128)(2,1)S(1)}, s16[29,24,128]{2,1,0:T(8,128)(2,1)S(1)}, u32[]{:S(2)}, u32[]{:S(2)}) collective-permute-start(s16[29,24,128]{2,1,0:T(8,128)(2,1)S(1)} %collective-permute-done.15.rest_1_), channel_id=1, source_target_pairs={{0,16},{16,32},{32,48},{48,0},{1,17},{17,33},{33,49},{49,1},{2,18}... | collective-permute-start | bytes 534536 | tf_op jit(solution)/shard_map/ppermute | solution.py:382
  175.8 12.8 %collective-permute-start.19 = (s16[29,24,128]{2,1,0:T(8,128)(2,1)S(1)}, s16[29,24,128]{2,1,0:T(8,128)(2,1)S(1)}, u32[]{:S(2)}, u32[]{:S(2)}) collective-permute-start(s16[29,24,128]{2,1,0:T(8,128)(2,1)S(1)} %collective-permute-done.15.rest_1_), channel_id=1, source_target_pairs={{0,32},{16,48},{32,0},{48,16},{1,33},{17,49},{33,1},{49,17},{2,34}... | collective-permute-start | bytes 534536 | tf_op jit(solution)/shard_map/ppermute | solution.py:382
  178.7 9.9 %collective-permute-start.17 = (s16[29,24,128]{2,1,0:T(8,128)(2,1)S(1)}, s16[29,24,128]{2,1,0:T(8,128)(2,1)S(1)}, u32[]{:S(2)}, u32[]{:S(2)}) collective-permute-start(s16[29,24,128]{2,1,0:T(8,128)(2,1)S(1)} %collective-permute-done.15.rest_1_), channel_id=1, source_target_pairs={{0,48},{16,0},{32,16},{48,32},{1,49},{17,1},{33,17},{49,33},{2,50}... | collective-permute-start | bytes 534536 | tf_op jit(solution)/shard_map/ppermute | solution.py:382
  (28 other events, 152.6 us)

commit v5 on v4

--- a/solution.py
+++ b/solution.py
@@ -297,7 +297,7 @@
         out_ref[s] = dispatch - 0.25 * gradient
         return carry
 
-    lax.fori_loop(0, count, step, 0)
+    lax.fori_loop(0, count, step, 0, unroll=4)
 
 
 def clip_kernel(
@@ -315,7 +315,7 @@
         send_ref[i] = one(8 * (1 - core) + i, pull_other_ref[i])
         return carry
 
-    lax.fori_loop(0, 8, step, 0)
+    lax.fori_loop(0, 8, step, 0, unroll=4)
     pack(ids_ref, out_ref, pack_ref)
 
 
@@ -329,7 +329,7 @@
         out_ref[s] = prices_ref[s] + (dispatch - average_of(s, dispatch))
         return carry
 
-    lax.fori_loop(0, count, step, 0)
+    lax.fori_loop(0, count, step, 0, unroll=4)
 
 
 def swapped(value, axis="core"):
@@ -378,8 +378,15 @@
         both = (2 * count + sum(NODE_WIDTH),) + payload[1:]
         return call(join_kernel, shape(both, jnp.int16))(own, beside)
 
+    def from_z(value, d):
+        return lax.ppermute(value, "z", [(i, (i - d) % 4) for i in range(4)])
+
     def round_z(value):
-        return [lax.ppermute(value, "z", [(i, (i - d) % 4) for i in range(4)]) for d in (1, 2, 3)]
+        return [from_z(value, d) for d in (1, 2, 3)]
+
+    def forwarded_z(value):
+        beyond = from_z(value, 1)
+        return [beyond, from_z(beyond, 1), from_z(value, 3)]
 
     lines = ptdf.T
     lines_other = swapped(lines)
@@ -455,7 +462,7 @@
         if step + 1 < ITERS:
             dispatch_other = swapped(send)
     beside = swapped(own, "ylo")
-    near, far = [own] + round_z(own), [beside] + round_z(beside)
+    near, far = [own] + forwarded_z(own), [beside] + forwarded_z(beside)
     nodes = [payloads[d] for d in range(4) for payloads in (near, far)]
     prices = call(prices_kernel, shape(whole, F32), unpacking)(ids, dispatch, prices, *nodes)
     return (dispatch, prices)

time: 193 us -> 192 us (level)
  waiting for transfers between devices: 26.4 us -> 22.1 us
  starting transfers between devices: 35.1 us -> 38.9 us
    ppermute x12, waiting for transfers between devices: 23.2 us -> 17.4 us  [from_z(): return lax.ppermute(value, 'z', [(i, (i - d) % 4) for i in range(4)])]
    ppermute x12, starting transfers between devices: 20.5 us -> 24.3 us  [from_z(): return lax.ppermute(value, 'z', [(i, (i - d) % 4) for i in range(4)])]
  transfers between devices with their start and end apart: 24 -> 24, of which waited for: 9 -> 10; matrix products, arithmetic and copies ran while one was open for 3% -> 3% of each run, Pallas kernels for 21% -> 21%
where the time goes in v5:
time: 192 us; the launch traced here: 191 us
  blocking collectives  57.7 us (30%)
  Pallas kernels  55.4 us (29%)
  starting transfers between devices  38.9 us (20%)
  waiting for transfers between devices  22.1 us (12%)
  local copies, waits for them, and re-layouts  11.5 us (6%)
  matrix products  3.82 us (2%)
    all_to_all x2, blocking collectives, exchanged(): return lax.all_to_all(blocks, ('yhi', 'x'), 0, 0, tiled=True)  57.7 us
    pallas_call x16, Pallas kernels, run(): pl.pallas_call(kernel, out_shape=list(outs) if many else outs, in_specs=s...  55.4 us
    ppermute x12, starting transfers between devices, from_z(): return lax.ppermute(value, 'z', [(i, (i - d) % 4) for i in range(4)])  24.3 us
    ppermute x12, waiting for transfers between devices, from_z(): return lax.ppermute(value, 'z', [(i, (i - d) % 4) for i in range(4)])  17.4 us
    all_to_all x2, starting transfers between devices, exchanged(): return lax.all_to_all(blocks, ('yhi', 'x'), 0, 0, tiled=True)  10.3 us
    unnamed x56, local copies, waits for them, and re-layouts  10.3 us
    ppermute x10, waiting for transfers between devices, swapped(): return lax.ppermute(value, axis, [(0, 1), (1, 0)])  4.64 us
    ppermute x10, starting transfers between devices, swapped(): return lax.ppermute(value, axis, [(0, 1), (1, 0)])  4.3 us
  transfers between devices with their start and end apart: 24, of which 10 were waited for; matrix products, arithmetic and copies ran while one was open for 3% of the time, Pallas kernels for 21%

profile of v5, /device:TPU:0, one launch (start us, length us, event | category | flops | bytes accessed | tf_op | source)
XLA Modules:
  0.0 191.4 jit_solution(11405535603967651013)
XLA Ops:
  10.4 8.4 %shard_map.133._ = s16[8,48,2048]{2,1,0:T(8,128)(2,1)} custom-call(s32[3]{0:T(128)} %pad_add_fusion.where_ref, f32[16,48,250]{2,1,0:T(8,128)} %dispatch_ref.1, f32[16,48,250]{2,1,0:T(8,128)} %collective-permute-done.other_ref, s32[1,250]{1,0:T(1,128)} %bitcast.35, s32[1,250]{1,0:T(1,128)} %bitcast.38, bf16[16,48,625]{2,1,0:T(8,128)(2,1)} %demand_own_ref.3, ...), custom_call_target="tpu_custom_call" | custom-call | tf_op jit(solution)/shard_map/pallas_call | solution.py:40
  18.9 6.7 %all-to-all-start = ((s16[8,48,2048]{2,1,0:T(8,128)(2,1)}), s16[8,48,2048]{2,1,0:T(8,128)(2,1)S(1)}, u32[]{:S(2)}, u32[]{:S(2)}) async-start(s16[8,48,2048]{2,1,0:T(8,128)(2,1)} %shard_map.133._), calls=%async_computation | async-start | bytes 3145728 | tf_op jit(solution)/shard_map/all_to_all | solution.py:340
  29.2 3.6 %collective-permute-start.6 = (s16[45,24,128]{2,1,0:T(8,128)(2,1)}, s16[45,24,128]{2,1,0:T(8,128)(2,1)S(1)}, u32[]{:S(2)}, u32[]{:S(2)}) collective-permute-start(s16[45,24,128]{2,1,0:T(8,128)(2,1)} %shard_map.134.rest_0_), channel_id=1, source_target_pairs={{0,32},{16,48},{32,0},{48,16},{1,33},{17,49},{33,1},{49,17},{2,34}... | collective-permute-start | bytes 829448 | tf_op jit(solution)/shard_map/ppermute | solution.py:382
  35.0 3.7 %shard_map.137.rest_1_ = bf16[2048,250]{1,0:T(8,128)(2,1)} custom-call(s32[1,250]{1,0:T(1,128)} %bitcast.36, bf16[2000,625]{1,0:T(8,128)(2,1)} %bitcast.32, s16[8,48,2048]{2,1,0:T(8,128)(2,1)} %shard_map.133._), custom_call_target="tpu_custom_call" | custom-call | tf_op jit(solution)/shard_map/pallas_call | solution.py:40
  40.6 3.8 %shard_map.138.rest_2_ = bf16[2048,250]{1,0:T(8,128)(2,1)} custom-call(s32[1,250]{1,0:T(1,128)} %bitcast.39, bf16[2000,625]{1,0:T(8,128)(2,1)} %copy-done.4, s16[8,48,2048]{2,1,0:T(8,128)(2,1)} %shard_map.133._), custom_call_target="tpu_custom_call" | custom-call | tf_op jit(solution)/shard_map/pallas_call | solution.py:40
  46.1 3.5 %shard_map.135 = (f32[16,48,250]{2,1,0:T(8,128)}, f32[16,48,250]{2,1,0:T(8,128)}) custom-call(s32[80]{0:T(128)} %shard_map.131.ids_ref, f32[16,48,250]{2,1,0:T(8,128)} %dispatch_ref.1, f32[16,48,250]{2,1,0:T(8,128)} %prices_ref.1, f32[1,250]{1,0:T(1,128)} %bitcast.42, f32[1,250]{1,0:T(1,128)} %bitcast.44, f32[1,250]{1,0:T(1,128)} %bitcast.46, ...), custom_call_target="tpu_custom_call" | custom-call | tf_op jit(solution)/shard_map/pallas_call | solution.py:40
  50.8 3.1 %shard_map.139 = bf16[8,48,2048]{2,1,0:T(8,128)(2,1)} custom-call(s16[8,48,2048]{2,1,0:T(8,128)(2,1)} %copy-done.5, f32[1,2048]{1,0:T(1,128)} %shard_map.136.limits_ref, f32[16,48,250]{2,1,0:T(8,128)} %get-tuple-element.16.rest_0_.stepped_ref, bf16[2048,250]{1,0:T(8,128)(2,1)} %shard_map.137.rest_1_, bf16[2048,250]{1,0:T(8,128)(2,1)} %shard_map.138.rest_2_), custom_call_target="tpu_custom_call" | custom-call | tf_op jit(solution)/shard_map/pallas_call | solution.py:40
  54.0 28.7 %all_to_all.20 = bf16[8,48,2048]{2,1,0:T(8,128)(2,1)S(1)} all-to-all(bf16[8,48,2048]{2,1,0:T(8,128)(2,1)} %shard_map.139), channel_id=1, replica_groups=mesh['ylo'=2,'z'=4,'yhi'=2,'x'=4,'core'=2] {'yhi','x'}, dimensions={0} | all-to-all | bytes 3145728 | tf_op jit(solution)/shard_map/all_to_all | solution.py:340
  86.0 2.9 %shard_map.140 = (f32[16,48,250]{2,1,0:T(8,128)}, f32[8,48,250]{2,1,0:T(8,128)}, s16[29,24,128]{2,1,0:T(8,128)(2,1)}) custom-call(s32[3]{0:T(128)} %pad_add_fusion.where_ref, s32[80]{0:T(128)} %shard_map.131.ids_ref, f32[16,48,250]{2,1,0:T(8,128)} %get-tuple-element.16.rest_0_.stepped_ref, f32[8,48,250]{2,1,0:T(8,128)} %fusion.6.pull_own_ref, ...), custom_call_target="tpu_custom_call" | custom-call | tf_op jit(solution)/shard_map/pallas_call | solution.py:40
  91.6 8.3 %shard_map.141 = s16[8,48,2048]{2,1,0:T(8,128)(2,1)} custom-call(s32[3]{0:T(128)} %pad_add_fusion.where_ref, f32[16,48,250]{2,1,0:T(8,128)} %get-tuple-element.18.own_ref.dispatch_ref, f32[8,48,250]{2,1,0:T(8,128)} %copy-done.8, s32[1,250]{1,0:T(1,128)} %bitcast.37, s32[1,250]{1,0:T(1,128)} %bitcast.40, bf16[16,48,625]{2,1,0:T(8,128)(2,1)} %demand_own_ref.3, ...), custom_call_target="tpu_custom_call" | custom-call | tf_op jit(solution)/shard_map/pallas_call | solution.py:40
  100.6 3.6 %all-to-all-start.2 = ((s16[8,48,2048]{2,1,0:T(8,128)(2,1)}), s16[8,48,2048]{2,1,0:T(8,128)(2,1)S(1)}, u32[]{:S(2)}, u32[]{:S(2)}) async-start(s16[8,48,2048]{2,1,0:T(8,128)(2,1)} %shard_map.141), calls=%async_computation.2 | async-start | bytes 3145728 | tf_op jit(solution)/shard_map/all_to_all | solution.py:340
  107.8 2.9 %collective-permute-start.12 = (s16[45,24,128]{2,1,0:T(8,128)(2,1)}, s16[45,24,128]{2,1,0:T(8,128)(2,1)S(1)}, u32[]{:S(2)}, u32[]{:S(2)}) collective-permute-start(s16[45,24,128]{2,1,0:T(8,128)(2,1)} %shard_map.142.rest_0_), channel_id=1, source_target_pairs={{0,32},{16,48},{32,0},{48,16},{1,33},{17,49},{33,1},{49,17},{2,34}... | collective-permute-start | bytes 829448 | tf_op jit(solution)/shard_map/ppermute | solution.py:382
  110.7 5.7 %collective-permute-done.13.rest_3_ = s16[45,24,128]{2,1,0:T(8,128)(2,1)S(1)} collective-permute-done((s16[45,24,128]{2,1,0:T(8,128)(2,1)}, s16[45,24,128]{2,1,0:T(8,128)(2,1)S(1)}, u32[]{:S(2)}, u32[]{:S(2)}) %collective-permute-start.13) | collective-permute-done | bytes 276512 | tf_op jit(solution)/shard_map/ppermute | solution.py:382
  116.4 7.1 %collective-permute-done.12.rest_2_ = s16[45,24,128]{2,1,0:T(8,128)(2,1)S(1)} collective-permute-done((s16[45,24,128]{2,1,0:T(8,128)(2,1)}, s16[45,24,128]{2,1,0:T(8,128)(2,1)S(1)}, u32[]{:S(2)}, u32[]{:S(2)}) %collective-permute-start.12) | collective-permute-done | bytes 276512 | tf_op jit(solution)/shard_map/ppermute | solution.py:382
  124.3 3.6 %shard_map.143 = (f32[16,48,250]{2,1,0:T(8,128)}, f32[16,48,250]{2,1,0:T(8,128)}) custom-call(s32[80]{0:T(128)} %shard_map.131.ids_ref, f32[16,48,250]{2,1,0:T(8,128)} %get-tuple-element.18.own_ref.dispatch_ref, f32[16,48,250]{2,1,0:T(8,128)} %get-tuple-element.19.prices_ref, f32[1,250]{1,0:T(1,128)} %bitcast.43, f32[1,250]{1,0:T(1,128)} %bitcast.45, ...), custom_call_target="tpu_custom_call" | custom-call | tf_op jit(solution)/shard_map/pallas_call | solution.py:40
  129.1 3.1 %shard_map.144 = bf16[8,48,2048]{2,1,0:T(8,128)(2,1)} custom-call(s16[8,48,2048]{2,1,0:T(8,128)(2,1)} %copy-done.6, f32[1,2048]{1,0:T(1,128)} %shard_map.136.limits_ref, f32[16,48,250]{2,1,0:T(8,128)} %get-tuple-element.23.rest_0_.stepped_ref, bf16[2048,250]{1,0:T(8,128)(2,1)} %shard_map.137.rest_1_, bf16[2048,250]{1,0:T(8,128)(2,1)} %shard_map.138.rest_2_), custom_call_target="tpu_custom_call" | custom-call | tf_op jit(solution)/shard_map/pallas_call | solution.py:40
  132.2 28.9 %all_to_all.21 = bf16[8,48,2048]{2,1,0:T(8,128)(2,1)S(1)} all-to-all(bf16[8,48,2048]{2,1,0:T(8,128)(2,1)} %shard_map.144), channel_id=1, replica_groups=mesh['ylo'=2,'z'=4,'yhi'=2,'x'=4,'core'=2] {'yhi','x'}, dimensions={0} | all-to-all | bytes 3145728 | tf_op jit(solution)/shard_map/all_to_all | solution.py:340
  164.4 2.9 %shard_map.145 = (f32[16,48,250]{2,1,0:T(8,128)}, f32[8,48,250]{2,1,0:T(8,128)}, s16[29,24,128]{2,1,0:T(8,128)(2,1)}) custom-call(s32[3]{0:T(128)} %pad_add_fusion.where_ref, s32[80]{0:T(128)} %shard_map.131.ids_ref, f32[16,48,250]{2,1,0:T(8,128)} %get-tuple-element.23.rest_0_.stepped_ref, f32[8,48,250]{2,1,0:T(8,128)} %fusion.4.pull_own_ref, ...), custom_call_target="tpu_custom_call" | custom-call | tf_op jit(solution)/shard_map/pallas_call | solution.py:40
  168.0 3.0 %collective-permute-start.16 = (s16[29,24,128]{2,1,0:T(8,128)(2,1)}, s16[29,24,128]{2,1,0:T(8,128)(2,1)S(1)}, u32[]{:S(2)}, u32[]{:S(2)}) collective-permute-start(s16[29,24,128]{2,1,0:T(8,128)(2,1)} %get-tuple-element.27.rest_0_), channel_id=1, source_target_pairs={{0,48},{16,0},{32,16},{48,32},{1,49},{17,1},{33,17},{49,33},{2,50}... | collective-permute-start | bytes 534536 | tf_op jit(solution)/shard_map/ppermute | solution.py:382
  171.0 2.9 %collective-permute-done.15.rest_1_ = s16[29,24,128]{2,1,0:T(8,128)(2,1)S(1)} collective-permute-done((s16[29,24,128]{2,1,0:T(8,128)(2,1)}, s16[29,24,128]{2,1,0:T(8,128)(2,1)S(1)}, u32[]{:S(2)}, u32[]{:S(2)}) %collective-permute-start.15) | collective-permute-done | bytes 178208 | tf_op jit(solution)/shard_map/ppermute | solution.py:336
  173.9 3.0 %collective-permute-start.17 = (s16[29,24,128]{2,1,0:T(8,128)(2,1)S(1)}, s16[29,24,128]{2,1,0:T(8,128)(2,1)S(1)}, u32[]{:S(2)}, u32[]{:S(2)}) collective-permute-start(s16[29,24,128]{2,1,0:T(8,128)(2,1)S(1)} %collective-permute-done.15.rest_1_), channel_id=1, source_target_pairs={{0,48},{16,0},{32,16},{48,32},{1,49},{17,1},{33,17},{49,33},{2,50}... | collective-permute-start | bytes 534536 | tf_op jit(solution)/shard_map/ppermute | solution.py:382
  177.5 2.7 %collective-permute-start.18 = (s16[29,24,128]{2,1,0:T(8,128)(2,1)S(1)}, s16[29,24,128]{2,1,0:T(8,128)(2,1)S(1)}, u32[]{:S(2)}, u32[]{:S(2)}) collective-permute-start(s16[29,24,128]{2,1,0:T(8,128)(2,1)S(1)} %collective-permute-done.16.rest_2_), channel_id=1, source_target_pairs={{0,48},{16,0},{32,16},{48,32},{1,49},{17,1},{33,17},{49,33},{2,50}... | collective-permute-start | bytes 534536 | tf_op jit(solution)/shard_map/ppermute | solution.py:382
  181.0 3.7 %collective-permute-start.19 = (s16[29,24,128]{2,1,0:T(8,128)(2,1)S(1)}, s16[29,24,128]{2,1,0:T(8,128)(2,1)S(1)}, u32[]{:S(2)}, u32[]{:S(2)}) collective-permute-start(s16[29,24,128]{2,1,0:T(8,128)(2,1)S(1)} %collective-permute-done.17.rest_3_), channel_id=1, source_target_pairs={{0,48},{16,0},{32,16},{48,32},{1,49},{17,1},{33,17},{49,33},{2,50}... | collective-permute-start | bytes 534536 | tf_op jit(solution)/shard_map/ppermute | solution.py:382
  188.4 3.0 %shard_map.146 = f32[16,48,250]{2,1,0:T(8,128)} custom-call(s32[80]{0:T(128)} %shard_map.131.ids_ref, f32[16,48,250]{2,1,0:T(8,128)} %get-tuple-element.13.dispatch_ref, f32[16,48,250]{2,1,0:T(8,128)} %get-tuple-element.26.prices_ref, s16[29,24,128]{2,1,0:T(8,128)(2,1)} %get-tuple-element.27.rest_0_, s16[29,24,128]{2,1,0:T(8,128)(2,1)} %copy-done.18, ...), custom_call_target="tpu_custom_call" | custom-call | tf_op jit(solution)/shard_map/pallas_call | solution.py:40
  (106 shorter events, 41.7 us)
Async XLA Ops:
  0.6 8.0 %collective-permute-start.3 = (bf16[2000,625]{1,0:T(8,128)(2,1)}, bf16[2000,625]{1,0:T(8,128)(2,1)S(1)}, u32[]{:S(2)}, u32[]{:S(2)}) collective-permute-start(bf16[2000,625]{1,0:T(8,128)(2,1)} %bitcast.30), channel_id=1, source_target_pairs={{0,1},{1,0},{2,3},{3,2},{4,5},{5,4},{6,7},{7,6},{8,9},{9,8},{10,11... | collective-permute-start | bytes 7500008 | tf_op jit(solution)/shard_map/ppermute | solution.py:336
  0.7 7.9 %collective-permute-start.2 = (bf16[16,48,625]{2,1,0:T(8,128)(2,1)}, bf16[16,48,625]{2,1,0:T(8,128)(2,1)S(1)}, u32[]{:S(2)}, u32[]{:S(2)}) collective-permute-start(bf16[16,48,625]{2,1,0:T(8,128)(2,1)} %demand_own_ref.3), channel_id=1, source_target_pairs={{0,1},{1,0},{2,3},{3,2},{4,5},{5,4},{6,7},{7,6},{8,9},{9,8},{10,11... | collective-permute-start | bytes 2880008 | tf_op jit(solution)/shard_map/ppermute | solution.py:336
  1.2 7.4 %collective-permute-start = (f32[16,48,250]{2,1,0:T(8,128)}, f32[16,48,250]{2,1,0:T(8,128)}, u32[]{:S(2)}, u32[]{:S(2)}) collective-permute-start(f32[16,48,250]{2,1,0:T(8,128)} %dispatch_ref.1), channel_id=1, source_target_pairs={{0,1},{1,0},{2,3},{3,2},{4,5},{5,4},{6,7},{7,6},{8,9},{9,8},{10,11... | collective-permute-start | bytes 2304008 | tf_op jit(solution)/shard_map/ppermute | solution.py:336
  5.6 13.2 %collective-permute-start.4 = (s16[29,24,128]{2,1,0:T(8,128)(2,1)}, s16[29,24,128]{2,1,0:T(8,128)(2,1)}, u32[]{:S(2)}, u32[]{:S(2)}) collective-permute-start(s16[29,24,128]{2,1,0:T(8,128)(2,1)} %shard_map.132.rest_0_.own_ref), channel_id=1, source_target_pairs={{0,64},{64,0},{1,65},{65,1},{2,66},{66,2},{3,67},{67,3},{4,68},{68... | collective-permute-start | bytes 534536 | tf_op jit(solution)/shard_map/ppermute | solution.py:336
  7.3 1.4 collective-permute-start.1
  18.9 30.8 %all-to-all-start = ((s16[8,48,2048]{2,1,0:T(8,128)(2,1)}), s16[8,48,2048]{2,1,0:T(8,128)(2,1)S(1)}, u32[]{:S(2)}, u32[]{:S(2)}) async-start(s16[8,48,2048]{2,1,0:T(8,128)(2,1)} %shard_map.133._), calls=%async_computation | async-start | bytes 3145728 | tf_op jit(solution)/shard_map/all_to_all | solution.py:340
  27.3 17.1 %collective-permute-start.7 = (s16[45,24,128]{2,1,0:T(8,128)(2,1)}, s16[45,24,128]{2,1,0:T(8,128)(2,1)S(1)}, u32[]{:S(2)}, u32[]{:S(2)}) collective-permute-start(s16[45,24,128]{2,1,0:T(8,128)(2,1)} %shard_map.134.rest_0_), channel_id=1, source_target_pairs={{0,16},{16,32},{32,48},{48,0},{1,17},{17,33},{33,49},{49,1},{2,18}... | collective-permute-start | bytes 829448 | tf_op jit(solution)/shard_map/ppermute | solution.py:382
  29.2 16.1 %collective-permute-start.6 = (s16[45,24,128]{2,1,0:T(8,128)(2,1)}, s16[45,24,128]{2,1,0:T(8,128)(2,1)S(1)}, u32[]{:S(2)}, u32[]{:S(2)}) collective-permute-start(s16[45,24,128]{2,1,0:T(8,128)(2,1)} %shard_map.134.rest_0_), channel_id=1, source_target_pairs={{0,32},{16,48},{32,0},{48,16},{1,33},{17,49},{33,1},{49,17},{2,34}... | collective-permute-start | bytes 829448 | tf_op jit(solution)/shard_map/ppermute | solution.py:382
  32.8 12.5 %collective-permute-start.5 = (s16[45,24,128]{2,1,0:T(8,128)(2,1)}, s16[45,24,128]{2,1,0:T(8,128)(2,1)S(1)}, u32[]{:S(2)}, u32[]{:S(2)}) collective-permute-start(s16[45,24,128]{2,1,0:T(8,128)(2,1)} %shard_map.134.rest_0_), channel_id=1, source_target_pairs={{0,48},{16,0},{32,16},{48,32},{1,49},{17,1},{33,17},{49,33},{2,50}... | collective-permute-start | bytes 829448 | tf_op jit(solution)/shard_map/ppermute | solution.py:382
  83.3 2.0 %collective-permute-start.8 = (f32[8,48,250]{2,1,0:T(8,128)S(1)}, f32[8,48,250]{2,1,0:T(8,128)S(1)}, u32[]{:S(2)}, u32[]{:S(2)}) collective-permute-start(f32[8,48,250]{2,1,0:T(8,128)S(1)} %fusion.2), channel_id=1, source_target_pairs={{0,1},{1,0},{2,3},{3,2},{4,5},{5,4},{6,7},{7,6},{8,9},{9,8},{10,11... | collective-permute-start | bytes 1152008 | tf_op jit(solution)/shard_map/ppermute | solution.py:336
  88.9 1.9 %collective-permute-start.9 = (f32[8,48,250]{2,1,0:T(8,128)}, f32[8,48,250]{2,1,0:T(8,128)S(1)}, u32[]{:S(2)}, u32[]{:S(2)}) collective-permute-start(f32[8,48,250]{2,1,0:T(8,128)} %get-tuple-element.21), channel_id=1, source_target_pairs={{0,1},{1,0},{2,3},{3,2},{4,5},{5,4},{6,7},{7,6},{8,9},{9,8},{10,11... | collective-permute-start | bytes 1152008 | tf_op jit(solution)/shard_map/ppermute | solution.py:336
  89.1 10.8 %collective-permute-start.10 = (s16[29,24,128]{2,1,0:T(8,128)(2,1)}, s16[29,24,128]{2,1,0:T(8,128)(2,1)S(1)}, u32[]{:S(2)}, u32[]{:S(2)}) collective-permute-start(s16[29,24,128]{2,1,0:T(8,128)(2,1)} %get-tuple-element.20.rest_0_.own_ref), channel_id=1, source_target_pairs={{0,64},{64,0},{1,65},{65,1},{2,66},{66,2},{3,67},{67,3},{4,68},{68... | collective-permute-start | bytes 534536 | tf_op jit(solution)/shard_map/ppermute | solution.py:336
  100.6 27.3 %all-to-all-start.2 = ((s16[8,48,2048]{2,1,0:T(8,128)(2,1)}), s16[8,48,2048]{2,1,0:T(8,128)(2,1)S(1)}, u32[]{:S(2)}, u32[]{:S(2)}) async-start(s16[8,48,2048]{2,1,0:T(8,128)(2,1)} %shard_map.141), calls=%async_computation.2 | async-start | bytes 3145728 | tf_op jit(solution)/shard_map/all_to_all | solution.py:340
  105.9 10.4 %collective-permute-start.13 = (s16[45,24,128]{2,1,0:T(8,128)(2,1)}, s16[45,24,128]{2,1,0:T(8,128)(2,1)S(1)}, u32[]{:S(2)}, u32[]{:S(2)}) collective-permute-start(s16[45,24,128]{2,1,0:T(8,128)(2,1)} %shard_map.142.rest_0_), channel_id=1, source_target_pairs={{0,16},{16,32},{32,48},{48,0},{1,17},{17,33},{33,49},{49,1},{2,18}... | collective-permute-start | bytes 829448 | tf_op jit(solution)/shard_map/ppermute | solution.py:382
  107.8 15.7 %collective-permute-start.12 = (s16[45,24,128]{2,1,0:T(8,128)(2,1)}, s16[45,24,128]{2,1,0:T(8,128)(2,1)S(1)}, u32[]{:S(2)}, u32[]{:S(2)}) collective-permute-start(s16[45,24,128]{2,1,0:T(8,128)(2,1)} %shard_map.142.rest_0_), channel_id=1, source_target_pairs={{0,32},{16,48},{32,0},{48,16},{1,33},{17,49},{33,1},{49,17},{2,34}... | collective-permute-start | bytes 829448 | tf_op jit(solution)/shard_map/ppermute | solution.py:382
  110.7 12.8 %collective-permute-start.11 = (s16[45,24,128]{2,1,0:T(8,128)(2,1)}, s16[45,24,128]{2,1,0:T(8,128)(2,1)S(1)}, u32[]{:S(2)}, u32[]{:S(2)}) collective-permute-start(s16[45,24,128]{2,1,0:T(8,128)(2,1)} %shard_map.142.rest_0_), channel_id=1, source_target_pairs={{0,48},{16,0},{32,16},{48,32},{1,49},{17,1},{33,17},{49,33},{2,50}... | collective-permute-start | bytes 829448 | tf_op jit(solution)/shard_map/ppermute | solution.py:382
  161.7 2.0 %collective-permute-start.14 = (f32[8,48,250]{2,1,0:T(8,128)S(1)}, f32[8,48,250]{2,1,0:T(8,128)S(1)}, u32[]{:S(2)}, u32[]{:S(2)}) collective-permute-start(f32[8,48,250]{2,1,0:T(8,128)S(1)} %fusion), channel_id=1, source_target_pairs={{0,1},{1,0},{2,3},{3,2},{4,5},{5,4},{6,7},{7,6},{8,9},{9,8},{10,11... | collective-permute-start | bytes 1152008 | tf_op jit(solution)/shard_map/ppermute | solution.py:336
  167.3 6.6 %collective-permute-start.15 = (s16[29,24,128]{2,1,0:T(8,128)(2,1)}, s16[29,24,128]{2,1,0:T(8,128)(2,1)S(1)}, u32[]{:S(2)}, u32[]{:S(2)}) collective-permute-start(s16[29,24,128]{2,1,0:T(8,128)(2,1)} %get-tuple-element.27.rest_0_), channel_id=1, source_target_pairs={{0,64},{64,0},{1,65},{65,1},{2,66},{66,2},{3,67},{67,3},{4,68},{68... | collective-permute-start | bytes 534536 | tf_op jit(solution)/shard_map/ppermute | solution.py:336
  168.0 9.5 %collective-permute-start.16 = (s16[29,24,128]{2,1,0:T(8,128)(2,1)}, s16[29,24,128]{2,1,0:T(8,128)(2,1)S(1)}, u32[]{:S(2)}, u32[]{:S(2)}) collective-permute-start(s16[29,24,128]{2,1,0:T(8,128)(2,1)} %get-tuple-element.27.rest_0_), channel_id=1, source_target_pairs={{0,48},{16,0},{32,16},{48,32},{1,49},{17,1},{33,17},{49,33},{2,50}... | collective-permute-start | bytes 534536 | tf_op jit(solution)/shard_map/ppermute | solution.py:382
  173.9 7.1 %collective-permute-start.17 = (s16[29,24,128]{2,1,0:T(8,128)(2,1)S(1)}, s16[29,24,128]{2,1,0:T(8,128)(2,1)S(1)}, u32[]{:S(2)}, u32[]{:S(2)}) collective-permute-start(s16[29,24,128]{2,1,0:T(8,128)(2,1)S(1)} %collective-permute-done.15.rest_1_), channel_id=1, source_target_pairs={{0,48},{16,0},{32,16},{48,32},{1,49},{17,1},{33,17},{49,33},{2,50}... | collective-permute-start | bytes 534536 | tf_op jit(solution)/shard_map/ppermute | solution.py:382
  176.9 8.6 %collective-permute-start.20 = (s16[29,24,128]{2,1,0:T(8,128)(2,1)}, s16[29,24,128]{2,1,0:T(8,128)(2,1)S(1)}, u32[]{:S(2)}, u32[]{:S(2)}) collective-permute-start(s16[29,24,128]{2,1,0:T(8,128)(2,1)} %get-tuple-element.27.rest_0_), channel_id=1, source_target_pairs={{0,16},{16,32},{32,48},{48,0},{1,17},{17,33},{33,49},{49,1},{2,18}... | collective-permute-start | bytes 534536 | tf_op jit(solution)/shard_map/ppermute | solution.py:382
  176.9 10.5 %collective-permute-start.21 = (s16[29,24,128]{2,1,0:T(8,128)(2,1)S(1)}, s16[29,24,128]{2,1,0:T(8,128)(2,1)S(1)}, u32[]{:S(2)}, u32[]{:S(2)}) collective-permute-start(s16[29,24,128]{2,1,0:T(8,128)(2,1)S(1)} %collective-permute-done.15.rest_1_), channel_id=1, source_target_pairs={{0,16},{16,32},{32,48},{48,0},{1,17},{17,33},{33,49},{49,1},{2,18}... | collective-permute-start | bytes 534536 | tf_op jit(solution)/shard_map/ppermute | solution.py:382
  177.5 8.0 %collective-permute-start.18 = (s16[29,24,128]{2,1,0:T(8,128)(2,1)S(1)}, s16[29,24,128]{2,1,0:T(8,128)(2,1)S(1)}, u32[]{:S(2)}, u32[]{:S(2)}) collective-permute-start(s16[29,24,128]{2,1,0:T(8,128)(2,1)S(1)} %collective-permute-done.16.rest_2_), channel_id=1, source_target_pairs={{0,48},{16,0},{32,16},{48,32},{1,49},{17,1},{33,17},{49,33},{2,50}... | collective-permute-start | bytes 534536 | tf_op jit(solution)/shard_map/ppermute | solution.py:382
  181.0 6.7 %collective-permute-start.19 = (s16[29,24,128]{2,1,0:T(8,128)(2,1)S(1)}, s16[29,24,128]{2,1,0:T(8,128)(2,1)S(1)}, u32[]{:S(2)}, u32[]{:S(2)}) collective-permute-start(s16[29,24,128]{2,1,0:T(8,128)(2,1)S(1)} %collective-permute-done.17.rest_3_), channel_id=1, source_target_pairs={{0,48},{16,0},{32,16},{48,32},{1,49},{17,1},{33,17},{49,33},{2,50}... | collective-permute-start | bytes 534536 | tf_op jit(solution)/shard_map/ppermute | solution.py:382
  (28 other events, 147.0 us)

commit v6 on v5

--- a/solution.py
+++ b/solution.py
@@ -128,7 +128,8 @@
     def injected(i, dispatch_ref, bus_ref):
         first = 8 * core if dispatch_ref.shape[0] > 8 else 0
         dispatch = dispatch_ref[pl.ds(first, 8)].reshape(rows, dispatch_ref.shape[2])
-        power = mm3(dispatch, pick(bus_ref, buses), NT)
+        stacked = mm(jnp.concatenate(parts3(dispatch), axis=0), pick(bus_ref, buses), NT)
+        power = stacked[:rows] + stacked[rows : 2 * rows] + stacked[2 * rows :]
         copies[i].wait()
         load = demand[i].astype(F32).reshape(rows, buses)
         return (power - load).astype(BF16)

time: 192 us -> 192 us (level)
  no operation moved by 1% of the time
where the time goes in v6:
time: 192 us; the launch traced here: 191 us
  blocking collectives  57.7 us (30%)
  Pallas kernels  55.2 us (29%)
  starting transfers between devices  38.8 us (20%)
  waiting for transfers between devices  22.1 us (12%)
  local copies, waits for them, and re-layouts  11.5 us (6%)
  matrix products  3.82 us (2%)
    all_to_all x2, blocking collectives, exchanged(): return lax.all_to_all(blocks, ('yhi', 'x'), 0, 0, tiled=True)  57.7 us
    pallas_call x16, Pallas kernels, run(): pl.pallas_call(kernel, out_shape=list(outs) if many else outs, in_specs=s...  55.2 us
    ppermute x12, starting transfers between devices, from_z(): return lax.ppermute(value, 'z', [(i, (i - d) % 4) for i in range(4)])  24.3 us
    ppermute x12, waiting for transfers between devices, from_z(): return lax.ppermute(value, 'z', [(i, (i - d) % 4) for i in range(4)])  17.4 us
    unnamed x56, local copies, waits for them, and re-layouts  10.3 us
    all_to_all x2, starting transfers between devices, exchanged(): return lax.all_to_all(blocks, ('yhi', 'x'), 0, 0, tiled=True)  10.3 us
    ppermute x10, waiting for transfers between devices, swapped(): return lax.ppermute(value, axis, [(0, 1), (1, 0)])  4.67 us
    ppermute x10, starting transfers between devices, swapped(): return lax.ppermute(value, axis, [(0, 1), (1, 0)])  4.26 us
  transfers between devices with their start and end apart: 24, of which 10 were waited for; matrix products, arithmetic and copies ran while one was open for 3% of the time, Pallas kernels for 21%

profile of v6, /device:TPU:0, one launch (start us, length us, event | category | flops | bytes accessed | tf_op | source)
XLA Modules:
  0.0 191.2 jit_solution(13740854533594317164)
XLA Ops:
  10.4 8.3 %shard_map.133._ = s16[8,48,2048]{2,1,0:T(8,128)(2,1)} custom-call(s32[3]{0:T(128)} %pad_add_fusion.where_ref, f32[16,48,250]{2,1,0:T(8,128)} %dispatch_ref.1, f32[16,48,250]{2,1,0:T(8,128)} %collective-permute-done.other_ref, s32[1,250]{1,0:T(1,128)} %bitcast.35, s32[1,250]{1,0:T(1,128)} %bitcast.38, bf16[16,48,625]{2,1,0:T(8,128)(2,1)} %demand_own_ref.3, ...), custom_call_target="tpu_custom_call" | custom-call | tf_op jit(solution)/shard_map/pallas_call | solution.py:40
  18.7 6.7 %all-to-all-start = ((s16[8,48,2048]{2,1,0:T(8,128)(2,1)}), s16[8,48,2048]{2,1,0:T(8,128)(2,1)S(1)}, u32[]{:S(2)}, u32[]{:S(2)}) async-start(s16[8,48,2048]{2,1,0:T(8,128)(2,1)} %shard_map.133._), calls=%async_computation | async-start | bytes 3145728 | tf_op jit(solution)/shard_map/all_to_all | solution.py:341
  29.1 3.6 %collective-permute-start.6 = (s16[45,24,128]{2,1,0:T(8,128)(2,1)}, s16[45,24,128]{2,1,0:T(8,128)(2,1)S(1)}, u32[]{:S(2)}, u32[]{:S(2)}) collective-permute-start(s16[45,24,128]{2,1,0:T(8,128)(2,1)} %shard_map.134.rest_0_), channel_id=1, source_target_pairs={{0,32},{16,48},{32,0},{48,16},{1,33},{17,49},{33,1},{49,17},{2,34}... | collective-permute-start | bytes 829448 | tf_op jit(solution)/shard_map/ppermute | solution.py:383
  34.9 3.7 %shard_map.137.rest_1_ = bf16[2048,250]{1,0:T(8,128)(2,1)} custom-call(s32[1,250]{1,0:T(1,128)} %bitcast.36, bf16[2000,625]{1,0:T(8,128)(2,1)} %bitcast.32, s16[8,48,2048]{2,1,0:T(8,128)(2,1)} %shard_map.133._), custom_call_target="tpu_custom_call" | custom-call | tf_op jit(solution)/shard_map/pallas_call | solution.py:40
  40.5 3.8 %shard_map.138.rest_2_ = bf16[2048,250]{1,0:T(8,128)(2,1)} custom-call(s32[1,250]{1,0:T(1,128)} %bitcast.39, bf16[2000,625]{1,0:T(8,128)(2,1)} %copy-done.4, s16[8,48,2048]{2,1,0:T(8,128)(2,1)} %shard_map.133._), custom_call_target="tpu_custom_call" | custom-call | tf_op jit(solution)/shard_map/pallas_call | solution.py:40
  46.0 3.5 %shard_map.135 = (f32[16,48,250]{2,1,0:T(8,128)}, f32[16,48,250]{2,1,0:T(8,128)}) custom-call(s32[80]{0:T(128)} %shard_map.131.ids_ref, f32[16,48,250]{2,1,0:T(8,128)} %dispatch_ref.1, f32[16,48,250]{2,1,0:T(8,128)} %prices_ref.1, f32[1,250]{1,0:T(1,128)} %bitcast.42, f32[1,250]{1,0:T(1,128)} %bitcast.44, f32[1,250]{1,0:T(1,128)} %bitcast.46, ...), custom_call_target="tpu_custom_call" | custom-call | tf_op jit(solution)/shard_map/pallas_call | solution.py:40
  50.7 3.1 %shard_map.139 = bf16[8,48,2048]{2,1,0:T(8,128)(2,1)} custom-call(s16[8,48,2048]{2,1,0:T(8,128)(2,1)} %copy-done.5, f32[1,2048]{1,0:T(1,128)} %shard_map.136.limits_ref, f32[16,48,250]{2,1,0:T(8,128)} %get-tuple-element.16.rest_0_.stepped_ref, bf16[2048,250]{1,0:T(8,128)(2,1)} %shard_map.137.rest_1_, bf16[2048,250]{1,0:T(8,128)(2,1)} %shard_map.138.rest_2_), custom_call_target="tpu_custom_call" | custom-call | tf_op jit(solution)/shard_map/pallas_call | solution.py:40
  53.8 28.7 %all_to_all.20 = bf16[8,48,2048]{2,1,0:T(8,128)(2,1)S(1)} all-to-all(bf16[8,48,2048]{2,1,0:T(8,128)(2,1)} %shard_map.139), channel_id=1, replica_groups=mesh['ylo'=2,'z'=4,'yhi'=2,'x'=4,'core'=2] {'yhi','x'}, dimensions={0} | all-to-all | bytes 3145728 | tf_op jit(solution)/shard_map/all_to_all | solution.py:341
  85.9 2.9 %shard_map.140 = (f32[16,48,250]{2,1,0:T(8,128)}, f32[8,48,250]{2,1,0:T(8,128)}, s16[29,24,128]{2,1,0:T(8,128)(2,1)}) custom-call(s32[3]{0:T(128)} %pad_add_fusion.where_ref, s32[80]{0:T(128)} %shard_map.131.ids_ref, f32[16,48,250]{2,1,0:T(8,128)} %get-tuple-element.16.rest_0_.stepped_ref, f32[8,48,250]{2,1,0:T(8,128)} %fusion.6.pull_own_ref, ...), custom_call_target="tpu_custom_call" | custom-call | tf_op jit(solution)/shard_map/pallas_call | solution.py:40
  91.5 8.2 %shard_map.141 = s16[8,48,2048]{2,1,0:T(8,128)(2,1)} custom-call(s32[3]{0:T(128)} %pad_add_fusion.where_ref, f32[16,48,250]{2,1,0:T(8,128)} %get-tuple-element.18.own_ref.dispatch_ref, f32[8,48,250]{2,1,0:T(8,128)} %copy-done.8, s32[1,250]{1,0:T(1,128)} %bitcast.37, s32[1,250]{1,0:T(1,128)} %bitcast.40, bf16[16,48,625]{2,1,0:T(8,128)(2,1)} %demand_own_ref.3, ...), custom_call_target="tpu_custom_call" | custom-call | tf_op jit(solution)/shard_map/pallas_call | solution.py:40
  100.4 3.6 %all-to-all-start.2 = ((s16[8,48,2048]{2,1,0:T(8,128)(2,1)}), s16[8,48,2048]{2,1,0:T(8,128)(2,1)S(1)}, u32[]{:S(2)}, u32[]{:S(2)}) async-start(s16[8,48,2048]{2,1,0:T(8,128)(2,1)} %shard_map.141), calls=%async_computation.2 | async-start | bytes 3145728 | tf_op jit(solution)/shard_map/all_to_all | solution.py:341
  107.6 2.9 %collective-permute-start.12 = (s16[45,24,128]{2,1,0:T(8,128)(2,1)}, s16[45,24,128]{2,1,0:T(8,128)(2,1)S(1)}, u32[]{:S(2)}, u32[]{:S(2)}) collective-permute-start(s16[45,24,128]{2,1,0:T(8,128)(2,1)} %shard_map.142.rest_0_), channel_id=1, source_target_pairs={{0,32},{16,48},{32,0},{48,16},{1,33},{17,49},{33,1},{49,17},{2,34}... | collective-permute-start | bytes 829448 | tf_op jit(solution)/shard_map/ppermute | solution.py:383
  110.5 5.7 %collective-permute-done.13.rest_3_ = s16[45,24,128]{2,1,0:T(8,128)(2,1)S(1)} collective-permute-done((s16[45,24,128]{2,1,0:T(8,128)(2,1)}, s16[45,24,128]{2,1,0:T(8,128)(2,1)S(1)}, u32[]{:S(2)}, u32[]{:S(2)}) %collective-permute-start.13) | collective-permute-done | bytes 276512 | tf_op jit(solution)/shard_map/ppermute | solution.py:383
  116.1 7.1 %collective-permute-done.12.rest_2_ = s16[45,24,128]{2,1,0:T(8,128)(2,1)S(1)} collective-permute-done((s16[45,24,128]{2,1,0:T(8,128)(2,1)}, s16[45,24,128]{2,1,0:T(8,128)(2,1)S(1)}, u32[]{:S(2)}, u32[]{:S(2)}) %collective-permute-start.12) | collective-permute-done | bytes 276512 | tf_op jit(solution)/shard_map/ppermute | solution.py:383
  124.0 3.6 %shard_map.143 = (f32[16,48,250]{2,1,0:T(8,128)}, f32[16,48,250]{2,1,0:T(8,128)}) custom-call(s32[80]{0:T(128)} %shard_map.131.ids_ref, f32[16,48,250]{2,1,0:T(8,128)} %get-tuple-element.18.own_ref.dispatch_ref, f32[16,48,250]{2,1,0:T(8,128)} %get-tuple-element.19.prices_ref, f32[1,250]{1,0:T(1,128)} %bitcast.43, f32[1,250]{1,0:T(1,128)} %bitcast.45, ...), custom_call_target="tpu_custom_call" | custom-call | tf_op jit(solution)/shard_map/pallas_call | solution.py:40
  128.8 3.1 %shard_map.144 = bf16[8,48,2048]{2,1,0:T(8,128)(2,1)} custom-call(s16[8,48,2048]{2,1,0:T(8,128)(2,1)} %copy-done.6, f32[1,2048]{1,0:T(1,128)} %shard_map.136.limits_ref, f32[16,48,250]{2,1,0:T(8,128)} %get-tuple-element.23.rest_0_.stepped_ref, bf16[2048,250]{1,0:T(8,128)(2,1)} %shard_map.137.rest_1_, bf16[2048,250]{1,0:T(8,128)(2,1)} %shard_map.138.rest_2_), custom_call_target="tpu_custom_call" | custom-call | tf_op jit(solution)/shard_map/pallas_call | solution.py:40
  131.9 29.0 %all_to_all.21 = bf16[8,48,2048]{2,1,0:T(8,128)(2,1)S(1)} all-to-all(bf16[8,48,2048]{2,1,0:T(8,128)(2,1)} %shard_map.144), channel_id=1, replica_groups=mesh['ylo'=2,'z'=4,'yhi'=2,'x'=4,'core'=2] {'yhi','x'}, dimensions={0} | all-to-all | bytes 3145728 | tf_op jit(solution)/shard_map/all_to_all | solution.py:341
  164.2 2.9 %shard_map.145 = (f32[16,48,250]{2,1,0:T(8,128)}, f32[8,48,250]{2,1,0:T(8,128)}, s16[29,24,128]{2,1,0:T(8,128)(2,1)}) custom-call(s32[3]{0:T(128)} %pad_add_fusion.where_ref, s32[80]{0:T(128)} %shard_map.131.ids_ref, f32[16,48,250]{2,1,0:T(8,128)} %get-tuple-element.23.rest_0_.stepped_ref, f32[8,48,250]{2,1,0:T(8,128)} %fusion.4.pull_own_ref, ...), custom_call_target="tpu_custom_call" | custom-call | tf_op jit(solution)/shard_map/pallas_call | solution.py:40
  167.7 3.0 %collective-permute-start.16 = (s16[29,24,128]{2,1,0:T(8,128)(2,1)}, s16[29,24,128]{2,1,0:T(8,128)(2,1)S(1)}, u32[]{:S(2)}, u32[]{:S(2)}) collective-permute-start(s16[29,24,128]{2,1,0:T(8,128)(2,1)} %get-tuple-element.27.rest_0_), channel_id=1, source_target_pairs={{0,48},{16,0},{32,16},{48,32},{1,49},{17,1},{33,17},{49,33},{2,50}... | collective-permute-start | bytes 534536 | tf_op jit(solution)/shard_map/ppermute | solution.py:383
  170.7 2.9 %collective-permute-done.15.rest_1_ = s16[29,24,128]{2,1,0:T(8,128)(2,1)S(1)} collective-permute-done((s16[29,24,128]{2,1,0:T(8,128)(2,1)}, s16[29,24,128]{2,1,0:T(8,128)(2,1)S(1)}, u32[]{:S(2)}, u32[]{:S(2)}) %collective-permute-start.15) | collective-permute-done | bytes 178208 | tf_op jit(solution)/shard_map/ppermute | solution.py:337
  173.7 3.0 %collective-permute-start.17 = (s16[29,24,128]{2,1,0:T(8,128)(2,1)S(1)}, s16[29,24,128]{2,1,0:T(8,128)(2,1)S(1)}, u32[]{:S(2)}, u32[]{:S(2)}) collective-permute-start(s16[29,24,128]{2,1,0:T(8,128)(2,1)S(1)} %collective-permute-done.15.rest_1_), channel_id=1, source_target_pairs={{0,48},{16,0},{32,16},{48,32},{1,49},{17,1},{33,17},{49,33},{2,50}... | collective-permute-start | bytes 534536 | tf_op jit(solution)/shard_map/ppermute | solution.py:383
  177.3 2.7 %collective-permute-start.18 = (s16[29,24,128]{2,1,0:T(8,128)(2,1)S(1)}, s16[29,24,128]{2,1,0:T(8,128)(2,1)S(1)}, u32[]{:S(2)}, u32[]{:S(2)}) collective-permute-start(s16[29,24,128]{2,1,0:T(8,128)(2,1)S(1)} %collective-permute-done.16.rest_2_), channel_id=1, source_target_pairs={{0,48},{16,0},{32,16},{48,32},{1,49},{17,1},{33,17},{49,33},{2,50}... | collective-permute-start | bytes 534536 | tf_op jit(solution)/shard_map/ppermute | solution.py:383
  180.8 3.7 %collective-permute-start.19 = (s16[29,24,128]{2,1,0:T(8,128)(2,1)S(1)}, s16[29,24,128]{2,1,0:T(8,128)(2,1)S(1)}, u32[]{:S(2)}, u32[]{:S(2)}) collective-permute-start(s16[29,24,128]{2,1,0:T(8,128)(2,1)S(1)} %collective-permute-done.17.rest_3_), channel_id=1, source_target_pairs={{0,48},{16,0},{32,16},{48,32},{1,49},{17,1},{33,17},{49,33},{2,50}... | collective-permute-start | bytes 534536 | tf_op jit(solution)/shard_map/ppermute | solution.py:383
  188.1 3.0 %shard_map.146 = f32[16,48,250]{2,1,0:T(8,128)} custom-call(s32[80]{0:T(128)} %shard_map.131.ids_ref, f32[16,48,250]{2,1,0:T(8,128)} %get-tuple-element.13.dispatch_ref, f32[16,48,250]{2,1,0:T(8,128)} %get-tuple-element.26.prices_ref, s16[29,24,128]{2,1,0:T(8,128)(2,1)} %get-tuple-element.27.rest_0_, s16[29,24,128]{2,1,0:T(8,128)(2,1)} %copy-done.18, ...), custom_call_target="tpu_custom_call" | custom-call | tf_op jit(solution)/shard_map/pallas_call | solution.py:40
  (106 shorter events, 41.7 us)
Async XLA Ops:
  0.6 8.0 %collective-permute-start.3 = (bf16[2000,625]{1,0:T(8,128)(2,1)}, bf16[2000,625]{1,0:T(8,128)(2,1)S(1)}, u32[]{:S(2)}, u32[]{:S(2)}) collective-permute-start(bf16[2000,625]{1,0:T(8,128)(2,1)} %bitcast.30), channel_id=1, source_target_pairs={{0,1},{1,0},{2,3},{3,2},{4,5},{5,4},{6,7},{7,6},{8,9},{9,8},{10,11... | collective-permute-start | bytes 7500008 | tf_op jit(solution)/shard_map/ppermute | solution.py:337
  0.7 7.9 %collective-permute-start.2 = (bf16[16,48,625]{2,1,0:T(8,128)(2,1)}, bf16[16,48,625]{2,1,0:T(8,128)(2,1)S(1)}, u32[]{:S(2)}, u32[]{:S(2)}) collective-permute-start(bf16[16,48,625]{2,1,0:T(8,128)(2,1)} %demand_own_ref.3), channel_id=1, source_target_pairs={{0,1},{1,0},{2,3},{3,2},{4,5},{5,4},{6,7},{7,6},{8,9},{9,8},{10,11... | collective-permute-start | bytes 2880008 | tf_op jit(solution)/shard_map/ppermute | solution.py:337
  1.2 7.4 %collective-permute-start = (f32[16,48,250]{2,1,0:T(8,128)}, f32[16,48,250]{2,1,0:T(8,128)}, u32[]{:S(2)}, u32[]{:S(2)}) collective-permute-start(f32[16,48,250]{2,1,0:T(8,128)} %dispatch_ref.1), channel_id=1, source_target_pairs={{0,1},{1,0},{2,3},{3,2},{4,5},{5,4},{6,7},{7,6},{8,9},{9,8},{10,11... | collective-permute-start | bytes 2304008 | tf_op jit(solution)/shard_map/ppermute | solution.py:337
  5.6 13.1 %collective-permute-start.4 = (s16[29,24,128]{2,1,0:T(8,128)(2,1)}, s16[29,24,128]{2,1,0:T(8,128)(2,1)}, u32[]{:S(2)}, u32[]{:S(2)}) collective-permute-start(s16[29,24,128]{2,1,0:T(8,128)(2,1)} %shard_map.132.rest_0_.own_ref), channel_id=1, source_target_pairs={{0,64},{64,0},{1,65},{65,1},{2,66},{66,2},{3,67},{67,3},{4,68},{68... | collective-permute-start | bytes 534536 | tf_op jit(solution)/shard_map/ppermute | solution.py:337
  7.3 1.4 collective-permute-start.1
  18.7 30.8 %all-to-all-start = ((s16[8,48,2048]{2,1,0:T(8,128)(2,1)}), s16[8,48,2048]{2,1,0:T(8,128)(2,1)S(1)}, u32[]{:S(2)}, u32[]{:S(2)}) async-start(s16[8,48,2048]{2,1,0:T(8,128)(2,1)} %shard_map.133._), calls=%async_computation | async-start | bytes 3145728 | tf_op jit(solution)/shard_map/all_to_all | solution.py:341
  27.2 17.1 %collective-permute-start.7 = (s16[45,24,128]{2,1,0:T(8,128)(2,1)}, s16[45,24,128]{2,1,0:T(8,128)(2,1)S(1)}, u32[]{:S(2)}, u32[]{:S(2)}) collective-permute-start(s16[45,24,128]{2,1,0:T(8,128)(2,1)} %shard_map.134.rest_0_), channel_id=1, source_target_pairs={{0,16},{16,32},{32,48},{48,0},{1,17},{17,33},{33,49},{49,1},{2,18}... | collective-permute-start | bytes 829448 | tf_op jit(solution)/shard_map/ppermute | solution.py:383
  29.1 16.1 %collective-permute-start.6 = (s16[45,24,128]{2,1,0:T(8,128)(2,1)}, s16[45,24,128]{2,1,0:T(8,128)(2,1)S(1)}, u32[]{:S(2)}, u32[]{:S(2)}) collective-permute-start(s16[45,24,128]{2,1,0:T(8,128)(2,1)} %shard_map.134.rest_0_), channel_id=1, source_target_pairs={{0,32},{16,48},{32,0},{48,16},{1,33},{17,49},{33,1},{49,17},{2,34}... | collective-permute-start | bytes 829448 | tf_op jit(solution)/shard_map/ppermute | solution.py:383
  32.7 12.5 %collective-permute-start.5 = (s16[45,24,128]{2,1,0:T(8,128)(2,1)}, s16[45,24,128]{2,1,0:T(8,128)(2,1)S(1)}, u32[]{:S(2)}, u32[]{:S(2)}) collective-permute-start(s16[45,24,128]{2,1,0:T(8,128)(2,1)} %shard_map.134.rest_0_), channel_id=1, source_target_pairs={{0,48},{16,0},{32,16},{48,32},{1,49},{17,1},{33,17},{49,33},{2,50}... | collective-permute-start | bytes 829448 | tf_op jit(solution)/shard_map/ppermute | solution.py:383
  83.2 2.0 %collective-permute-start.8 = (f32[8,48,250]{2,1,0:T(8,128)S(1)}, f32[8,48,250]{2,1,0:T(8,128)S(1)}, u32[]{:S(2)}, u32[]{:S(2)}) collective-permute-start(f32[8,48,250]{2,1,0:T(8,128)S(1)} %fusion.2), channel_id=1, source_target_pairs={{0,1},{1,0},{2,3},{3,2},{4,5},{5,4},{6,7},{7,6},{8,9},{9,8},{10,11... | collective-permute-start | bytes 1152008 | tf_op jit(solution)/shard_map/ppermute | solution.py:337
  88.8 1.9 %collective-permute-start.9 = (f32[8,48,250]{2,1,0:T(8,128)}, f32[8,48,250]{2,1,0:T(8,128)S(1)}, u32[]{:S(2)}, u32[]{:S(2)}) collective-permute-start(f32[8,48,250]{2,1,0:T(8,128)} %get-tuple-element.21), channel_id=1, source_target_pairs={{0,1},{1,0},{2,3},{3,2},{4,5},{5,4},{6,7},{7,6},{8,9},{9,8},{10,11... | collective-permute-start | bytes 1152008 | tf_op jit(solution)/shard_map/ppermute | solution.py:337
  89.0 10.7 %collective-permute-start.10 = (s16[29,24,128]{2,1,0:T(8,128)(2,1)}, s16[29,24,128]{2,1,0:T(8,128)(2,1)S(1)}, u32[]{:S(2)}, u32[]{:S(2)}) collective-permute-start(s16[29,24,128]{2,1,0:T(8,128)(2,1)} %get-tuple-element.20.rest_0_.own_ref), channel_id=1, source_target_pairs={{0,64},{64,0},{1,65},{65,1},{2,66},{66,2},{3,67},{67,3},{4,68},{68... | collective-permute-start | bytes 534536 | tf_op jit(solution)/shard_map/ppermute | solution.py:337
  100.4 27.3 %all-to-all-start.2 = ((s16[8,48,2048]{2,1,0:T(8,128)(2,1)}), s16[8,48,2048]{2,1,0:T(8,128)(2,1)S(1)}, u32[]{:S(2)}, u32[]{:S(2)}) async-start(s16[8,48,2048]{2,1,0:T(8,128)(2,1)} %shard_map.141), calls=%async_computation.2 | async-start | bytes 3145728 | tf_op jit(solution)/shard_map/all_to_all | solution.py:341
  105.7 10.4 %collective-permute-start.13 = (s16[45,24,128]{2,1,0:T(8,128)(2,1)}, s16[45,24,128]{2,1,0:T(8,128)(2,1)S(1)}, u32[]{:S(2)}, u32[]{:S(2)}) collective-permute-start(s16[45,24,128]{2,1,0:T(8,128)(2,1)} %shard_map.142.rest_0_), channel_id=1, source_target_pairs={{0,16},{16,32},{32,48},{48,0},{1,17},{17,33},{33,49},{49,1},{2,18}... | collective-permute-start | bytes 829448 | tf_op jit(solution)/shard_map/ppermute | solution.py:383
  107.6 15.7 %collective-permute-start.12 = (s16[45,24,128]{2,1,0:T(8,128)(2,1)}, s16[45,24,128]{2,1,0:T(8,128)(2,1)S(1)}, u32[]{:S(2)}, u32[]{:S(2)}) collective-permute-start(s16[45,24,128]{2,1,0:T(8,128)(2,1)} %shard_map.142.rest_0_), channel_id=1, source_target_pairs={{0,32},{16,48},{32,0},{48,16},{1,33},{17,49},{33,1},{49,17},{2,34}... | collective-permute-start | bytes 829448 | tf_op jit(solution)/shard_map/ppermute | solution.py:383
  110.5 12.8 %collective-permute-start.11 = (s16[45,24,128]{2,1,0:T(8,128)(2,1)}, s16[45,24,128]{2,1,0:T(8,128)(2,1)S(1)}, u32[]{:S(2)}, u32[]{:S(2)}) collective-permute-start(s16[45,24,128]{2,1,0:T(8,128)(2,1)} %shard_map.142.rest_0_), channel_id=1, source_target_pairs={{0,48},{16,0},{32,16},{48,32},{1,49},{17,1},{33,17},{49,33},{2,50}... | collective-permute-start | bytes 829448 | tf_op jit(solution)/shard_map/ppermute | solution.py:383
  161.5 2.0 %collective-permute-start.14 = (f32[8,48,250]{2,1,0:T(8,128)S(1)}, f32[8,48,250]{2,1,0:T(8,128)S(1)}, u32[]{:S(2)}, u32[]{:S(2)}) collective-permute-start(f32[8,48,250]{2,1,0:T(8,128)S(1)} %fusion), channel_id=1, source_target_pairs={{0,1},{1,0},{2,3},{3,2},{4,5},{5,4},{6,7},{7,6},{8,9},{9,8},{10,11... | collective-permute-start | bytes 1152008 | tf_op jit(solution)/shard_map/ppermute | solution.py:337
  167.1 6.6 %collective-permute-start.15 = (s16[29,24,128]{2,1,0:T(8,128)(2,1)}, s16[29,24,128]{2,1,0:T(8,128)(2,1)S(1)}, u32[]{:S(2)}, u32[]{:S(2)}) collective-permute-start(s16[29,24,128]{2,1,0:T(8,128)(2,1)} %get-tuple-element.27.rest_0_), channel_id=1, source_target_pairs={{0,64},{64,0},{1,65},{65,1},{2,66},{66,2},{3,67},{67,3},{4,68},{68... | collective-permute-start | bytes 534536 | tf_op jit(solution)/shard_map/ppermute | solution.py:337
  167.7 9.5 %collective-permute-start.16 = (s16[29,24,128]{2,1,0:T(8,128)(2,1)}, s16[29,24,128]{2,1,0:T(8,128)(2,1)S(1)}, u32[]{:S(2)}, u32[]{:S(2)}) collective-permute-start(s16[29,24,128]{2,1,0:T(8,128)(2,1)} %get-tuple-element.27.rest_0_), channel_id=1, source_target_pairs={{0,48},{16,0},{32,16},{48,32},{1,49},{17,1},{33,17},{49,33},{2,50}... | collective-permute-start | bytes 534536 | tf_op jit(solution)/shard_map/ppermute | solution.py:383
  173.7 7.1 %collective-permute-start.17 = (s16[29,24,128]{2,1,0:T(8,128)(2,1)S(1)}, s16[29,24,128]{2,1,0:T(8,128)(2,1)S(1)}, u32[]{:S(2)}, u32[]{:S(2)}) collective-permute-start(s16[29,24,128]{2,1,0:T(8,128)(2,1)S(1)} %collective-permute-done.15.rest_1_), channel_id=1, source_target_pairs={{0,48},{16,0},{32,16},{48,32},{1,49},{17,1},{33,17},{49,33},{2,50}... | collective-permute-start | bytes 534536 | tf_op jit(solution)/shard_map/ppermute | solution.py:383
  176.7 8.6 %collective-permute-start.20 = (s16[29,24,128]{2,1,0:T(8,128)(2,1)}, s16[29,24,128]{2,1,0:T(8,128)(2,1)S(1)}, u32[]{:S(2)}, u32[]{:S(2)}) collective-permute-start(s16[29,24,128]{2,1,0:T(8,128)(2,1)} %get-tuple-element.27.rest_0_), channel_id=1, source_target_pairs={{0,16},{16,32},{32,48},{48,0},{1,17},{17,33},{33,49},{49,1},{2,18}... | collective-permute-start | bytes 534536 | tf_op jit(solution)/shard_map/ppermute | solution.py:383
  176.7 10.5 %collective-permute-start.21 = (s16[29,24,128]{2,1,0:T(8,128)(2,1)S(1)}, s16[29,24,128]{2,1,0:T(8,128)(2,1)S(1)}, u32[]{:S(2)}, u32[]{:S(2)}) collective-permute-start(s16[29,24,128]{2,1,0:T(8,128)(2,1)S(1)} %collective-permute-done.15.rest_1_), channel_id=1, source_target_pairs={{0,16},{16,32},{32,48},{48,0},{1,17},{17,33},{33,49},{49,1},{2,18}... | collective-permute-start | bytes 534536 | tf_op jit(solution)/shard_map/ppermute | solution.py:383
  177.3 8.0 %collective-permute-start.18 = (s16[29,24,128]{2,1,0:T(8,128)(2,1)S(1)}, s16[29,24,128]{2,1,0:T(8,128)(2,1)S(1)}, u32[]{:S(2)}, u32[]{:S(2)}) collective-permute-start(s16[29,24,128]{2,1,0:T(8,128)(2,1)S(1)} %collective-permute-done.16.rest_2_), channel_id=1, source_target_pairs={{0,48},{16,0},{32,16},{48,32},{1,49},{17,1},{33,17},{49,33},{2,50}... | collective-permute-start | bytes 534536 | tf_op jit(solution)/shard_map/ppermute | solution.py:383
  180.8 6.7 %collective-permute-start.19 = (s16[29,24,128]{2,1,0:T(8,128)(2,1)S(1)}, s16[29,24,128]{2,1,0:T(8,128)(2,1)S(1)}, u32[]{:S(2)}, u32[]{:S(2)}) collective-permute-start(s16[29,24,128]{2,1,0:T(8,128)(2,1)S(1)} %collective-permute-done.17.rest_3_), channel_id=1, source_target_pairs={{0,48},{16,0},{32,16},{48,32},{1,49},{17,1},{33,17},{49,33},{2,50}... | collective-permute-start | bytes 534536 | tf_op jit(solution)/shard_map/ppermute | solution.py:383
  (28 other events, 147.0 us)
